TPU v7x, 32 devices: a whole 2x2x4 slice. The times are simulated.
32 devices in a mesh: wide: 8 (over y, x, core), narrow: 4 (over z).
Axes of the slice: x: 2, y: 2, z: 4, core: 2. Of those that a mesh axis runs over, the one named last changes fastest.
Arguments:
- enc_in: bfloat16 [8192, 768], P('wide'), may hold values from -6 to 6
- dec_in: bfloat16 [8192, 768], P('wide'), may hold values from -6 to 6
- dec_cot: bfloat16 [8192, 768], P('wide'), may hold values from -6 to 6
- segments: int32 [16, 512], P('wide'), may hold values from 0 to 3, never falling along the last dimension, each value on 1 to 256 neighbouring positions
- enc_attn_gain: bfloat16 [768], replicated, may hold values from 0.5 to 1.5
- enc_query: bfloat16 [768, 768], P('wide'), may hold values from -0.02734375 to 0.02734375
- enc_key: bfloat16 [768, 768], P('wide'), may hold values from -0.21875 to 0.21875
- enc_value: bfloat16 [768, 768], P('wide'), may hold values from -0.21875 to 0.21875
- enc_output: bfloat16 [768, 768], P('wide'), may hold values from -1.25 to 1.25
- enc_table: bfloat16 [32, 12], replicated, may hold values from -4 to 4
- enc_ffn_gain: bfloat16 [768], replicated, may hold values from 0.5 to 1.5
- enc_ffn_in: bfloat16 [768, 3072], P('wide'), may hold values from -0.21875 to 0.21875
- enc_ffn_out: bfloat16 [3072, 768], P('wide'), may hold values from -0.109375 to 0.109375
- dec_self_gain: bfloat16 [768], replicated, may hold values from 0.5 to 1.5
- dec_query: bfloat16 [768, 768], P('wide'), may hold values from -0.02734375 to 0.02734375
- dec_key: bfloat16 [768, 768], P('wide'), may hold values from -0.21875 to 0.21875
- dec_value: bfloat16 [768, 768], P('wide'), may hold values from -0.21875 to 0.21875
- dec_output: bfloat16 [768, 768], P('wide'), may hold values from -1.25 to 1.25
- dec_table: bfloat16 [32, 12], replicated, may hold values from -4 to 4
- dec_cross_gain: bfloat16 [768], replicated, may hold values from 0.5 to 1.5
- cross_query: bfloat16 [768, 768], P('wide'), may hold values from -0.02734375 to 0.02734375
- cross_key: bfloat16 [768, 768], P('wide'), may hold values from -0.21875 to 0.21875
- cross_value: bfloat16 [768, 768], P('wide'), may hold values from -0.21875 to 0.21875
- cross_output: bfloat16 [768, 768], P('wide'), may hold values from -1.25 to 1.25
- dec_ffn_gain: bfloat16 [768], replicated, may hold values from 0.5 to 1.5
- dec_ffn_in: bfloat16 [768, 3072], P('wide'), may hold values from -0.21875 to 0.21875
- dec_ffn_out: bfloat16 [3072, 768], P('wide'), may hold values from -0.109375 to 0.109375
Outputs:
- enc_out: bfloat16 [8192, 768], P('wide', 'narrow')
- dec_out: bfloat16 [8192, 768], P('wide', 'narrow')
- enc_in_grad: bfloat16 [8192, 768], P('wide', 'narrow')
- dec_in_grad: bfloat16 [8192, 768], P('wide', 'narrow')
- enc_attn_gain_grad: float32 [768], replicated
- enc_query_grad: float32 [768, 768], P('wide')
- enc_key_grad: float32 [768, 768], P('wide')
- enc_value_grad: float32 [768, 768], P('wide')
- enc_output_grad: float32 [768, 768], P('wide')
- enc_table_grad: float32 [32, 12], replicated
- enc_ffn_gain_grad: float32 [768], replicated
- enc_ffn_in_grad: float32 [768, 3072], P('wide')
- enc_ffn_out_grad: float32 [3072, 768], P('wide')
- dec_self_gain_grad: float32 [768], replicated
- dec_query_grad: float32 [768, 768], P('wide')
- dec_key_grad: float32 [768, 768], P('wide')
- dec_value_grad: float32 [768, 768], P('wide')
- dec_output_grad: float32 [768, 768], P('wide')
- dec_table_grad: float32 [32, 12], replicated
- dec_cross_gain_grad: float32 [768], replicated
- cross_query_grad: float32 [768, 768], P('wide')
- cross_key_grad: float32 [768, 768], P('wide')
- cross_value_grad: float32 [768, 768], P('wide')
- cross_output_grad: float32 [768, 768], P('wide')
- dec_ffn_gain_grad: float32 [768], replicated
- dec_ffn_in_grad: float32 [768, 3072], P('wide')
- dec_ffn_out_grad: float32 [3072, 768], P('wide')
Inputs may be any that keep to these rules, and one draw needn't show every extreme that they name: `segments`: within each row of 512 positions the numbers never fall, each of the 4 documents has 1 to 256 positions, and one has exactly 256.
All inputs are finite; a program needn't handle non-finite values.
Results may differ from a plain program's by a relative error of at most 0.034.
Values may be sent and summed in bfloat16 or wider, within the bound.
No kernel may reach another device: no remote copies, remote signals or barrier semaphores. Data moves between devices by JAX's collectives and lax.ppermute only.
A program may use at most 384 MiB of HBM per device.

v0:
```python
import jax
import jax.numpy as jnp
import numpy as np
from jax import lax
from jax.sharding import PartitionSpec as P

D = 768
HEADS = 12
HEAD = 64
FF = 3072
BUCKETS = 32
MAXDIST = 128
LEN = 512
MICRO = 2


EPSILON = 1e-06
MASKED = -1000000000.0
HIGHEST = lax.Precision.HIGHEST


def for_sending(shard):
    return jax.tree.map(lambda a: a.astype(jnp.bfloat16) if a.dtype == jnp.float32 else a, shard)


def passed_along(shard, axis, by):
    count = lax.axis_size(axis)
    pairs = [(i, i + by) for i in range(count) if 0 <= i + by < count]
    return lax.ppermute(shard, axis, pairs)


def bucket_table(length, both_ways, buckets, distance):
    offsets = np.arange(-(length - 1), length)
    reverse = -offsets
    result = np.zeros(offsets.shape, np.int64)
    if both_ways:
        half_count = buckets // 2
        result = result + (reverse < 0) * half_count
        reverse = np.abs(reverse)
    else:
        half_count = buckets
        reverse = np.maximum(reverse, 0)
    exact_count = half_count // 2
    scaled = (
        np.log(np.maximum(reverse, 1) / exact_count)
        / np.log(distance / exact_count)
        * (half_count - exact_count)
    )
    far_bucket = np.minimum(
        exact_count + np.floor(np.maximum(scaled, 0.0)).astype(np.int64), half_count - 1
    )
    return result + np.where(reverse < exact_count, reverse, far_bucket)


def toeplitz(vector, length):
    head_count = vector.shape[0]
    padded = jnp.pad(vector, ((0, 0), (0, 1)))
    flattened = jnp.tile(padded, (1, length))[:, : length * (2 * length - 1)]
    return flattened.reshape(head_count, length, 2 * length - 1)[:, :, length - 1 :]


def toeplitz_back(bias_grad, length):
    head_count = bias_grad.shape[0]
    widened = jnp.pad(bias_grad, ((0, 0), (0, 0), (length - 1, 0))).reshape(
        head_count, length * (2 * length - 1)
    )
    widened = jnp.pad(widened, ((0, 0), (0, length)))
    return jnp.sum(widened.reshape(head_count, length, 2 * length), axis=1)[:, : 2 * length - 1]


def bias_parts(table, both_ways):
    bucket_ids = bucket_table(LEN, both_ways, BUCKETS, MAXDIST)
    one_hot = jnp.asarray((bucket_ids[:, None] == np.arange(BUCKETS)[None, :]).astype(np.float32))
    vector = jnp.dot(one_hot, table.astype(jnp.float32), precision=HIGHEST)
    return (toeplitz(vector.T, LEN), one_hot)


def table_grad(bias_grad, one_hot):
    vector_grad = toeplitz_back(bias_grad, LEN)
    return jnp.dot(one_hot.T, vector_grad.T, precision=HIGHEST)


def project(values, matrix):
    return jnp.dot(values, matrix, preferred_element_type=jnp.float32)


def project_back(grads, matrix):
    return lax.dot_general(
        grads, matrix, (((1,), (1,)), ((), ())), preferred_element_type=jnp.float32
    )


def outer_sum(values, grads):
    return lax.dot_general(
        values, grads, (((0,), (0,)), ((), ())), preferred_element_type=jnp.float32
    )


def rms_norm(values, gain):
    return values * lax.rsqrt(jnp.mean(values * values, axis=-1, keepdims=True) + EPSILON) * gain


def segment_masks(seg_rows):
    same_doc = seg_rows[:, :, None] == seg_rows[:, None, :]
    query_pos = lax.broadcasted_iota(jnp.int32, (LEN, LEN), 0)
    key_pos = lax.broadcasted_iota(jnp.int32, (LEN, LEN), 1)
    return (same_doc, same_doc & (key_pos <= query_pos)[None])


def split_heads(values):
    return values.reshape(values.shape[0], HEADS, HEAD)


def by_rows(values, row_count):
    return values.reshape(row_count, LEN, D)


def attention_probs(queries, key_rows, pos_bias, allowed):
    scores = jnp.einsum(
        "qhd,khd->hqk",
        split_heads(queries),
        split_heads(key_rows),
        preferred_element_type=jnp.float32,
    )
    if pos_bias is not None:
        scores = scores + pos_bias
    scores = jnp.where(allowed[None], scores, MASKED)
    powers = jnp.exp(scores - jnp.max(scores, axis=-1, keepdims=True))
    return powers / jnp.sum(powers, axis=-1, keepdims=True)


def attend_forward(queries, key_rows, value_rows, pos_bias, allowed):
    weights_low = attention_probs(queries, key_rows, pos_bias, allowed).astype(jnp.bfloat16)
    mixed = jnp.einsum(
        "hqk,khd->qhd", weights_low, split_heads(value_rows), preferred_element_type=jnp.float32
    )
    return mixed.reshape(queries.shape[0], D).astype(jnp.bfloat16)


def attend_backward(queries, key_rows, value_rows, pos_bias, allowed, mixed_grad):
    weights_full = attention_probs(queries, key_rows, pos_bias, allowed)
    weights_low = weights_full.astype(jnp.bfloat16)
    value_heads = split_heads(value_rows)
    grad_heads = split_heads(mixed_grad)
    row_count = queries.shape[0]
    mixed = jnp.einsum("hqk,khd->qhd", weights_low, value_heads, preferred_element_type=jnp.float32)
    weight_grad = jnp.einsum(
        "qhd,khd->hqk", grad_heads, value_heads, preferred_element_type=jnp.float32
    )
    value_grad = jnp.einsum(
        "hqk,qhd->khd", weights_low, grad_heads, preferred_element_type=jnp.float32
    )
    centred = weight_grad - jnp.sum(weights_full * weight_grad, axis=-1, keepdims=True)
    score_grad = (weights_full * centred).astype(jnp.bfloat16)
    query_grad = jnp.einsum(
        "hqk,khd->qhd", score_grad, split_heads(key_rows), preferred_element_type=jnp.float32
    )
    key_grad = jnp.einsum(
        "hqk,qhd->khd", score_grad, split_heads(queries), preferred_element_type=jnp.float32
    )
    return (
        mixed.reshape(row_count, D).astype(jnp.bfloat16),
        query_grad.reshape(row_count, D).astype(jnp.bfloat16),
        key_grad.reshape(row_count, D).astype(jnp.bfloat16),
        value_grad.reshape(row_count, D).astype(jnp.bfloat16),
        score_grad,
    )


def attention_forward(query_src, key_src, weights, pos_bias, allowed):
    row_count = allowed.shape[0]
    queries = by_rows(project(query_src, weights[0]).astype(jnp.bfloat16), row_count)
    key_rows = by_rows(project(key_src, weights[1]).astype(jnp.bfloat16), row_count)
    value_rows = by_rows(project(key_src, weights[2]).astype(jnp.bfloat16), row_count)

    def one_row(pieces):
        return attend_forward(pieces[0], pieces[1], pieces[2], pos_bias, pieces[3])

    mixed = lax.map(one_row, (queries, key_rows, value_rows, allowed))
    return project(mixed.reshape(-1, D), weights[3])


def attention_backward(query_src, key_src, weights, pos_bias, allowed, branch_grad):
    row_count = allowed.shape[0]
    queries = project(query_src, weights[0]).astype(jnp.bfloat16)
    key_rows = project(key_src, weights[1]).astype(jnp.bfloat16)
    value_rows = project(key_src, weights[2]).astype(jnp.bfloat16)
    mixed_grad = project_back(branch_grad, weights[3]).astype(jnp.bfloat16)

    def one_row(total, pieces):
        q_row, k_row, v_row, mask_row, g_row = pieces
        mixed, query_grad, key_grad, value_grad, score_grad = attend_backward(
            q_row, k_row, v_row, pos_bias, mask_row, g_row
        )
        if pos_bias is not None:
            total = total + score_grad.astype(jnp.float32)
        return (total, (mixed, query_grad, key_grad, value_grad))

    if pos_bias is not None:
        start = jnp.zeros((HEADS, LEN, LEN), jnp.float32)
    else:
        start = jnp.zeros((), jnp.float32)
    bias_grad, (mixed, query_grad, key_grad, value_grad) = lax.scan(
        one_row,
        start,
        (
            by_rows(queries, row_count),
            by_rows(key_rows, row_count),
            by_rows(value_rows, row_count),
            allowed,
            by_rows(mixed_grad, row_count),
        ),
    )
    mixed = mixed.reshape(-1, D)
    query_grad = query_grad.reshape(-1, D)
    key_grad = key_grad.reshape(-1, D)
    value_grad = value_grad.reshape(-1, D)
    weight_grads = jnp.stack(
        [
            outer_sum(query_src, query_grad),
            outer_sum(key_src, key_grad),
            outer_sum(key_src, value_grad),
            outer_sum(mixed, branch_grad),
        ]
    )
    query_side = project_back(query_grad, weights[0])
    key_side = project_back(key_grad, weights[1]) + project_back(value_grad, weights[2])
    return (query_side, key_side, weight_grads, bias_grad)


def feed_forward(normed, section_units, shards):
    row_count = normed.shape[0]
    shard_rows = D // shards
    pre_act = jnp.einsum(
        "nd,jdc->njc", normed, section_units[:4], preferred_element_type=jnp.float32
    ).reshape(row_count, FF)
    hidden = jax.nn.gelu(pre_act).astype(jnp.bfloat16).reshape(row_count, shards, 4, shard_rows)
    out_blocks = section_units[4:].reshape(4, shards, shard_rows, D)
    return jnp.einsum("nwjr,jwrd->nd", hidden, out_blocks, preferred_element_type=jnp.float32)


def feed_backward(normed, section_units, shards, branch_grad):
    row_count = normed.shape[0]
    shard_rows = D // shards
    pre_act = jnp.einsum(
        "nd,jdc->njc", normed, section_units[:4], preferred_element_type=jnp.float32
    ).reshape(row_count, FF)
    hidden = jax.nn.gelu(pre_act).astype(jnp.bfloat16).reshape(row_count, shards, 4, shard_rows)
    out_blocks = section_units[4:].reshape(4, shards, shard_rows, D)
    hidden_grad = jnp.einsum(
        "nd,jwrd->nwjr", branch_grad, out_blocks, preferred_element_type=jnp.float32
    ).reshape(row_count, FF)
    out_grad = jnp.einsum(
        "nwjr,nd->jwrd", hidden, branch_grad, preferred_element_type=jnp.float32
    ).reshape(4, D, D)
    _, gelu_pull = jax.vjp(jax.nn.gelu, pre_act)
    pre_grad = gelu_pull(hidden_grad)[0].astype(jnp.bfloat16).reshape(row_count, 4, D)
    in_grad = jnp.einsum("nd,njc->jdc", normed, pre_grad, preferred_element_type=jnp.float32)
    normed_grad = jnp.einsum(
        "njc,jdc->nd", pre_grad, section_units[:4], preferred_element_type=jnp.float32
    )
    return (normed_grad, jnp.concatenate([in_grad, out_grad], axis=0))


def in_units(local):
    return jnp.transpose(local.reshape(local.shape[0], 4, D), (1, 0, 2))


def out_units(local):
    return local.reshape(4, local.shape[0] // 4, D)


def keep_if(buffer, value, slot_index, active):
    previous = lax.dynamic_index_in_dim(buffer, slot_index, 0, keepdims=False)
    return lax.dynamic_update_index_in_dim(
        buffer, jnp.where(active, value, previous), slot_index, 0
    )


def on_device(
    enc_in,
    dec_in,
    dec_cot,
    segments,
    enc_attn_gain,
    enc_query,
    enc_key,
    enc_value,
    enc_output,
    enc_table,
    enc_ffn_gain,
    enc_ffn_in,
    enc_ffn_out,
    dec_self_gain,
    dec_query,
    dec_key,
    dec_value,
    dec_output,
    dec_table,
    dec_cross_gain,
    cross_query,
    cross_key,
    cross_value,
    cross_output,
    dec_ffn_gain,
    dec_ffn_in,
    dec_ffn_out,
):
    shards = lax.axis_size("wide")
    shard_rows = D // shards
    section_index = lax.axis_index("narrow")
    sections = lax.axis_size("narrow")
    micro_rows = enc_in.shape[0] // MICRO
    seg_count = segments.shape[0] // MICRO
    padding = jnp.zeros((4, shard_rows, D), jnp.bfloat16)
    all_packs = jnp.stack(
        [
            jnp.concatenate([jnp.stack([enc_query, enc_key, enc_value, enc_output]), padding]),
            jnp.concatenate([in_units(enc_ffn_in), out_units(enc_ffn_out)]),
            jnp.stack(
                [
                    dec_query,
                    dec_key,
                    dec_value,
                    dec_output,
                    cross_query,
                    cross_key,
                    cross_value,
                    cross_output,
                ]
            ),
            jnp.concatenate([in_units(dec_ffn_in), out_units(dec_ffn_out)]),
        ]
    )
    own_pack = lax.dynamic_index_in_dim(all_packs, section_index, 0, keepdims=False)
    section_units = lax.all_gather(own_pack, "wide", axis=1, tiled=True)
    gain_enc_attn = enc_attn_gain.astype(jnp.float32)
    gain_enc_ffn = enc_ffn_gain.astype(jnp.float32)
    gain_dec_self = dec_self_gain.astype(jnp.float32)
    gain_dec_cross = dec_cross_gain.astype(jnp.float32)
    gain_dec_ffn = dec_ffn_gain.astype(jnp.float32)
    enc_bias, enc_hot = bias_parts(enc_table, True)
    dec_bias, dec_hot = bias_parts(dec_table, False)
    empty_rows = jnp.zeros((micro_rows, D), jnp.bfloat16)
    empty_middle = jnp.zeros((micro_rows, D), jnp.float32)

    def forward_enc_attn(incoming, enc_rows, dec_rows, seg_rows):
        source = enc_rows.astype(jnp.float32)
        same_doc, _ = segment_masks(seg_rows)
        normed = rms_norm(source, gain_enc_attn).astype(jnp.bfloat16)
        branch = attention_forward(normed, normed, section_units[0:4], enc_bias, same_doc)
        return ((source + branch).astype(jnp.bfloat16), empty_middle)

    def ffn_forward(gain):

        def run(incoming, enc_rows, dec_rows, seg_rows):
            source = incoming.astype(jnp.float32)
            normed = rms_norm(source, gain).astype(jnp.bfloat16)
            return (
                (source + feed_forward(normed, section_units, shards)).astype(jnp.bfloat16),
                empty_middle,
            )

        return run

    def forward_dec_attn(incoming, enc_rows, dec_rows, seg_rows):
        source = dec_rows.astype(jnp.float32)
        same_doc, causal = segment_masks(seg_rows)
        normed = rms_norm(source, gain_dec_self).astype(jnp.bfloat16)
        first = source + attention_forward(normed, normed, section_units[0:4], dec_bias, causal)
        normed_cross = rms_norm(first, gain_dec_cross).astype(jnp.bfloat16)
        second = first + attention_forward(
            normed_cross, incoming, section_units[4:8], None, same_doc
        )
        return (second.astype(jnp.bfloat16), first)

    def forward_spare(incoming, enc_rows, dec_rows, seg_rows):
        return (empty_rows, empty_middle)

    forward_branches = [
        forward_enc_attn,
        ffn_forward(gain_enc_ffn),
        forward_dec_attn,
        ffn_forward(gain_dec_ffn),
        forward_spare,
    ]

    def forward_tick(carried, tick_index):
        incoming, stored, middles, owned = carried
        micro_index = tick_index - section_index
        active = (micro_index >= 0) & (micro_index < MICRO)
        slot_index = jnp.clip(micro_index, 0, MICRO - 1)
        enc_rows = lax.dynamic_slice_in_dim(enc_in, slot_index * micro_rows, micro_rows, 0)
        dec_rows = lax.dynamic_slice_in_dim(dec_in, slot_index * micro_rows, micro_rows, 0)
        seg_rows = lax.dynamic_slice_in_dim(segments, slot_index * seg_count, seg_count, 0)
        branch_index = jnp.where(active, section_index, 4)
        result, middle = lax.switch(
            branch_index, forward_branches, incoming, enc_rows, dec_rows, seg_rows
        )
        stored = keep_if(stored, incoming, slot_index, active)
        middles = keep_if(middles, middle, slot_index, active)
        owned = keep_if(owned, result, slot_index, active)
        outgoing = jax.tree.map(
            lambda part, own: part.astype(own.dtype),
            passed_along(for_sending(result), "narrow", 1),
            result,
        )
        return ((outgoing, stored, middles, owned), None)

    ticks = MICRO + sections - 1
    start_state = (
        empty_rows,
        jnp.zeros((MICRO, micro_rows, D), jnp.bfloat16),
        jnp.zeros((MICRO, micro_rows, D), jnp.float32),
        jnp.zeros((MICRO, micro_rows, D), jnp.bfloat16),
    )
    (_, stored, middles, owned), _ = lax.scan(forward_tick, start_state, jnp.arange(ticks))

    def back_enc_attn(
        grad_in,
        stored_rows,
        mid_rows,
        enc_rows,
        dec_rows,
        cot_rows,
        seg_rows,
        own_rows,
        big_sums,
        gain_sums,
        table_sums,
    ):
        source = enc_rows.astype(jnp.float32)
        same_doc, _ = segment_masks(seg_rows)
        normed = rms_norm(source, gain_enc_attn).astype(jnp.bfloat16)
        query_side, key_side, weight_grads, bias_grad = attention_backward(
            normed, normed, section_units[0:4], enc_bias, same_doc, grad_in
        )
        _, norm_pull = jax.vjp(rms_norm, source, gain_enc_attn)
        source_grad, gain_grad = norm_pull(query_side + key_side)
        input_grad = (grad_in.astype(jnp.float32) + source_grad).astype(jnp.bfloat16)
        big_sums = big_sums.at[0:4].add(weight_grads)
        gain_sums = gain_sums.at[0].add(gain_grad)
        table_sums = table_sums.at[0].add(table_grad(bias_grad, enc_hot))
        return (input_grad, input_grad, big_sums, gain_sums, table_sums)

    def ffn_back(gain, gain_slot, take_cot):

        def run(
            grad_in,
            stored_rows,
            mid_rows,
            enc_rows,
            dec_rows,
            cot_rows,
            seg_rows,
            own_rows,
            big_sums,
            gain_sums,
            table_sums,
        ):
            out_grad = cot_rows if take_cot else grad_in
            source = stored_rows.astype(jnp.float32)
            normed = rms_norm(source, gain).astype(jnp.bfloat16)
            normed_grad, unit_grads = feed_backward(normed, section_units, shards, out_grad)
            _, norm_pull = jax.vjp(rms_norm, source, gain)
            source_grad, gain_grad = norm_pull(normed_grad)
            outgoing = (out_grad.astype(jnp.float32) + source_grad).astype(jnp.bfloat16)
            return (
                outgoing,
                own_rows,
                big_sums + unit_grads,
                gain_sums.at[gain_slot].add(gain_grad),
                table_sums,
            )

        return run

    def back_dec_attn(
        grad_in,
        stored_rows,
        mid_rows,
        enc_rows,
        dec_rows,
        cot_rows,
        seg_rows,
        own_rows,
        big_sums,
        gain_sums,
        table_sums,
    ):
        source = dec_rows.astype(jnp.float32)
        same_doc, causal = segment_masks(seg_rows)
        normed_cross = rms_norm(mid_rows, gain_dec_cross).astype(jnp.bfloat16)
        cross_side, enc_side, cross_grads, _ = attention_backward(
            normed_cross, stored_rows, section_units[4:8], None, same_doc, grad_in
        )
        outgoing = enc_side.astype(jnp.bfloat16)
        _, cross_pull = jax.vjp(rms_norm, mid_rows, gain_dec_cross)
        first_norm_grad, cross_gain_grad = cross_pull(cross_side)
        first_grad = grad_in.astype(jnp.float32) + first_norm_grad
        normed = rms_norm(source, gain_dec_self).astype(jnp.bfloat16)
        query_side, key_side, self_grads, bias_grad = attention_backward(
            normed, normed, section_units[0:4], dec_bias, causal, first_grad.astype(jnp.bfloat16)
        )
        _, self_pull = jax.vjp(rms_norm, source, gain_dec_self)
        source_grad, self_gain_grad = self_pull(query_side + key_side)
        input_grad = (first_grad + source_grad).astype(jnp.bfloat16)
        big_sums = big_sums + jnp.concatenate([self_grads, cross_grads], axis=0)
        gain_sums = gain_sums.at[2].add(self_gain_grad).at[3].add(cross_gain_grad)
        table_sums = table_sums.at[1].add(table_grad(bias_grad, dec_hot))
        return (outgoing, input_grad, big_sums, gain_sums, table_sums)

    def back_spare(
        grad_in,
        stored_rows,
        mid_rows,
        enc_rows,
        dec_rows,
        cot_rows,
        seg_rows,
        own_rows,
        big_sums,
        gain_sums,
        table_sums,
    ):
        return (empty_rows, own_rows, big_sums, gain_sums, table_sums)

    backward_branches = [
        back_enc_attn,
        ffn_back(gain_enc_ffn, 1, False),
        back_dec_attn,
        ffn_back(gain_dec_ffn, 4, True),
        back_spare,
    ]

    def backward_tick(carried, tick_index):
        grad_in, owned, grad_acc, gain_sums, table_sums = carried
        micro_index = tick_index - (sections - 1 - section_index)
        active = (micro_index >= 0) & (micro_index < MICRO)
        slot_index = jnp.clip(micro_index, 0, MICRO - 1)
        enc_rows = lax.dynamic_slice_in_dim(enc_in, slot_index * micro_rows, micro_rows, 0)
        dec_rows = lax.dynamic_slice_in_dim(dec_in, slot_index * micro_rows, micro_rows, 0)
        cot_rows = lax.dynamic_slice_in_dim(dec_cot, slot_index * micro_rows, micro_rows, 0)
        seg_rows = lax.dynamic_slice_in_dim(segments, slot_index * seg_count, seg_count, 0)
        stored_rows = lax.dynamic_index_in_dim(stored, slot_index, 0, keepdims=False)
        mid_rows = lax.dynamic_index_in_dim(middles, slot_index, 0, keepdims=False)
        own_rows = lax.dynamic_index_in_dim(owned, slot_index, 0, keepdims=False)
        branch_index = jnp.where(active, section_index, 4)
        outgoing, own_new, grad_acc, gain_sums, table_sums = lax.switch(
            branch_index,
            backward_branches,
            grad_in,
            stored_rows,
            mid_rows,
            enc_rows,
            dec_rows,
            cot_rows,
            seg_rows,
            own_rows,
            grad_acc,
            gain_sums,
            table_sums,
        )
        owned = lax.dynamic_update_index_in_dim(owned, own_new, slot_index, 0)
        received = jax.tree.map(
            lambda part, own: part.astype(own.dtype),
            passed_along(for_sending(outgoing), "narrow", -1),
            outgoing,
        )
        return ((received, owned, grad_acc, gain_sums, table_sums), None)

    back_state = (
        empty_rows,
        owned,
        jnp.zeros((8, D, D), jnp.float32),
        jnp.zeros((5, D), jnp.float32),
        jnp.zeros((2, BUCKETS, HEADS), jnp.float32),
    )
    (_, owned, grad_acc, gain_sums, table_sums), _ = lax.scan(
        backward_tick, back_state, jnp.arange(ticks)
    )
    grad_share = lax.psum_scatter(grad_acc, "wide", scatter_dimension=1, tiled=True)
    every_grad = lax.all_gather(
        grad_share.astype(jnp.bfloat16), "narrow", axis=0, tiled=True
    ).astype(grad_share.dtype)
    gain_total, table_total = lax.psum((gain_sums, table_sums), ("wide", "narrow"))
    token_rows = MICRO * micro_rows
    results = lax.all_to_all(
        owned.reshape(token_rows, D), "narrow", split_axis=1, concat_axis=0, tiled=True
    )
    enc_in_grad = results[0:token_rows]
    enc_out = results[token_rows : 2 * token_rows]
    dec_in_grad = results[2 * token_rows : 3 * token_rows]
    dec_out = results[3 * token_rows : 4 * token_rows]
    enc_ffn_in_grad = jnp.transpose(every_grad[8:12], (1, 0, 2)).reshape(shard_rows, FF)
    enc_ffn_out_grad = every_grad[12:16].reshape(4 * shard_rows, D)
    dec_ffn_in_grad = jnp.transpose(every_grad[24:28], (1, 0, 2)).reshape(shard_rows, FF)
    dec_ffn_out_grad = every_grad[28:32].reshape(4 * shard_rows, D)
    return (
        enc_out,
        dec_out,
        enc_in_grad,
        dec_in_grad,
        gain_total[0],
        every_grad[0],
        every_grad[1],
        every_grad[2],
        every_grad[3],
        table_total[0],
        gain_total[1],
        enc_ffn_in_grad,
        enc_ffn_out_grad,
        gain_total[2],
        every_grad[16],
        every_grad[17],
        every_grad[18],
        every_grad[19],
        table_total[1],
        gain_total[3],
        every_grad[20],
        every_grad[21],
        every_grad[22],
        every_grad[23],
        gain_total[4],
        dec_ffn_in_grad,
        dec_ffn_out_grad,
    )


def solution(mesh):
    placed = (
        P("wide", None),
        P("wide", None),
        P("wide", None),
        P("wide", None),
        P(),
        P("wide", None),
        P("wide", None),
        P("wide", None),
        P("wide", None),
        P(),
        P(),
        P("wide", None),
        P("wide", None),
        P(),
        P("wide", None),
        P("wide", None),
        P("wide", None),
        P("wide", None),
        P(),
        P(),
        P("wide", None),
        P("wide", None),
        P("wide", None),
        P("wide", None),
        P(),
        P("wide", None),
        P("wide", None),
    )
    return jax.shard_map(
        on_device,
        mesh=mesh,
        in_specs=placed,
        out_specs=(
            P("wide", "narrow"),
            P("wide", "narrow"),
            P("wide", "narrow"),
            P("wide", "narrow"),
            P(),
            P("wide", None),
            P("wide", None),
            P("wide", None),
            P("wide", None),
            P(),
            P(),
            P("wide", None),
            P("wide", None),
            P(),
            P("wide", None),
            P("wide", None),
            P("wide", None),
            P("wide", None),
            P(),
            P(),
            P("wide", None),
            P("wide", None),
            P("wide", None),
            P("wide", None),
            P(),
            P("wide", None),
            P("wide", None),
        ),
        check_vma=False,
    )
```

profile of v0, /device:TPU:0, one launch (start us, length us, event | category | flops | bytes accessed | tf_op | source)
XLA Modules:
  0.0 2384.2 jit_solution(5208483534353112565)
XLA Ops:
  71.7 39.7 %copy.488 = f32[2,8,512,1024]{3,1,2,0:T(8,128)} copy(f32[2,8,512,1024]{3,2,1,0:T(8,128)S(1)} %bitcast.644) | data formatting | bytes 67108864
  111.4 22.6 slice.506
  134.0 41.6 %reshape.1155 = f32[12,512,1023]{2,1,0:T(8,128)} reshape(f32[12,523776]{1,0:T(8,128)} %slice.506) | data formatting | bytes 50282496 | tf_op jit(solution)/shard_map/reshape | solution.py:59
  175.7 13.4 slice.507
  224.6 39.7 %copy.489 = f32[2,8,512,1024]{3,1,2,0:T(8,128)} copy(f32[2,8,512,1024]{3,2,1,0:T(8,128)S(1)} %bitcast.645) | data formatting | bytes 67108864
  264.3 22.6 slice.508
  286.8 41.6 %reshape.1156 = f32[12,512,1023]{2,1,0:T(8,128)} reshape(f32[12,523776]{1,0:T(8,128)} %slice.508) | data formatting | bytes 50282496 | tf_op jit(solution)/shard_map/reshape | solution.py:59
  328.5 13.4 slice.509
  367.5 421.3 %while.49 = (s32[]{:T(128)}, bf16[512,768]{1,0:T(8,128)(2,1)}, bf16[2,512,768]{2,1,0:T(8,128)(2,1)}, f32[2,512,768]{2,1,0:T(8,128)S(1)}, bf16[2,512,768]{2,1,0:T...) while((s32[]{:T(128)}, bf16[512,768]{1,0:T(8,128)(2,1)}, ...), condition=%wide.region_17.18_spmd, body=%wide.region_0.17_spmd.sunk | while | flops 6903702016 | bytes 147727120 | solution.py:417
  369.6 62.2 %conditional.6 = (bf16[512,768]{1,0:T(8,128)(2,1)}, f32[512,768]{1,0:T(8,128)}) conditional(s32[]{:T(128)} %clamp.11, (bf16[1024,768]{1,0:T(8,128)(2,1)}, s32[]{:T(128)}, f32[768]{0:T(1024)S(1)}, bf16[8,768,768]{2,1,0:T(8,128)(2,1)}, s32[1,512]{1,0:T(1,128)S(1)}, /*index=5*/f32[12,512,512]{1,2,0:T(8,128)}) %tuple.247, ...), branch_computations={%region_1.4_spmd, %region_5.6_spmd, %region_7.13_spmd, %region_14.... | conditional | flops 6902522368 | bytes 98963504 | solution.py:397
  455.4 62.4 %conditional.6 = (bf16[512,768]{1,0:T(8,128)(2,1)}, f32[512,768]{1,0:T(8,128)}) conditional(s32[]{:T(128)} %clamp.11, (bf16[1024,768]{1,0:T(8,128)(2,1)}, s32[]{:T(128)}, f32[768]{0:T(1024)S(1)}, bf16[8,768,768]{2,1,0:T(8,128)(2,1)}, s32[1,512]{1,0:T(1,128)S(1)}, /*index=5*/f32[12,512,512]{1,2,0:T(8,128)}) %tuple.247, ...), branch_computations={%region_1.4_spmd, %region_5.6_spmd, %region_7.13_spmd, %region_14.... | conditional | flops 6902522368 | bytes 98963504 | solution.py:397
  540.7 24.6 %conditional.6 = (bf16[512,768]{1,0:T(8,128)(2,1)}, f32[512,768]{1,0:T(8,128)}) conditional(s32[]{:T(128)} %clamp.11, (bf16[1024,768]{1,0:T(8,128)(2,1)}, s32[]{:T(128)}, f32[768]{0:T(1024)S(1)}, bf16[8,768,768]{2,1,0:T(8,128)(2,1)}, s32[1,512]{1,0:T(1,128)S(1)}, /*index=5*/f32[12,512,512]{1,2,0:T(8,128)}) %tuple.247, ...), branch_computations={%region_1.4_spmd, %region_5.6_spmd, %region_7.13_spmd, %region_14.... | conditional | flops 6902522368 | bytes 98963504 | solution.py:397
  590.8 17.7 conditional.6
  608.6 37.2 %collective-permute-start = (bf16[512,768]{1,0:T(8,128)(2,1)}, bf16[512,768]{1,0:T(8,128)(2,1)}, u32[]{:S(2)}, u32[]{:S(2)}) collective-permute-start(bf16[512,768]{1,0:T(8,128)(2,1)} %get-tuple-element.1790), channel_id=1, source_target_pairs={{0,1},{1,2},{2,3},{4,5},{5,6},{6,7},{8,9},{9,10},{10,11},{12,13},{... | collective-permute-start | bytes 2359304 | tf_op jit(solution)/shard_map/while/body/eval_jaxpr/ppermute | solution.py:29
  664.8 24.6 %conditional.6 = (bf16[512,768]{1,0:T(8,128)(2,1)}, f32[512,768]{1,0:T(8,128)}) conditional(s32[]{:T(128)} %clamp.11, (bf16[1024,768]{1,0:T(8,128)(2,1)}, s32[]{:T(128)}, f32[768]{0:T(1024)S(1)}, bf16[8,768,768]{2,1,0:T(8,128)(2,1)}, s32[1,512]{1,0:T(1,128)S(1)}, /*index=5*/f32[12,512,512]{1,2,0:T(8,128)}) %tuple.247, ...), branch_computations={%region_1.4_spmd, %region_5.6_spmd, %region_7.13_spmd, %region_14.... | conditional | flops 6902522368 | bytes 98963504 | solution.py:397
  689.4 81.3 %collective-permute-start = (bf16[512,768]{1,0:T(8,128)(2,1)}, bf16[512,768]{1,0:T(8,128)(2,1)}, u32[]{:S(2)}, u32[]{:S(2)}) collective-permute-start(bf16[512,768]{1,0:T(8,128)(2,1)} %get-tuple-element.1790), channel_id=1, source_target_pairs={{0,1},{1,2},{2,3},{4,5},{5,6},{6,7},{8,9},{9,10},{10,11},{12,13},{... | collective-permute-start | bytes 2359304 | tf_op jit(solution)/shard_map/while/body/eval_jaxpr/ppermute | solution.py:29
  799.8 1319.9 %while.50 = (s32[]{:T(128)}, bf16[512,768]{1,0:T(8,128)(2,1)S(1)}, bf16[2,512,768]{2,1,0:T(8,128)(2,1)}, f32[8,768,768]{2,1,0:T(8,128)}, f32[5,768]{1,0:T(8,128)...) while((s32[]{:T(128)}, bf16[512,768]{1,0:T(8,128)(2,1)S(1)}, ...), condition=%wide.region_50.51_spmd.clone, body=%wide.region_18.50_spmd.sunk.clone.sunk | while | flops 19091017728 | bytes 798990336 | solution.py:579
  806.8 33.0 %conditional.7 = (bf16[512,768]{1,0:T(8,128)(2,1)}, f32[8,768,768]{2,1,0:T(8,128)}, f32[5,768]{1,0:T(8,128)}, f32[2,32,12]{1,2,0:T(8,128)}, bf16[1,512,768]{2,1,0:T(8,128)(2,1)}) conditional(s32[]{:T(128)} %clamp.12, (bf16[512,768]{1,0:T(8,128)(2,1)S(1)}, bf16[1024,768]{1,0:T(8,128)(2,1)}, s32[]{:T(128)}, ...), branch_computations={%region_19.26_spmd.clone, %region_27.30_spmd, %region_31.44_spmd.c... | conditional | flops 19091017728 | bytes 786352704 | solution.py:549
  843.2 15.5 collective-permute-done.1
  865.6 33.0 %conditional.7 = (bf16[512,768]{1,0:T(8,128)(2,1)}, f32[8,768,768]{2,1,0:T(8,128)}, f32[5,768]{1,0:T(8,128)}, f32[2,32,12]{1,2,0:T(8,128)}, bf16[1,512,768]{2,1,0:T(8,128)(2,1)}) conditional(s32[]{:T(128)} %clamp.12, (bf16[512,768]{1,0:T(8,128)(2,1)S(1)}, bf16[1024,768]{1,0:T(8,128)(2,1)}, s32[]{:T(128)}, ...), branch_computations={%region_19.26_spmd.clone, %region_27.30_spmd, %region_31.44_spmd.c... | conditional | flops 19091017728 | bytes 786352704 | solution.py:549
  902.1 24.8 %collective-permute-done.1 = bf16[512,768]{1,0:T(8,128)(2,1)S(1)} collective-permute-done((bf16[512,768]{1,0:T(8,128)(2,1)}, bf16[512,768]{1,0:T(8,128)(2,1)S(1)}, u32[]{:S(2)}, u32[]{:S(2)}) %collective-permute-start.1) | collective-permute-done | bytes 786464 | tf_op jit(solution)/shard_map/while/body/eval_jaxpr/ppermute | solution.py:29
  933.8 33.0 %conditional.7 = (bf16[512,768]{1,0:T(8,128)(2,1)}, f32[8,768,768]{2,1,0:T(8,128)}, f32[5,768]{1,0:T(8,128)}, f32[2,32,12]{1,2,0:T(8,128)}, bf16[1,512,768]{2,1,0:T(8,128)(2,1)}) conditional(s32[]{:T(128)} %clamp.12, (bf16[512,768]{1,0:T(8,128)(2,1)S(1)}, bf16[1024,768]{1,0:T(8,128)(2,1)}, s32[]{:T(128)}, ...), branch_computations={%region_19.26_spmd.clone, %region_27.30_spmd, %region_31.44_spmd.c... | conditional | flops 19091017728 | bytes 786352704 | solution.py:549
  970.3 526.9 %collective-permute-done.1 = bf16[512,768]{1,0:T(8,128)(2,1)S(1)} collective-permute-done((bf16[512,768]{1,0:T(8,128)(2,1)}, bf16[512,768]{1,0:T(8,128)(2,1)S(1)}, u32[]{:S(2)}, u32[]{:S(2)}) %collective-permute-start.1) | collective-permute-done | bytes 786464 | tf_op jit(solution)/shard_map/while/body/eval_jaxpr/ppermute | solution.py:29
  1504.2 243.8 %conditional.7 = (bf16[512,768]{1,0:T(8,128)(2,1)}, f32[8,768,768]{2,1,0:T(8,128)}, f32[5,768]{1,0:T(8,128)}, f32[2,32,12]{1,2,0:T(8,128)}, bf16[1,512,768]{2,1,0:T(8,128)(2,1)}) conditional(s32[]{:T(128)} %clamp.12, (bf16[512,768]{1,0:T(8,128)(2,1)S(1)}, bf16[1024,768]{1,0:T(8,128)(2,1)}, s32[]{:T(128)}, ...), branch_computations={%region_19.26_spmd.clone, %region_27.30_spmd, %region_31.44_spmd.c... | conditional | flops 19091017728 | bytes 786352704 | solution.py:549
  1629.3 34.7 %reshape.1177 = bf16[12,523776]{1,0:T(8,128)(2,1)} reshape(bf16[12,512,1023]{2,1,0:T(8,128)(2,1)} %pad.49.clone) | data formatting | bytes 25141248 | tf_op jit(solution)/shard_map/while/body/eval_jaxpr/cond/branch_0_fun/reshape | solution.py:64
  1672.6 35.9 %copy.484 = f32[2,8,512,1024]{3,2,1,0:T(8,128)} copy(f32[2,8,512,1024]{3,1,2,0:T(8,128)S(1)} %bitcast.602) | data formatting | bytes 67108864 | tf_op jit(solution)/shard_map/while/body/eval_jaxpr/cond
  1751.3 98.7 %collective-permute-done.1 = bf16[512,768]{1,0:T(8,128)(2,1)S(1)} collective-permute-done((bf16[512,768]{1,0:T(8,128)(2,1)}, bf16[512,768]{1,0:T(8,128)(2,1)S(1)}, u32[]{:S(2)}, u32[]{:S(2)}) %collective-permute-start.1) | collective-permute-done | bytes 786464 | tf_op jit(solution)/shard_map/while/body/eval_jaxpr/ppermute | solution.py:29
  1857.0 243.8 %conditional.7 = (bf16[512,768]{1,0:T(8,128)(2,1)}, f32[8,768,768]{2,1,0:T(8,128)}, f32[5,768]{1,0:T(8,128)}, f32[2,32,12]{1,2,0:T(8,128)}, bf16[1,512,768]{2,1,0:T(8,128)(2,1)}) conditional(s32[]{:T(128)} %clamp.12, (bf16[512,768]{1,0:T(8,128)(2,1)S(1)}, bf16[1024,768]{1,0:T(8,128)(2,1)}, s32[]{:T(128)}, ...), branch_computations={%region_19.26_spmd.clone, %region_27.30_spmd, %region_31.44_spmd.c... | conditional | flops 19091017728 | bytes 786352704 | solution.py:549
  1982.2 34.7 %reshape.1177 = bf16[12,523776]{1,0:T(8,128)(2,1)} reshape(bf16[12,512,1023]{2,1,0:T(8,128)(2,1)} %pad.49.clone) | data formatting | bytes 25141248 | tf_op jit(solution)/shard_map/while/body/eval_jaxpr/cond/branch_0_fun/reshape | solution.py:64
  2025.4 35.9 %copy.484 = f32[2,8,512,1024]{3,2,1,0:T(8,128)} copy(f32[2,8,512,1024]{3,1,2,0:T(8,128)S(1)} %bitcast.602) | data formatting | bytes 67108864 | tf_op jit(solution)/shard_map/while/body/eval_jaxpr/cond
  2119.8 122.1 %reduce-scatter.2.cloned.1.call-done = f32[8,96,768]{2,1,0:T(8,128)} async-done(((f32[8,768,768]{2,1,0:T(8,128)}), f32[8,96,768]{2,1,0:T(8,128)}) %reduce-scatter.2.cloned.1.call-update) | async-done | bytes 2359312 | tf_op jit(solution)/shard_map/reduce_scatter | solution.py:582
  2253.1 103.2 %all-reduce.6 = (f32[5,768]{1,0:T(8,128)S(1)}, f32[2,32,12]{1,2,0:T(8,128)S(1)}) all-reduce(f32[5,768]{1,0:T(8,128)} %get-tuple-element.962, f32[2,32,12]{1,2,0:T(8,128)} %get-tuple-element.964), channel_id=1, replica_groups=mesh['wide'=8,'narrow'=4] {'wide','narrow'}, use_global_device_ids=true, to_apply=%region_51.52 | all-reduce | flops 4608 | bytes 36864 | tf_op jit(solution)/shard_map/psum | solution.py:586
  (452 shorter events, 723.8 us)
Async XLA Ops:
  7.2 39.5 %copy-start = (bf16[32,12]{0,1:T(8,128)(2,1)S(1)}, bf16[32,12]{0,1:T(8,128)(2,1)}, u32[]{:S(2)}) copy-start(bf16[32,12]{0,1:T(8,128)(2,1)} %param.68) | copy-start | bytes 2308
  7.3 347.3 %all-gather.6.cloned.1.call-start = ((), (), s32[]{:S(2)}) async-start(), calls=%async_computation.4 | async-start | bytes 10616832 | tf_op jit(solution)/shard_map/all_gather | solution.py:336
  45.4 2196.4 %reduce-scatter.2.cloned.1.call-start = ((), (), s32[]{:S(2)}) async-start(), calls=%async_computation.2 | async-start | bytes 21233664 | tf_op jit(solution)/shard_map/reduce_scatter | solution.py:582
  189.0 12.7 copy-start.51
  189.0 12.7 copy-start.68
  341.9 12.7 copy-start.72
  341.9 12.7 copy-start.73
  431.8 19.3 collective-permute-start
  437.9 15.3 copy-start.30
  437.9 15.3 copy-start.35
  517.8 18.7 collective-permute-start
  523.9 14.7 copy-start.30
  523.9 14.7 copy-start.35
  565.3 21.3 collective-permute-start
  573.6 15.0 copy-start.30
  573.6 15.0 copy-start.35
  608.6 52.0 %collective-permute-start = (bf16[512,768]{1,0:T(8,128)(2,1)}, bf16[512,768]{1,0:T(8,128)(2,1)}, u32[]{:S(2)}, u32[]{:S(2)}) collective-permute-start(bf16[512,768]{1,0:T(8,128)(2,1)} %get-tuple-element.1790), channel_id=1, source_target_pairs={{0,1},{1,2},{2,3},{4,5},{5,6},{6,7},{8,9},{9,10},{10,11},{12,13},{... | collective-permute-start | bytes 2359304 | tf_op jit(solution)/shard_map/while/body/eval_jaxpr/ppermute | solution.py:29
  648.6 14.1 copy-start.30
  648.6 14.1 copy-start.35
  689.4 95.1 %collective-permute-start = (bf16[512,768]{1,0:T(8,128)(2,1)}, bf16[512,768]{1,0:T(8,128)(2,1)}, u32[]{:S(2)}, u32[]{:S(2)}) collective-permute-start(bf16[512,768]{1,0:T(8,128)(2,1)} %get-tuple-element.1790), channel_id=1, source_target_pairs={{0,1},{1,2},{2,3},{4,5},{5,6},{6,7},{8,9},{9,10},{10,11},{12,13},{... | collective-permute-start | bytes 2359304 | tf_op jit(solution)/shard_map/while/body/eval_jaxpr/ppermute | solution.py:29
  773.4 13.1 copy-start.30
  773.4 13.1 copy-start.35
  839.8 18.9 collective-permute-start.1
  898.7 28.2 %collective-permute-start.1 = (bf16[512,768]{1,0:T(8,128)(2,1)}, bf16[512,768]{1,0:T(8,128)(2,1)S(1)}, u32[]{:S(2)}, u32[]{:S(2)}) collective-permute-start(bf16[512,768]{1,0:T(8,128)(2,1)} %get-tuple-element.1819), channel_id=1, source_target_pairs={{1,0},{2,1},{3,2},{5,4},{6,5},{7,6},{9,8},{10,9},{11,10},{13,12},{... | collective-permute-start | bytes 2359304 | tf_op jit(solution)/shard_map/while/body/eval_jaxpr/ppermute | solution.py:29
  966.9 530.3 %collective-permute-start.1 = (bf16[512,768]{1,0:T(8,128)(2,1)}, bf16[512,768]{1,0:T(8,128)(2,1)S(1)}, u32[]{:S(2)}, u32[]{:S(2)}) collective-permute-start(bf16[512,768]{1,0:T(8,128)(2,1)} %get-tuple-element.1819), channel_id=1, source_target_pairs={{1,0},{2,1},{3,2},{5,4},{6,5},{7,6},{9,8},{10,9},{11,10},{13,12},{... | collective-permute-start | bytes 2359304 | tf_op jit(solution)/shard_map/while/body/eval_jaxpr/ppermute | solution.py:29
  1529.9 13.1 slice-start.14
  1747.9 102.1 %collective-permute-start.1 = (bf16[512,768]{1,0:T(8,128)(2,1)}, bf16[512,768]{1,0:T(8,128)(2,1)S(1)}, u32[]{:S(2)}, u32[]{:S(2)}) collective-permute-start(bf16[512,768]{1,0:T(8,128)(2,1)} %get-tuple-element.1819), channel_id=1, source_target_pairs={{1,0},{2,1},{3,2},{5,4},{6,5},{7,6},{9,8},{10,9},{11,10},{13,12},{... | collective-permute-start | bytes 2359304 | tf_op jit(solution)/shard_map/while/body/eval_jaxpr/ppermute | solution.py:29
  1882.7 13.1 slice-start.14
  2100.8 15.6 collective-permute-start.1
  2119.7 125.0 %copy-start.31 = (bf16[2,512,768]{2,1,0:T(8,128)(2,1)S(1)}, bf16[2,512,768]{2,1,0:T(8,128)(2,1)}, u32[]{:S(2)}) copy-start(bf16[2,512,768]{2,1,0:T(8,128)(2,1)} %get-tuple-element.961) | copy-start | bytes 4718596
  2119.7 247.7 %all-gather.4.cloned.1.call-start = ((), (), s32[]{:S(2)}) async-start(), calls=%async_computation.3 | async-start | bytes 5898240 | tf_op jit(solution)/shard_map/all_gather | solution.py:583
  2248.5 109.1 %all-to-all-start = ((bf16[1024,4,192]{0,2,1:T(8,128)(2,1)}), bf16[1024,4,192]{0,2,1:T(8,128)(2,1)S(1)}, u32[]{:S(2)}, u32[]{:S(2)}) async-start(bf16[1024,4,192]{0,2,1:T(8,128)(2,1)} %all_to_all.12), calls=%async_computation | async-start | bytes 3145728 | tf_op jit(solution)/shard_map/all_to_all | solution.py:588
  (74 other events, 392.9 us)
Sparse Core Ops, SparseCore 0:
  45.6 60.2 all-gather.5
  2119.8 121.9 reduce-scatter.1
  2244.8 122.5 all-gather.3
where the time goes:
time: 2400 us; the launch traced here: 2380 us
  waiting for transfers between devices  864 us (36%)
  local copies, waits for them, and re-layouts  669 us (28%)
  loops' own time  261 us (11%)
  matrix products  229 us (10%)
  starting transfers between devices  140 us (6%)
  other arithmetic  103 us (4%)
  blocking collectives  103 us (4%)
    ppermute x10, waiting for transfers between devices, passed_along(): return lax.ppermute(shard, axis, pairs)  733 us
    another operation x5, loops' own time, backward_tick(): lax.switch(branch_index, backward_branches, grad_in, stored_rows, mid_row...  150 us
    ppermute x10, starting transfers between devices, passed_along(): return lax.ppermute(shard, axis, pairs)  135 us
    reduce_scatter x1, waiting for transfers between devices, on_device(): lax.psum_scatter(grad_acc, 'wide', scatter_dimension=1, tiled=True)  122 us
    psum x1, blocking collectives, on_device(): lax.psum((gain_sums, table_sums), ('wide', 'narrow'))  103 us
    unnamed x63, local copies, waits for them, and re-layouts  103 us
    cond x42, local copies, waits for them, and re-layouts  100 us
    another operation x5, loops' own time, forward_tick(): lax.switch(branch_index, forward_branches, incoming, enc_rows, dec_rows,...  95.8 us
  transfers between devices with their start and end apart: 14, of which 12 were waited for; matrix products, arithmetic and copies ran while one was open for 14% of the time, Pallas kernels for 0%

commit v1 on v0

v1 whole, which is shorter than its diff:
```python
import functools

import jax
import jax.numpy as jnp
import numpy as np
from jax import lax
from jax.experimental import pallas as pl
from jax.experimental.pallas import tpu as pltpu
from jax.sharding import PartitionSpec as P

D = 768
HEADS = 12
HEAD = 64
PAIRS = HEADS // 2
FF = 3072
BUCKETS = 32
MAXDIST = 128
LEN = 512
TILE = 128
BLOCKS = LEN // TILE
CHUNK = 512

EPSILON = 1e-06
MASKED = -1000000000.0
VMEM_LIMIT = 60 * 1024 * 1024
f32 = jnp.float32
bf16 = jnp.bfloat16


def bucket_of(reverse, both_ways):
    result = np.zeros(reverse.shape, np.int64)
    if both_ways:
        half_count = BUCKETS // 2
        result = result + (reverse < 0) * half_count
        reverse = np.abs(reverse)
    else:
        half_count = BUCKETS
        reverse = np.maximum(reverse, 0)
    exact_count = half_count // 2
    scaled = (
        np.log(np.maximum(reverse, 1) / exact_count)
        / np.log(MAXDIST / exact_count)
        * (half_count - exact_count)
    )
    far_bucket = np.minimum(
        exact_count + np.floor(np.maximum(scaled, 0.0)).astype(np.int64), half_count - 1
    )
    return result + np.where(reverse < exact_count, reverse, far_bucket)


def tile_ids(both_ways):
    i = np.arange(TILE)[:, None]
    j = np.arange(TILE)[None, :]
    tiles = []
    for step in (0, 1, -1):
        n = i - j + step * TILE
        ids = bucket_of(n, both_ways)
        tiles.append(ids if both_ways else np.where(n < 0, BUCKETS, ids))
    far = bucket_of(np.array([2 * TILE - TILE + 1, -(2 * TILE - TILE + 1)]), both_ways)
    if not both_ways:
        far[1] = BUCKETS
    return np.stack(tiles).astype(np.int32), far.astype(np.int32)


def dot(a, b):
    return jnp.dot(a, b, preferred_element_type=f32)


def dot_nt(a, b):
    return lax.dot_general(a, b, (((1,), (1,)), ((), ())), preferred_element_type=f32)


def rms(v, gain):
    return v * lax.rsqrt(jnp.mean(v * v, axis=-1, keepdims=True) + EPSILON) * gain


def rms_back(v, gain, dy):
    r = lax.rsqrt(jnp.mean(v * v, axis=-1, keepdims=True) + EPSILON)
    dgain = jnp.sum(dy * v * r, axis=0, keepdims=True)
    gdy = dy * gain
    dv = r * gdy - v * (r * r * r * jnp.mean(gdy * v, axis=-1, keepdims=True))
    return dv, dgain


def half_lanes(value, which):
    lane = lax.broadcasted_iota(jnp.int32, value.shape, 1)
    return jnp.where((lane // HEAD) == which, value, jnp.zeros_like(value))


def tile_of(step):
    return {0: 0, 1: 1, -1: 2}.get(step)


def attn_fwd_kernel(has_bias, *refs):
    refs = list(refs)
    src, gain = refs[:2]
    refs = refs[2:]
    ksrc = None
    if not has_bias:
        ksrc = refs.pop(0)
    w, segr, segc = refs[:3]
    refs = refs[3:]
    if has_bias:
        bias, far = refs[:2]
        refs = refs[2:]
    z, q_o, k_o, v_o, o_o, p_o, q_s, k_s, v_s, o_s = refs

    a = rms(src[...].astype(f32), gain[...]).astype(bf16)
    b = a if ksrc is None else ksrc[...]
    for value, weight, out, scr in ((a, 0, q_o, q_s), (b, 1, k_o, k_s), (b, 2, v_o, v_s)):
        full = dot(value, w[weight]).astype(bf16)
        out[...] = full
        for p in range(PAIRS):
            scr[p] = full[:, p * TILE : (p + 1) * TILE]

    def pair(p, carry):
        qp, kp, vp = q_s[p], k_s[p], v_s[p]
        total = [None] * BLOCKS
        for which in range(2):
            h = 2 * p + which
            kz, vz = half_lanes(kp, which), half_lanes(vp, which)
            for bi in range(BLOCKS):
                rows = slice(bi * TILE, (bi + 1) * TILE)
                s = dot_nt(qp[rows], kz)
                if has_bias:
                    parts = []
                    for bj in range(BLOCKS):
                        step = bi - bj
                        part = s[:, bj * TILE : (bj + 1) * TILE]
                        if abs(step) < 2:
                            part = part + bias[h, tile_of(step)]
                        else:
                            part = part + far[h, 0 if step > 0 else 1]
                        parts.append(part)
                    s = jnp.concatenate(parts, axis=1)
                s = jnp.where(segc[rows] == segr[...], s, MASKED)
                e = jnp.exp(s - jnp.max(s, axis=-1, keepdims=True))
                prob = (e * (1.0 / jnp.sum(e, axis=-1, keepdims=True))).astype(bf16)
                p_o[h, rows, :] = prob
                o = dot(prob, vz)
                total[bi] = o if total[bi] is None else total[bi] + o
        o_s[p] = jnp.concatenate(total, axis=0).astype(bf16)
        return carry

    lax.fori_loop(0, PAIRS, pair, 0)
    mixed = jnp.concatenate([o_s[p] for p in range(PAIRS)], axis=1)
    o_o[...] = mixed
    z[...] = src[...].astype(f32) + dot(mixed, w[3])


def attn_fwd(src, gain, w, segr, segc, ksrc=None, bias=None, far=None):
    has_bias = bias is not None
    args = [src, gain] + ([] if has_bias else [ksrc]) + [w, segr, segc]
    vm = pl.BlockSpec(memory_space=pltpu.VMEM)
    specs = [vm] * len(args)
    if has_bias:
        args += [bias, far]
        specs += [vm, pl.BlockSpec(memory_space=pltpu.SMEM)]
    rows = jax.ShapeDtypeStruct((LEN, D), bf16)
    return pl.pallas_call(
        functools.partial(attn_fwd_kernel, has_bias),
        out_shape=(
            jax.ShapeDtypeStruct((LEN, D), f32),
            rows,
            rows,
            rows,
            rows,
            jax.ShapeDtypeStruct((HEADS, LEN, LEN), bf16),
        ),
        in_specs=specs,
        out_specs=(vm,) * 6,
        scratch_shapes=[pltpu.VMEM((PAIRS, LEN, TILE), bf16)] * 4,
        compiler_params=pltpu.CompilerParams(vmem_limit_bytes=VMEM_LIMIT),
        name="self_fwd" if has_bias else "cross_fwd",
    )(*args)


def attn_bwd_kernel(has_bias, *refs):
    refs = list(refs)
    gres, src, gain = refs[:3]
    refs = refs[3:]
    ksrc = None
    if not has_bias:
        ksrc = refs.pop(0)
    w, q_i, k_i, v_i, o_i, p_i = refs[:6]
    refs = refs[6:]
    din, dw, dgain = refs[:3]
    refs = refs[3:]
    if has_bias:
        dtile, dfar = refs[:2]
        refs = refs[2:]
    else:
        dkey = refs.pop(0)
    q_s, k_s, v_s, do_s, dq_s, dk_s, dv_s, ds_s = refs

    g = gres[...].astype(bf16)
    do = dot_nt(g, w[3]).astype(bf16)
    for value, scr in ((q_i[...], q_s), (k_i[...], k_s), (v_i[...], v_s), (do, do_s)):
        for p in range(PAIRS):
            scr[p] = value[:, p * TILE : (p + 1) * TILE]

    def pair(p, carry):
        qp, kp, vp, dop = q_s[p], k_s[p], v_s[p], do_s[p]
        q_t, do_t = qp.T, dop.T
        total = [None] * BLOCKS
        for which in range(2):
            h = 2 * p + which
            kz, vz = half_lanes(kp, which), half_lanes(vp, which)
            diag = {0: None, 1: None, -1: None, 2: None, -2: None}
            for bi in range(BLOCKS):
                rows = slice(bi * TILE, (bi + 1) * TILE)
                dp = dot_nt(dop[rows], vz)
                prob = p_i[h, rows, :].astype(f32)
                t = prob * dp
                ds = t - prob * jnp.sum(t, axis=-1, keepdims=True)
                if has_bias:
                    for bj in range(BLOCKS):
                        step = max(-2, min(2, bi - bj))
                        part = ds[:, bj * TILE : (bj + 1) * TILE]
                        diag[step] = part if diag[step] is None else diag[step] + part
                low = ds.astype(bf16)
                ds_s[which, rows, :] = low
                dq = dot(low, kz)
                total[bi] = dq if total[bi] is None else total[bi] + dq
            if has_bias:
                for step in (0, 1, -1):
                    dtile[h, tile_of(step)] = diag[step]
                for n, step in ((0, 2), (1, -2)):
                    dfar[h, n : n + 1, :] = jnp.sum(diag[step], axis=0, keepdims=True)
            half = slice(which * HEAD, (which + 1) * HEAD)
            dk_s[p, half, :] = dot(q_t[half], ds_s[which]).astype(bf16)
            dv_s[p, half, :] = dot(do_t[half], p_i[h]).astype(bf16)
        dq_s[p] = jnp.concatenate(total, axis=0).astype(bf16)
        return carry

    lax.fori_loop(0, PAIRS, pair, 0)
    v = src[...].astype(f32)
    a = rms(v, gain[...]).astype(bf16)
    a_t = a.T
    b_t = a_t if ksrc is None else ksrc[...].T
    dq = jnp.concatenate([dq_s[p] for p in range(PAIRS)], axis=1)
    dk_t = dk_s[...].reshape(D, LEN)
    dv_t = dv_s[...].reshape(D, LEN)
    query_side = dot_nt(dq, w[0])
    key_side = dot_nt(dk_t.T, w[1]) + dot_nt(dv_t.T, w[2])
    if has_bias:
        query_side = query_side + key_side
    else:
        dkey[...] = key_side.astype(bf16)
    dv, dg = rms_back(v, gain[...], query_side)
    dgain[...] = dg
    din[...] = gres[...].astype(f32) + dv
    dw[0] = dot(a_t, dq).astype(bf16)
    dw[1] = dot_nt(b_t, dk_t).astype(bf16)
    dw[2] = dot_nt(b_t, dv_t).astype(bf16)
    dw[3] = dot(o_i[...].T, g).astype(bf16)


def attn_bwd(gres, src, gain, w, saved, ksrc=None):
    has_bias = ksrc is None
    args = [gres, src, gain] + ([] if has_bias else [ksrc]) + [w, *saved]
    vm = pl.BlockSpec(memory_space=pltpu.VMEM)
    outs = [
        jax.ShapeDtypeStruct((LEN, D), f32),
        jax.ShapeDtypeStruct((4, D, D), bf16),
        jax.ShapeDtypeStruct((1, D), f32),
    ]
    if has_bias:
        outs += [
            jax.ShapeDtypeStruct((HEADS, 3, TILE, TILE), f32),
            jax.ShapeDtypeStruct((HEADS, 2, TILE), f32),
        ]
    else:
        outs += [jax.ShapeDtypeStruct((LEN, D), bf16)]
    return pl.pallas_call(
        functools.partial(attn_bwd_kernel, has_bias),
        out_shape=tuple(outs),
        in_specs=[vm] * len(args),
        out_specs=(vm,) * len(outs),
        scratch_shapes=[pltpu.VMEM((PAIRS, LEN, TILE), bf16)] * 5
        + [pltpu.VMEM((PAIRS, TILE, LEN), bf16)] * 2
        + [pltpu.VMEM((2, LEN, LEN), bf16)],
        compiler_params=pltpu.CompilerParams(vmem_limit_bytes=VMEM_LIMIT),
        name="self_bwd" if has_bias else "cross_bwd",
    )(*args)


GELU_C = float(np.sqrt(2.0 / np.pi))


def gelu_parts(u):
    inner = GELU_C * (u + 0.044715 * (u * u * u))
    t = jnp.tanh(inner)
    h = 0.5 * u * (1.0 + t)
    slope = 0.5 * (1.0 + t) + 0.5 * u * (1.0 - t * t) * GELU_C * (1.0 + 3 * 0.044715 * (u * u))
    return h, slope


def ffn_fwd_kernel(x, gain, wi, wo, out, n_s, acc):
    step = pl.program_id(0)

    @pl.when(step == 0)
    def _():
        v = x[...].astype(f32)
        n_s[...] = rms(v, gain[...]).astype(bf16)
        acc[...] = v

    h, _ = gelu_parts(dot(n_s[...], wi[...]))
    acc[...] += dot(h.astype(bf16), wo[...])

    @pl.when(step == pl.num_programs(0) - 1)
    def _():
        out[...] = acc[...].astype(bf16)


def ffn_fwd(x, gain, wi, wo):
    whole = pl.BlockSpec((LEN, D), lambda c: (0, 0))
    return pl.pallas_call(
        ffn_fwd_kernel,
        grid=(FF // CHUNK,),
        out_shape=jax.ShapeDtypeStruct((LEN, D), bf16),
        in_specs=[
            whole,
            pl.BlockSpec((1, D), lambda c: (0, 0)),
            pl.BlockSpec((D, CHUNK), lambda c: (0, c)),
            pl.BlockSpec((CHUNK, D), lambda c: (c, 0)),
        ],
        out_specs=whole,
        scratch_shapes=[pltpu.VMEM((LEN, D), bf16), pltpu.VMEM((LEN, D), f32)],
        compiler_params=pltpu.CompilerParams(vmem_limit_bytes=VMEM_LIMIT),
        name="ffn_fwd",
    )(x, gain, wi, wo)


def ffn_both_kernel(x, gain, g, wi, wo, out, dx, dgain, dwi, dwo, n_s, nt_s, acc, dn):
    step = pl.program_id(0)

    @pl.when(step == 0)
    def _():
        v = x[...].astype(f32)
        n = rms(v, gain[...]).astype(bf16)
        n_s[...] = n
        nt_s[...] = n.T
        acc[...] = v
        dn[...] = jnp.zeros_like(dn)

    h, slope = gelu_parts(dot(n_s[...], wi[...]))
    h = h.astype(bf16)
    acc[...] += dot(h, wo[...])
    dh = dot_nt(g[...], wo[...])
    du = (slope * dh).astype(bf16)
    dn[...] += dot_nt(du, wi[...])
    dwo[...] = dot(h.T, g[...]).astype(bf16)
    dwi[...] = dot(nt_s[...], du).astype(bf16)

    @pl.when(step == pl.num_programs(0) - 1)
    def _():
        out[...] = acc[...].astype(bf16)
        dv, dg = rms_back(x[...].astype(f32), gain[...], dn[...])
        dgain[...] = dg
        dx[...] = (g[...].astype(f32) + dv).astype(bf16)


def ffn_both(x, gain, g, wi, wo):
    whole = pl.BlockSpec((LEN, D), lambda c: (0, 0))
    one = pl.BlockSpec((1, D), lambda c: (0, 0))
    in_part = pl.BlockSpec((D, CHUNK), lambda c: (0, c))
    out_part = pl.BlockSpec((CHUNK, D), lambda c: (c, 0))
    rows = jax.ShapeDtypeStruct((LEN, D), bf16)
    return pl.pallas_call(
        ffn_both_kernel,
        grid=(FF // CHUNK,),
        out_shape=(
            rows,
            rows,
            jax.ShapeDtypeStruct((1, D), f32),
            jax.ShapeDtypeStruct((D, FF), bf16),
            jax.ShapeDtypeStruct((FF, D), bf16),
        ),
        in_specs=[whole, one, whole, in_part, out_part],
        out_specs=(whole, whole, one, in_part, out_part),
        scratch_shapes=[
            pltpu.VMEM((LEN, D), bf16),
            pltpu.VMEM((D, LEN), bf16),
            pltpu.VMEM((LEN, D), f32),
            pltpu.VMEM((LEN, D), f32),
        ],
        compiler_params=pltpu.CompilerParams(vmem_limit_bytes=VMEM_LIMIT),
        name="ffn_both",
    )(x, gain, g, wi, wo)


ALL = (0, 1, 2, 3)
ENC = (1, 2)
DEC = (0, 3)


def across(x, flip, planes):
    wide, narrow = lax.axis_size("wide"), lax.axis_size("narrow")
    pairs = [(i * narrow + n, (i ^ flip) * narrow + n) for i in range(wide) for n in planes]
    return lax.ppermute(x, ("wide", "narrow"), pairs)


def between(x, pairs):
    return lax.ppermute(x, "narrow", pairs)


def add(a, *others):
    total = a.astype(f32)
    for other in others:
        total = total + other.astype(f32)
    return total.astype(bf16)


def gathered(shard, planes=ALL):
    wide = lax.axis_size("wide")
    if wide != 8:
        return lax.all_gather(shard, "wide", axis=1, tiled=True)
    k, r, c = shard.shape
    h = r // 2
    me = lax.axis_index("wide")
    px = across(shard, 2, planes)
    py = across(shard, 4, planes)
    pc = across(shard, 1, planes)
    pd = jnp.concatenate([across(px[:, :h], 4, planes), across(py[:, h:], 2, planes)], axis=1)
    pieces = {0: shard, 2: px, 4: py, 6: pd, 1: pc}
    for flip in (2, 4, 6):
        pieces[flip ^ 1] = across(pieces[flip], 1, planes)
    full = jnp.zeros((k, 8, r, c), shard.dtype)
    for flip, piece in pieces.items():
        full = lax.dynamic_update_slice(full, piece[:, None], (0, me ^ flip, 0, 0))
    return full.reshape(k, 8 * r, c)


def scattered(full, planes=ALL):
    wide = lax.axis_size("wide")
    k, rows, c = full.shape
    r = rows // wide
    if wide != 8:
        return lax.psum_scatter(full, "wide", scatter_dimension=1, tiled=True)
    h = r // 2
    me = lax.axis_index("wide")
    blocks = full.reshape(k, 8, r, c)

    def block(flip):
        return lax.dynamic_slice(blocks, (0, me ^ flip, 0, 0), (k, 1, r, c))[:, 0]

    part = {f: add(block(f), across(block(f ^ 1), 1, planes)) for f in (6, 2, 4, 0)}
    to_y = across(part[6][:, :h], 2, planes)
    to_x = across(part[6][:, h:], 4, planes)
    for_x = jnp.concatenate([part[2][:, :h], add(part[2][:, h:], to_x)], axis=1)
    for_y = jnp.concatenate([add(part[4][:, :h], to_y), part[4][:, h:]], axis=1)
    return add(part[0], across(for_x, 2, planes), across(for_y, 4, planes))


def from_encoder(share, middle):
    total = add(share, between(share, [(1, 2), (2, 1)]))
    return jnp.where(middle, total, between(total, [(1, 0), (2, 3)]))


def from_decoder(share, middle):
    return from_encoder(between(share, [(0, 1), (3, 2)]), middle)


def summed(x):
    if lax.axis_size("wide") != 8:
        return lax.psum(x, ("wide", "narrow"))
    for flip in (1, 2, 4):
        x = x + across(x, flip, ALL)
    for flip in (1, 2):
        x = x + between(x, [(n, n ^ flip) for n in range(4)])
    return x


def on_device(
    enc_in,
    dec_in,
    dec_cot,
    segments,
    enc_attn_gain,
    enc_query,
    enc_key,
    enc_value,
    enc_output,
    enc_table,
    enc_ffn_gain,
    enc_ffn_in,
    enc_ffn_out,
    dec_self_gain,
    dec_query,
    dec_key,
    dec_value,
    dec_output,
    dec_table,
    dec_cross_gain,
    cross_query,
    cross_key,
    cross_value,
    cross_output,
    dec_ffn_gain,
    dec_ffn_in,
    dec_ffn_out,
):
    plane = lax.axis_index("narrow")
    is_enc = (plane == 1) | (plane == 2)
    row = plane // 2

    def own(x):
        return lax.dynamic_slice_in_dim(x, row * LEN, LEN, 0)

    def pick(enc, dec):
        return jnp.where(is_enc, enc, dec)

    def gain_of(g):
        return g.astype(f32).reshape(1, D)

    seg = lax.dynamic_slice_in_dim(segments, row, 1, 0)
    segr, segc = seg, seg.reshape(LEN, 1)
    src = pick(own(enc_in), own(dec_in))
    cot = own(dec_cot)

    w_attn = gathered(
        jnp.stack(
            [
                pick(enc_query, dec_query),
                pick(enc_key, dec_key),
                pick(enc_value, dec_value),
                pick(enc_output, dec_output),
            ]
        )
    )
    w_in = gathered(pick(enc_ffn_in, dec_ffn_in)[None])[0]
    w_out = gathered(pick(enc_ffn_out, dec_ffn_out)[None])[0]
    w_cross = gathered(jnp.stack([cross_query, cross_key, cross_value, cross_output]), DEC)

    enc_ids, enc_far = tile_ids(True)
    dec_ids, dec_far = tile_ids(False)
    ids = pick(jnp.asarray(enc_ids), jnp.asarray(dec_ids))
    far_ids = pick(jnp.asarray(enc_far), jnp.asarray(dec_far))
    buckets = jnp.arange(BUCKETS + 1, dtype=jnp.int32)
    hot = (ids[None] == buckets[:, None, None, None]).astype(bf16)
    far_hot = (far_ids[None] == buckets[:, None]).astype(bf16)
    table = jnp.concatenate([pick(enc_table, dec_table), jnp.full((1, HEADS), MASKED, bf16)])
    bias = jnp.einsum("bh,bsij->hsij", table, hot, preferred_element_type=f32)
    far = jnp.einsum("bh,bs->hs", table, far_hot, preferred_element_type=f32)

    gain_a = pick(gain_of(enc_attn_gain), gain_of(dec_self_gain))
    z1, *saved = attn_fwd(src, gain_a, w_attn, segr, segc, bias=bias, far=far)
    x1 = z1.astype(bf16)
    enc_gain = gain_of(enc_ffn_gain)
    enc_out = ffn_fwd(x1, enc_gain, w_in, w_out)
    memory = between(enc_out, [(1, 0), (2, 3)])
    gain_c = gain_of(dec_cross_gain)
    z2, *saved_c = attn_fwd(z1, gain_c, w_cross, segr, segc, ksrc=memory)
    z2 = z2.astype(bf16)

    dec_out, gz2, dgain_df, dwi_d, dwo_d = ffn_both(z2, gain_of(dec_ffn_gain), cot, w_in, w_out)
    gz1, dw_c, dgain_c, genc_out = attn_bwd(gz2, z1, gain_c, w_cross, saved_c, ksrc=memory)
    genc = between(genc_out, [(0, 1), (3, 2)])
    _, gx1, dgain_ef, dwi_e, dwo_e = ffn_both(x1, enc_gain, genc, w_in, w_out)
    gres = pick(gx1.astype(f32), gz1)
    din, dw_a, dgain_a, dtile, dfar = attn_bwd(gres, src, gain_a, w_attn, saved)

    def ffn_shares(dwi, dwo, planes):
        return scattered(dwi[None], planes)[0], scattered(dwo[None], planes)[0]

    si_d, so_d = ffn_shares(dwi_d, dwo_d, DEC)
    s_c = scattered(dw_c, DEC)
    si_e, so_e = ffn_shares(dwi_e, dwo_e, ENC)
    s_a = scattered(dw_a)
    gi_d, go_d, g_c, g_s = (from_decoder(s, is_enc).astype(f32) for s in (si_d, so_d, s_c, s_a))
    gi_e, go_e, g_e = (from_encoder(s, is_enc).astype(f32) for s in (si_e, so_e, s_a))

    dtable = jnp.einsum("hsij,bsij->bh", dtile.astype(bf16), hot, preferred_element_type=f32)
    dtable = dtable + jnp.einsum("hsj,bs->bh", dfar, far_hot.astype(f32))
    dtable = jnp.pad(dtable[:BUCKETS].reshape(1, BUCKETS * HEADS), ((0, 0), (0, D - BUCKETS * HEADS)))
    none = jnp.zeros((1, D), f32)

    def when_enc(x):
        return jnp.where(is_enc, x, 0.0)

    def when_dec(x):
        return jnp.where(is_enc, 0.0, x)

    small = jnp.concatenate(
        [
            when_enc(dgain_a),
            when_enc(dgain_ef),
            when_dec(dgain_a),
            when_dec(dgain_c),
            when_dec(dgain_df),
            when_enc(dtable),
            when_dec(dtable),
            none,
        ]
    )
    small = summed(small)
    tables = small[5:7, : BUCKETS * HEADS].reshape(2, BUCKETS, HEADS)

    def by_columns(x):
        parts = lax.all_to_all(x, "narrow", split_axis=1, concat_axis=0, tiled=True)
        rows = [parts[n * LEN : (n + 1) * LEN] for n in range(4)]
        return jnp.concatenate([rows[1], rows[2]]), jnp.concatenate([rows[0], rows[3]])

    enc_cols, dec_cols = by_columns(pick(enc_out, dec_out))
    enc_grad_cols, dec_grad_cols = by_columns(din.astype(bf16))
    return (
        enc_cols,
        dec_cols,
        enc_grad_cols,
        dec_grad_cols,
        small[0],
        g_e[0],
        g_e[1],
        g_e[2],
        g_e[3],
        tables[0],
        small[1],
        gi_e,
        go_e,
        small[2],
        g_s[0],
        g_s[1],
        g_s[2],
        g_s[3],
        tables[1],
        small[3],
        g_c[0],
        g_c[1],
        g_c[2],
        g_c[3],
        small[4],
        gi_d,
        go_d,
    )


def solution(mesh):
    rows, copied = P("wide", None), P()
    block = P("wide", "narrow")
    gains = (copied,)
    attention = (rows,) * 4
    placed = (
        (rows,) * 4
        + gains
        + attention
        + (copied,)
        + gains
        + (rows,) * 2
        + gains
        + attention
        + (copied,)
        + gains
        + attention
        + gains
        + (rows,) * 2
    )
    return jax.shard_map(
        on_device,
        mesh=mesh,
        in_specs=placed,
        out_specs=(block,) * 4 + placed[4:],
        check_vma=False,
    )
```

time: 2400 us -> 738 us (0.31)
  waiting for transfers between devices: 864 us -> 174 us
  local copies, waits for them, and re-layouts: 669 us -> 91.7 us
  loops' own time: 261 us -> 0 us
  matrix products: 229 us -> 3.8 us
  Pallas kernels: 0 us -> 151 us
  blocking collectives: 103 us -> 0 us
  starting transfers between devices: 140 us -> 235 us
  other arithmetic: 103 us -> 70.3 us
    ppermute x10 -> x105, waiting for transfers between devices: 733 us -> 174 us  [the longest x22 119 us: between(): return lax.ppermute(x, 'narrow', pairs)]
    another operation x12 -> x0, loops' own time: 261 us -> none  [the longest x5 150 us: backward_tick(): lax.switch(branch_index, backward_branches, grad_in, stored_rows, mid_row...]
    dot_general x46 -> x4, matrix products: 189 us -> 3.8 us  [the longest x1 1.66 us: on_device(): jnp.einsum('hsij,bsij->bh', dtile.astype(bf16), hot, preferred_element_ty...]
    reshape x10 -> x6, local copies, waits for them, and re-layouts: 159 us -> 2.73 us  [the longest x3 1.74 us: gain_of(): return g.astype(f32).reshape(1, D)]
    pallas_call x0 -> x7, Pallas kernels: none -> 151 us  [the longest x2 52.9 us: attn_bwd(): pl.pallas_call(functools.partial(attn_bwd_kernel, has_bias), out_shape=tu...]
    reduce_scatter x1 -> x0, waiting for transfers between devices: 122 us -> none  [on_device(): lax.psum_scatter(grad_acc, 'wide', scatter_dimension=1, tiled=True)]
    psum x1 -> x0, blocking collectives: 103 us -> none  [on_device(): lax.psum((gain_sums, table_sums), ('wide', 'narrow'))]
    cond x42 -> x0, local copies, waits for them, and re-layouts: 100 us -> none
  transfers between devices with their start and end apart: 14 -> 107, of which waited for: 12 -> 27; matrix products, arithmetic and copies ran while one was open for 14% -> 20% of each run, Pallas kernels for 0% -> 15%
where the time goes in v1:
time: 738 us; the launch traced here: 728 us
  starting transfers between devices  235 us (32%)
  waiting for transfers between devices  174 us (24%)
  Pallas kernels  151 us (20%)
  local copies, waits for them, and re-layouts  91.7 us (12%)
  other arithmetic  70.3 us (10%)
    ppermute x83, starting transfers between devices, across(): return lax.ppermute(x, ('wide', 'narrow'), pairs)  135 us
    ppermute x22, waiting for transfers between devices, between(): return lax.ppermute(x, 'narrow', pairs)  119 us
    ppermute x22, starting transfers between devices, between(): return lax.ppermute(x, 'narrow', pairs)  89.2 us
    ppermute x83, waiting for transfers between devices, across(): return lax.ppermute(x, ('wide', 'narrow'), pairs)  55.7 us
    pallas_call x2, Pallas kernels, attn_bwd(): pl.pallas_call(functools.partial(attn_bwd_kernel, has_bias), out_shape=tu...  52.9 us
    pallas_call x2, Pallas kernels, ffn_both(): pl.pallas_call(ffn_both_kernel, grid=(FF // CHUNK,), out_shape=(rows, row...  45.1 us
    pallas_call x2, Pallas kernels, attn_fwd(): pl.pallas_call(functools.partial(attn_fwd_kernel, has_bias), out_shape=(j...  42.1 us
    dynamic_update_slice x28, local copies, waits for them, and re-layouts, gathered(): full = lax.dynamic_update_slice(full, piece[:, None], (0, me ^ flip, 0, 0))  33.9 us
  transfers between devices with their start and end apart: 107, of which 27 were waited for; matrix products, arithmetic and copies ran while one was open for 20% of the time, Pallas kernels for 15%

profile of v1, /device:TPU:0, one launch (start us, length us, event | category | flops | bytes accessed | tf_op | source)
XLA Modules:
  0.0 728.5 jit_solution(17407833174190246323)
XLA Ops:
  53.2 4.6 collective-permute-done.16
  64.2 5.8 collective-permute-done.25
  84.0 5.0 collective-permute-done.11
  106.0 5.0 collective-permute-done.19
  116.6 4.9 collective-permute-start.21
  141.3 21.2 %self_fwd.1 = (f32[512,768]{1,0:T(8,128)}, bf16[512,768]{1,0:T(8,128)(2,1)}, bf16[512,768]{1,0:T(8,128)(2,1)}, bf16[512,768]{1,0:T(8,128)(2,1)}, bf16[512,768]{1...) custom-call(bf16[512,768]{1,0:T(8,128)(2,1)} %dynamic-slice_select_fusion.refs_0_.refs_1_, f32[1,768]{1,0:T(1,128)} %select_n.269.refs_1_.refs_2_, ...), custom_call_target="tpu_custom_call" | custom-call | tf_op jit(solution)/shard_map/self_fwd/pallas_call | solution.py:160
  164.9 10.4 %ffn_fwd.1 = bf16[512,768]{1,0:T(8,128)(2,1)} custom-call(bf16[512,768]{1,0:T(8,128)(2,1)} %convert_element_type.711.x, f32[1,768]{1,0:T(1,128)} %reshape.364.gain, bf16[768,3072]{1,0:T(8,128)(2,1)} %bitcast.33.wi, bf16[3072,768]{1,0:T(8,128)(2,1)} %bitcast.43.wo), custom_call_target="tpu_custom_call" | custom-call | tf_op jit(solution)/shard_map/ffn_fwd/pallas_call | solution.py:318
  184.5 12.7 %collective-permute-done.24.refs_2_.refs_3_ = bf16[512,768]{1,0:T(8,128)(2,1)S(1)} collective-permute-done((bf16[512,768]{1,0:T(8,128)(2,1)}, bf16[512,768]{1,0:T(8,128)(2,1)S(1)}, u32[]{:S(2)}, u32[]{:S(2)}) %collective-permute-start.24) | collective-permute-done | bytes 786464 | tf_op jit(solution)/shard_map/ppermute | solution.py:405
  198.1 20.9 %cross_fwd.1 = (f32[512,768]{1,0:T(8,128)}, bf16[512,768]{1,0:T(8,128)(2,1)}, bf16[512,768]{1,0:T(8,128)(2,1)}, bf16[512,768]{1,0:T(8,128)(2,1)}, bf16[512,768]{...) custom-call(f32[512,768]{1,0:T(8,128)} %get-tuple-element.57.refs_0_.refs_1_, f32[1,768]{1,0:T(1,128)} %reshape.366.refs_1_.refs_2_, ...), custom_call_target="tpu_custom_call" | custom-call | tf_op jit(solution)/shard_map/cross_fwd/pallas_call | solution.py:160
  221.4 22.4 %ffn_both.2 = (bf16[512,768]{1,0:T(8,128)(2,1)}, bf16[512,768]{1,0:T(8,128)(2,1)}, f32[1,768]{1,0:T(1,128)}, bf16[768,3072]{1,0:T(8,128)(2,1)}, bf16[3072,768]{1,0:T(8,128)(2,1)}) custom-call(bf16[512,768]{1,0:T(8,128)(2,1)} %convert_element_type.712.x, f32[1,768]{1,0:T(1,128)} %reshape.368.gain, bf16[512,768]{1,0:T(8,128)(2,1)} %constant_dynamic-slice_fusion.g, ...), custom_call_target="tpu_custom_call" | custom-call | tf_op jit(solution)/shard_map/ffn_both/pallas_call | solution.py:370
  259.6 26.4 %cross_bwd.1 = (f32[512,768]{1,0:T(8,128)}, bf16[4,768,768]{2,1,0:T(8,128)(2,1)}, f32[1,768]{1,0:T(1,128)}, bf16[512,768]{1,0:T(8,128)(2,1)}) custom-call(bf16[512,768]{1,0:T(8,128)(2,1)} %get-tuple-element.60.refs_0_, f32[512,768]{1,0:T(8,128)} %get-tuple-element.57.refs_0_.refs_1_, f32[1,768]{1,0:T(1,128)} %reshape.366.refs_1_.refs_2_, ...), custom_call_target="tpu_custom_call" | custom-call | tf_op jit(solution)/shard_map/cross_bwd/pallas_call | solution.py:275
  293.5 4.8 all-to-all-start
  298.2 4.8 collective-permute-start.33
  333.7 22.7 %ffn_both.3 = (bf16[512,768]{1,0:T(8,128)(2,1)}, bf16[512,768]{1,0:T(8,128)(2,1)}, f32[1,768]{1,0:T(1,128)}, bf16[768,3072]{1,0:T(8,128)(2,1)}, bf16[3072,768]{1,0:T(8,128)(2,1)}) custom-call(bf16[512,768]{1,0:T(8,128)(2,1)} %convert_element_type.711.x, f32[1,768]{1,0:T(1,128)} %reshape.364.gain, bf16[512,768]{1,0:T(8,128)(2,1)} %collective-permute-done.33.g, ...), custom_call_target="tpu_custom_call" | custom-call | tf_op jit(solution)/shard_map/ffn_both/pallas_call | solution.py:370
  359.3 26.5 %self_bwd.1 = (f32[512,768]{1,0:T(8,128)}, bf16[4,768,768]{2,1,0:T(8,128)(2,1)}, f32[1,768]{1,0:T(1,128)}, f32[12,3,128,128]{3,2,1,0:T(8,128)}, f32[12,2,128]{2,1,0:T(2,128)}) custom-call(f32[512,768]{1,0:T(8,128)} %convert_select_fusion.refs_0_, bf16[512,768]{1,0:T(8,128)(2,1)} %dynamic-slice_select_fusion.refs_0_.refs_1_, ...), custom_call_target="tpu_custom_call" | custom-call | tf_op jit(solution)/shard_map/self_bwd/pallas_call | solution.py:275
  402.8 4.1 collective-permute-start.37
  439.9 5.7 all-to-all-start.1
  498.7 5.1 collective-permute-done.76
  511.3 4.0 collective-permute-done.42
  518.6 4.6 collective-permute-start.65
  533.5 16.6 %collective-permute-start.102 = (bf16[384,768]{1,0:T(8,128)(2,1)}, bf16[384,768]{1,0:T(8,128)(2,1)S(1)}, u32[]{:S(2)}, u32[]{:S(2)}) collective-permute-start(bf16[384,768]{1,0:T(8,128)(2,1)} %fusion.34), channel_id=1, source_target_pairs={{0,1},{3,2},{4,5},{7,6},{8,9},{11,10},{12,13},{15,14},{16,17},{19,... | collective-permute-start | bytes 1769480 | tf_op jit(solution)/shard_map/ppermute | solution.py:405
  550.1 5.9 collective-permute-start.91
  556.0 3.8 collective-permute-start.80
  565.8 13.5 %collective-permute-start.103 = (bf16[384,768]{1,0:T(8,128)(2,1)S(1)}, bf16[384,768]{1,0:T(8,128)(2,1)S(1)}, u32[]{:S(2)}, u32[]{:S(2)}) collective-permute-start(bf16[384,768]{1,0:T(8,128)(2,1)S(1)} %collective-permute-done.102), channel_id=1, source_target_pairs={{1,2},{2,1},{5,6},{6,5},{9,10},{10,9},{13,14},{14,13},{17,18},{18,... | collective-permute-start | bytes 1769480 | tf_op jit(solution)/shard_map/ppermute | solution.py:405
  580.0 6.7 collective-permute-done.80
  586.7 5.9 collective-permute-start.81
  592.6 4.4 collective-permute-start.69
  599.4 13.2 %collective-permute-start.67 = (bf16[384,768]{1,0:T(8,128)(2,1)S(1)}, bf16[384,768]{1,0:T(8,128)(2,1)S(1)}, u32[]{:S(2)}, u32[]{:S(2)}) collective-permute-start(bf16[384,768]{1,0:T(8,128)(2,1)S(1)} %fusion.32), channel_id=1, source_target_pairs={{1,2},{2,1},{5,6},{6,5},{9,10},{10,9},{13,14},{14,13},{17,18},{18,... | collective-permute-start | bytes 1769480 | tf_op jit(solution)/shard_map/ppermute | solution.py:405
  620.8 42.6 %collective-permute-done.93 = bf16[96,3072]{1,0:T(8,128)(2,1)S(1)} collective-permute-done((bf16[96,3072]{1,0:T(8,128)(2,1)S(1)}, bf16[96,3072]{1,0:T(8,128)(2,1)S(1)}, u32[]{:S(2)}, u32[]{:S(2)}) %collective-permute-start.93) | collective-permute-done | bytes 589856 | tf_op jit(solution)/shard_map/ppermute | solution.py:405
  669.0 32.3 %collective-permute-done.48 = bf16[4,96,768]{2,1,0:T(8,128)(2,1)S(1)} collective-permute-done((bf16[4,96,768]{2,1,0:T(8,128)(2,1)S(1)}, bf16[4,96,768]{2,1,0:T(8,128)(2,1)S(1)}, u32[]{:S(2)}, u32[]{:S(2)}) %collective-permute-start.48) | collective-permute-done | bytes 589856 | tf_op jit(solution)/shard_map/ppermute | solution.py:405
  703.5 10.4 %collective-permute-done.58 = bf16[96,3072]{1,0:T(8,128)(2,1)S(1)} collective-permute-done((bf16[96,3072]{1,0:T(8,128)(2,1)S(1)}, bf16[96,3072]{1,0:T(8,128)(2,1)S(1)}, u32[]{:S(2)}, u32[]{:S(2)}) %collective-permute-start.58) | collective-permute-done | bytes 589856 | tf_op jit(solution)/shard_map/ppermute | solution.py:405
  715.0 10.0 %collective-permute-done.71 = bf16[4,96,768]{2,1,0:T(8,128)(2,1)S(1)} collective-permute-done((bf16[4,96,768]{2,1,0:T(8,128)(2,1)S(1)}, bf16[4,96,768]{2,1,0:T(8,128)(2,1)S(1)}, u32[]{:S(2)}, u32[]{:S(2)}) %collective-permute-start.71) | collective-permute-done | bytes 589856 | tf_op jit(solution)/shard_map/ppermute | solution.py:405
  (516 shorter events, 338.5 us)
Async XLA Ops:
  4.7 40.6 %collective-permute-start = (bf16[4,96,768]{2,1,0:T(8,128)(2,1)}, bf16[4,96,768]{2,1,0:T(8,128)(2,1)}, u32[]{:S(2)}, u32[]{:S(2)}) collective-permute-start(bf16[4,96,768]{2,1,0:T(8,128)(2,1)} %pad_maximum_fusion), channel_id=1, source_target_pairs={{0,8},{1,9},{2,10},{3,11},{4,12},{5,13},{6,14},{7,15},{8,0},{9,1},... | collective-permute-start | bytes 1769480 | tf_op jit(solution)/shard_map/ppermute | solution.py:401
  7.7 41.2 %collective-permute-start.1 = (bf16[4,96,768]{2,1,0:T(8,128)(2,1)}, bf16[4,96,768]{2,1,0:T(8,128)(2,1)}, u32[]{:S(2)}, u32[]{:S(2)}) collective-permute-start(bf16[4,96,768]{2,1,0:T(8,128)(2,1)} %pad_maximum_fusion), channel_id=1, source_target_pairs={{0,16},{1,17},{2,18},{3,19},{4,20},{5,21},{6,22},{7,23},{8,24},{9,... | collective-permute-start | bytes 1769480 | tf_op jit(solution)/shard_map/ppermute | solution.py:401
  9.2 107.4 %collective-permute-start.4 = (bf16[4,96,768]{2,1,0:T(8,128)(2,1)}, bf16[4,96,768]{2,1,0:T(8,128)(2,1)}, u32[]{:S(2)}, u32[]{:S(2)}) collective-permute-start(bf16[4,96,768]{2,1,0:T(8,128)(2,1)} %pad_maximum_fusion), channel_id=1, source_target_pairs={{0,4},{1,5},{2,6},{3,7},{4,0},{5,1},{6,2},{7,3},{8,12},{9,13},{10,... | collective-permute-start | bytes 1769480 | tf_op jit(solution)/shard_map/ppermute | solution.py:401
  39.5 52.1 %collective-permute-start.12 = (bf16[1,96,3072]{2,1,0:T(8,128)(2,1)}, bf16[1,96,3072]{2,1,0:T(8,128)(2,1)S(1)}, u32[]{:S(2)}, u32[]{:S(2)}) collective-permute-start(bf16[1,96,3072]{2,1,0:T(8,128)(2,1)} %fusion.35), channel_id=1, source_target_pairs={{0,4},{1,5},{2,6},{3,7},{4,0},{5,1},{6,2},{7,3},{8,12},{9,13},{10,... | collective-permute-start | bytes 1769480 | tf_op jit(solution)/shard_map/ppermute | solution.py:401
  63.3 60.1 %collective-permute-start.20 = (bf16[1,384,768]{2,1,0:T(8,128)(2,1)S(1)}, bf16[1,384,768]{2,1,0:T(8,128)(2,1)S(1)}, u32[]{:S(2)}, u32[]{:S(2)}) collective-permute-start(bf16[1,384,768]{2,1,0:T(8,128)(2,1)S(1)} %copy-done.41), channel_id=1, source_target_pairs={{0,4},{1,5},{2,6},{3,7},{4,0},{5,1},{6,2},{7,3},{8,12},{9,13},{10,... | collective-permute-start | bytes 1769480 | tf_op jit(solution)/shard_map/ppermute | solution.py:401
  97.9 78.8 %collective-permute-start.29 = (bf16[4,96,768]{2,1,0:T(8,128)(2,1)S(1)}, bf16[4,96,768]{2,1,0:T(8,128)(2,1)}, u32[]{:S(2)}, u32[]{:S(2)}) collective-permute-start(bf16[4,96,768]{2,1,0:T(8,128)(2,1)S(1)} %pad_maximum_fusion.1), channel_id=1, source_target_pairs={{0,4},{3,7},{4,0},{7,3},{8,12},{11,15},{12,8},{15,11},{16,20},{19,... | collective-permute-start | bytes 1769480 | tf_op jit(solution)/shard_map/ppermute | solution.py:401
  126.9 51.8 %collective-permute-start.30 = (bf16[4,96,768]{2,1,0:T(8,128)(2,1)S(1)}, bf16[4,96,768]{2,1,0:T(8,128)(2,1)}, u32[]{:S(2)}, u32[]{:S(2)}) collective-permute-start(bf16[4,96,768]{2,1,0:T(8,128)(2,1)S(1)} %collective-permute-done.25), channel_id=1, source_target_pairs={{0,4},{3,7},{4,0},{7,3},{8,12},{11,15},{12,8},{15,11},{16,20},{19,... | collective-permute-start | bytes 1769480 | tf_op jit(solution)/shard_map/ppermute | solution.py:401
  129.8 50.9 %collective-permute-start.31 = (bf16[4,96,768]{2,1,0:T(8,128)(2,1)S(1)}, bf16[4,96,768]{2,1,0:T(8,128)(2,1)}, u32[]{:S(2)}, u32[]{:S(2)}) collective-permute-start(bf16[4,96,768]{2,1,0:T(8,128)(2,1)S(1)} %collective-permute-done.26), channel_id=1, source_target_pairs={{0,4},{3,7},{4,0},{7,3},{8,12},{11,15},{12,8},{15,11},{16,20},{19,... | collective-permute-start | bytes 1769480 | tf_op jit(solution)/shard_map/ppermute | solution.py:401
  137.3 45.4 %collective-permute-start.32 = (bf16[4,96,768]{2,1,0:T(8,128)(2,1)S(1)}, bf16[4,96,768]{2,1,0:T(8,128)(2,1)}, u32[]{:S(2)}, u32[]{:S(2)}) collective-permute-start(bf16[4,96,768]{2,1,0:T(8,128)(2,1)S(1)} %constant_dynamic-update-slice_fusion.6), channel_id=1, source_target_pairs={{0,4},{3,7},{4,0},{7,3},{8,12},{11,15},{12,8},{15,11},{16,20},{19,... | collective-permute-start | bytes 1769480 | tf_op jit(solution)/shard_map/ppermute | solution.py:401
  247.0 39.8 %collective-permute-start.95 = (bf16[1,384,768]{2,1,0:T(8,128)(2,1)}, bf16[1,384,768]{2,1,0:T(8,128)(2,1)S(1)}, u32[]{:S(2)}, u32[]{:S(2)}) collective-permute-start(bf16[1,384,768]{2,1,0:T(8,128)(2,1)} %get-tuple-element.151), channel_id=1, source_target_pairs={{0,4},{3,7},{4,0},{7,3},{8,12},{11,15},{12,8},{15,11},{16,20},{19,... | collective-permute-start | bytes 1769480 | tf_op jit(solution)/shard_map/ppermute | solution.py:401
  248.9 49.3 %collective-permute-start.96 = (bf16[1,384,768]{2,1,0:T(8,128)(2,1)}, bf16[1,384,768]{2,1,0:T(8,128)(2,1)}, u32[]{:S(2)}, u32[]{:S(2)}) collective-permute-start(bf16[1,384,768]{2,1,0:T(8,128)(2,1)} %get-tuple-element.150), channel_id=1, source_target_pairs={{0,4},{3,7},{4,0},{7,3},{8,12},{11,15},{12,8},{15,11},{16,20},{19,... | collective-permute-start | bytes 1769480 | tf_op jit(solution)/shard_map/ppermute | solution.py:401
  251.4 51.7 %collective-permute-start.99 = (bf16[1,384,768]{2,1,0:T(8,128)(2,1)}, bf16[1,384,768]{2,1,0:T(8,128)(2,1)}, u32[]{:S(2)}, u32[]{:S(2)}) collective-permute-start(bf16[1,384,768]{2,1,0:T(8,128)(2,1)} %get-tuple-element.149), channel_id=1, source_target_pairs={{0,4},{3,7},{4,0},{7,3},{8,12},{11,15},{12,8},{15,11},{16,20},{19,... | collective-permute-start | bytes 1769480 | tf_op jit(solution)/shard_map/ppermute | solution.py:401
  254.7 55.0 %collective-permute-start.84 = (bf16[1,96,3072]{2,1,0:T(8,128)(2,1)}, bf16[1,96,3072]{2,1,0:T(8,128)(2,1)S(1)}, u32[]{:S(2)}, u32[]{:S(2)}) collective-permute-start(bf16[1,96,3072]{2,1,0:T(8,128)(2,1)} %get-tuple-element.158), channel_id=1, source_target_pairs={{0,4},{3,7},{4,0},{7,3},{8,12},{11,15},{12,8},{15,11},{16,20},{19,... | collective-permute-start | bytes 1769480 | tf_op jit(solution)/shard_map/ppermute | solution.py:401
  257.1 55.0 %collective-permute-start.85 = (bf16[1,96,3072]{2,1,0:T(8,128)(2,1)}, bf16[1,96,3072]{2,1,0:T(8,128)(2,1)}, u32[]{:S(2)}, u32[]{:S(2)}) collective-permute-start(bf16[1,96,3072]{2,1,0:T(8,128)(2,1)} %get-tuple-element.157), channel_id=1, source_target_pairs={{0,4},{3,7},{4,0},{7,3},{8,12},{11,15},{12,8},{15,11},{16,20},{19,... | collective-permute-start | bytes 1769480 | tf_op jit(solution)/shard_map/ppermute | solution.py:401
  293.5 146.4 %all-to-all-start = ((bf16[512,4,192]{0,2,1:T(8,128)(2,1)}), bf16[512,4,192]{0,2,1:T(8,128)(2,1)S(1)}, u32[]{:S(2)}, u32[]{:S(2)}) async-start(bf16[512,4,192]{0,2,1:T(8,128)(2,1)} %bitcast.65), calls=%async_computation | async-start | bytes 1572864 | tf_op jit(solution)/shard_map/all_to_all | solution.py:601
  298.2 35.5 %collective-permute-start.33 = (bf16[512,768]{1,0:T(8,128)(2,1)}, bf16[512,768]{1,0:T(8,128)(2,1)}, u32[]{:S(2)}, u32[]{:S(2)}) collective-permute-start(bf16[512,768]{1,0:T(8,128)(2,1)} %get-tuple-element.66), channel_id=1, source_target_pairs={{0,1},{3,2},{4,5},{7,6},{8,9},{11,10},{12,13},{15,14},{16,17},{19,... | collective-permute-start | bytes 2359304 | tf_op jit(solution)/shard_map/ppermute | solution.py:405
  314.1 106.9 %collective-permute-start.97 = (bf16[1,192,768]{2,1,0:T(8,128)(2,1)}, bf16[1,192,768]{2,1,0:T(8,128)(2,1)}, u32[]{:S(2)}, u32[]{:S(2)}) collective-permute-start(bf16[1,192,768]{2,1,0:T(8,128)(2,1)} %get-tuple-element.210), channel_id=1, source_target_pairs={{0,16},{3,19},{4,20},{7,23},{8,24},{11,27},{12,28},{15,31},{16,0},... | collective-permute-start | bytes 884744 | tf_op jit(solution)/shard_map/ppermute | solution.py:401
  322.3 101.1 %collective-permute-start.100 = (bf16[1,192,768]{2,1,0:T(8,128)(2,1)}, bf16[1,192,768]{2,1,0:T(8,128)(2,1)}, u32[]{:S(2)}, u32[]{:S(2)}) collective-permute-start(bf16[1,192,768]{2,1,0:T(8,128)(2,1)} %get-tuple-element.211), channel_id=1, source_target_pairs={{0,8},{3,11},{4,12},{7,15},{8,0},{11,3},{12,4},{15,7},{16,24},{19,... | collective-permute-start | bytes 884744 | tf_op jit(solution)/shard_map/ppermute | solution.py:401
  325.8 88.6 %collective-permute-start.86 = (bf16[1,48,3072]{2,1,0:T(8,128)(2,1)}, bf16[1,48,3072]{2,1,0:T(8,128)(2,1)}, u32[]{:S(2)}, u32[]{:S(2)}) collective-permute-start(bf16[1,48,3072]{2,1,0:T(8,128)(2,1)} %get-tuple-element.212), channel_id=1, source_target_pairs={{0,16},{3,19},{4,20},{7,23},{8,24},{11,27},{12,28},{15,31},{16,0},... | collective-permute-start | bytes 884744 | tf_op jit(solution)/shard_map/ppermute | solution.py:401
  328.2 90.7 %collective-permute-start.89 = (bf16[1,48,3072]{2,1,0:T(8,128)(2,1)}, bf16[1,48,3072]{2,1,0:T(8,128)(2,1)}, u32[]{:S(2)}, u32[]{:S(2)}) collective-permute-start(bf16[1,48,3072]{2,1,0:T(8,128)(2,1)} %get-tuple-element.213), channel_id=1, source_target_pairs={{0,8},{3,11},{4,12},{7,15},{8,0},{11,3},{12,4},{15,7},{16,24},{19,... | collective-permute-start | bytes 884744 | tf_op jit(solution)/shard_map/ppermute | solution.py:401
  439.9 93.5 %all-to-all-start.1 = ((bf16[512,4,192]{0,2,1:T(8,128)(2,1)}), bf16[512,4,192]{0,2,1:T(8,128)(2,1)S(1)}, u32[]{:S(2)}, u32[]{:S(2)}) async-start(bf16[512,4,192]{0,2,1:T(8,128)(2,1)} %bitcast.71), calls=%async_computation.1 | async-start | bytes 1572864 | tf_op jit(solution)/shard_map/all_to_all | solution.py:601
  458.9 39.1 %collective-permute-start.72 = (bf16[4,96,768]{2,1,0:T(8,128)(2,1)S(1)}, bf16[4,96,768]{2,1,0:T(8,128)(2,1)S(1)}, u32[]{:S(2)}, u32[]{:S(2)}) collective-permute-start(bf16[4,96,768]{2,1,0:T(8,128)(2,1)S(1)} %copy-done.34), channel_id=1, source_target_pairs={{0,4},{3,7},{4,0},{7,3},{8,12},{11,15},{12,8},{15,11},{16,20},{19,... | collective-permute-start | bytes 1769480 | tf_op jit(solution)/shard_map/ppermute | solution.py:401
  491.5 38.8 %collective-permute-start.39 = (bf16[4,96,768]{2,1,0:T(8,128)(2,1)S(1)}, bf16[4,96,768]{2,1,0:T(8,128)(2,1)S(1)}, u32[]{:S(2)}, u32[]{:S(2)}) collective-permute-start(bf16[4,96,768]{2,1,0:T(8,128)(2,1)S(1)} %copy-done.36), channel_id=1, source_target_pairs={{0,4},{1,5},{2,6},{3,7},{4,0},{5,1},{6,2},{7,3},{8,12},{9,13},{10,... | collective-permute-start | bytes 1769480 | tf_op jit(solution)/shard_map/ppermute | solution.py:401
  560.6 36.5 %collective-permute-start.56 = (bf16[1,96,3072]{2,1,0:T(8,128)(2,1)S(1)}, bf16[1,96,3072]{2,1,0:T(8,128)(2,1)S(1)}, u32[]{:S(2)}, u32[]{:S(2)}) collective-permute-start(bf16[1,96,3072]{2,1,0:T(8,128)(2,1)S(1)} %pad_maximum_fusion.5), channel_id=1, source_target_pairs={{1,17},{2,18},{5,21},{6,22},{9,25},{10,26},{13,29},{14,30},{17,1},... | collective-permute-start | bytes 1769480 | tf_op jit(solution)/shard_map/ppermute | solution.py:401
  565.8 47.0 %collective-permute-start.103 = (bf16[384,768]{1,0:T(8,128)(2,1)S(1)}, bf16[384,768]{1,0:T(8,128)(2,1)S(1)}, u32[]{:S(2)}, u32[]{:S(2)}) collective-permute-start(bf16[384,768]{1,0:T(8,128)(2,1)S(1)} %collective-permute-done.102), channel_id=1, source_target_pairs={{1,2},{2,1},{5,6},{6,5},{9,10},{10,9},{13,14},{14,13},{17,18},{18,... | collective-permute-start | bytes 1769480 | tf_op jit(solution)/shard_map/ppermute | solution.py:405
  613.6 51.5 %collective-permute-start.104 = (bf16[384,768]{1,0:T(8,128)(2,1)S(1)}, bf16[384,768]{1,0:T(8,128)(2,1)S(1)}, u32[]{:S(2)}, u32[]{:S(2)}) collective-permute-start(bf16[384,768]{1,0:T(8,128)(2,1)S(1)} %add_convert_fusion), channel_id=1, source_target_pairs={{1,0},{2,3},{5,4},{6,7},{9,8},{10,11},{13,12},{14,15},{17,16},{18,... | collective-permute-start | bytes 1769480 | tf_op jit(solution)/shard_map/ppermute | solution.py:405
  615.1 48.3 %collective-permute-start.93 = (bf16[96,3072]{1,0:T(8,128)(2,1)S(1)}, bf16[96,3072]{1,0:T(8,128)(2,1)S(1)}, u32[]{:S(2)}, u32[]{:S(2)}) collective-permute-start(bf16[96,3072]{1,0:T(8,128)(2,1)S(1)} %add_convert_fusion.2), channel_id=1, source_target_pairs={{1,0},{2,3},{5,4},{6,7},{9,8},{10,11},{13,12},{14,15},{17,16},{18,... | collective-permute-start | bytes 1769480 | tf_op jit(solution)/shard_map/ppermute | solution.py:405
  616.6 98.5 %collective-permute-start.82 = (bf16[4,96,768]{2,1,0:T(8,128)(2,1)S(1)}, bf16[4,96,768]{2,1,0:T(8,128)(2,1)S(1)}, u32[]{:S(2)}, u32[]{:S(2)}) collective-permute-start(bf16[4,96,768]{2,1,0:T(8,128)(2,1)S(1)} %add_convert_fusion.4), channel_id=1, source_target_pairs={{1,0},{2,3},{5,4},{6,7},{9,8},{10,11},{13,12},{14,15},{17,16},{18,... | collective-permute-start | bytes 1769480 | tf_op jit(solution)/shard_map/ppermute | solution.py:405
  618.0 84.4 %collective-permute-start.68 = (bf16[384,768]{1,0:T(8,128)(2,1)S(1)}, bf16[384,768]{1,0:T(8,128)(2,1)S(1)}, u32[]{:S(2)}, u32[]{:S(2)}) collective-permute-start(bf16[384,768]{1,0:T(8,128)(2,1)S(1)} %add_convert_fusion.7), channel_id=1, source_target_pairs={{1,0},{2,3},{5,4},{6,7},{9,8},{10,11},{13,12},{14,15},{17,16},{18,... | collective-permute-start | bytes 1769480 | tf_op jit(solution)/shard_map/ppermute | solution.py:405
  619.5 81.8 %collective-permute-start.48 = (bf16[4,96,768]{2,1,0:T(8,128)(2,1)S(1)}, bf16[4,96,768]{2,1,0:T(8,128)(2,1)S(1)}, u32[]{:S(2)}, u32[]{:S(2)}) collective-permute-start(bf16[4,96,768]{2,1,0:T(8,128)(2,1)S(1)} %add_convert_fusion.11), channel_id=1, source_target_pairs={{1,0},{2,3},{5,4},{6,7},{9,8},{10,11},{13,12},{14,15},{17,16},{18,... | collective-permute-start | bytes 1769480 | tf_op jit(solution)/shard_map/ppermute | solution.py:405
  665.2 48.8 %collective-permute-start.58 = (bf16[96,3072]{1,0:T(8,128)(2,1)S(1)}, bf16[96,3072]{1,0:T(8,128)(2,1)S(1)}, u32[]{:S(2)}, u32[]{:S(2)}) collective-permute-start(bf16[96,3072]{1,0:T(8,128)(2,1)S(1)} %add_convert_fusion.9), channel_id=1, source_target_pairs={{1,0},{2,3},{5,4},{6,7},{9,8},{10,11},{13,12},{14,15},{17,16},{18,... | collective-permute-start | bytes 1769480 | tf_op jit(solution)/shard_map/ppermute | solution.py:405
  667.7 57.3 %collective-permute-start.71 = (bf16[4,96,768]{2,1,0:T(8,128)(2,1)S(1)}, bf16[4,96,768]{2,1,0:T(8,128)(2,1)S(1)}, u32[]{:S(2)}, u32[]{:S(2)}) collective-permute-start(bf16[4,96,768]{2,1,0:T(8,128)(2,1)S(1)} %add_convert_fusion.6), channel_id=1, source_target_pairs={{1,0},{2,3},{5,4},{6,7},{9,8},{10,11},{13,12},{14,15},{17,16},{18,... | collective-permute-start | bytes 1769480 | tf_op jit(solution)/shard_map/ppermute | solution.py:405
  (144 other events, 1706.0 us)

commit v2 on v1

v2 whole, which is shorter than its diff:
```python
import functools

import jax
import jax.numpy as jnp
import numpy as np
from jax import lax
from jax.experimental import pallas as pl
from jax.experimental.pallas import tpu as pltpu
from jax.sharding import PartitionSpec as P

D = 768
HEADS = 12
HEAD = 64
PAIRS = HEADS // 2
FF = 3072
BUCKETS = 32
MAXDIST = 128
LEN = 512
TILE = 128
BLOCKS = LEN // TILE
ROWS8 = D // 8

EPSILON = 1e-06
MASKED = -1000000000.0
VMEM_LIMIT = 60 * 1024 * 1024
f32 = jnp.float32
bf16 = jnp.bfloat16


def bucket_of(reverse, both_ways):
    result = np.zeros(reverse.shape, np.int64)
    if both_ways:
        half_count = BUCKETS // 2
        result = result + (reverse < 0) * half_count
        reverse = np.abs(reverse)
    else:
        half_count = BUCKETS
        reverse = np.maximum(reverse, 0)
    exact_count = half_count // 2
    scaled = (
        np.log(np.maximum(reverse, 1) / exact_count)
        / np.log(MAXDIST / exact_count)
        * (half_count - exact_count)
    )
    far_bucket = np.minimum(
        exact_count + np.floor(np.maximum(scaled, 0.0)).astype(np.int64), half_count - 1
    )
    return result + np.where(reverse < exact_count, reverse, far_bucket)


def tile_ids(both_ways):
    i = np.arange(TILE)[:, None]
    j = np.arange(TILE)[None, :]
    tiles = []
    for step in (0, 1, -1):
        n = i - j + step * TILE
        ids = bucket_of(n, both_ways)
        tiles.append(ids if both_ways else np.where(n < 0, BUCKETS, ids))
    far = bucket_of(np.array([2 * TILE - TILE + 1, -(2 * TILE - TILE + 1)]), both_ways)
    if not both_ways:
        far[1] = BUCKETS
    return np.stack(tiles).astype(np.int32), far.astype(np.int32)


def dot(a, b):
    return jnp.dot(a, b, preferred_element_type=f32)


def dot_nt(a, b):
    return lax.dot_general(a, b, (((1,), (1,)), ((), ())), preferred_element_type=f32)


def rms(v, gain):
    return v * lax.rsqrt(jnp.mean(v * v, axis=-1, keepdims=True) + EPSILON) * gain


def rms_back(v, gain, dy):
    r = lax.rsqrt(jnp.mean(v * v, axis=-1, keepdims=True) + EPSILON)
    dgain = jnp.sum(dy * v * r, axis=0, keepdims=True)
    gdy = dy * gain
    dv = r * gdy - v * (r * r * r * jnp.mean(gdy * v, axis=-1, keepdims=True))
    return dv, dgain


def half_lanes(value, which):
    lane = lax.broadcasted_iota(jnp.int32, value.shape, 1)
    return jnp.where((lane // HEAD) == which, value, jnp.zeros_like(value))


def tile_of(step):
    return {0: 0, 1: 1, -1: 2}.get(step)


def part_plan(count, k):
    if count == 1:
        return [(None, 0, k)]
    half = k // 2
    plan = [(0, 0, k), (2, 0, k), (4, 0, k), (6, 0, half), (6, half, half)]
    return plan + [(flip ^ 1, first, units) for flip, first, units in plan]


def attn_loads(me, parts, w_s, units, sem):
    copies = []
    for part, (flip, first, count) in zip(parts, part_plan(len(parts), 4)):
        for u in units:
            if first <= u < first + count:
                to = w_s.at[u] if flip is None else w_s.at[u, me ^ flip]
                copies.append(pltpu.make_async_copy(part.at[u - first], to, sem))
    return copies


def start_all(copies):
    for copy in copies:
        copy.start()


def wait_all(copies):
    for copy in copies:
        copy.wait()


def matrix(w_s, unit):
    return w_s[unit].reshape(D, D)


def put_blocks(me, value, unit, keep, send):
    value = value.astype(bf16)
    odd = (me % 2) == 1
    for i in range(4):
        even_rows = value[2 * i * ROWS8 : (2 * i + 1) * ROWS8]
        odd_rows = value[(2 * i + 1) * ROWS8 : (2 * i + 2) * ROWS8]
        slot = i ^ (me // 2)
        keep[slot, unit] = jnp.where(odd, odd_rows, even_rows)
        send[slot, unit] = jnp.where(odd, even_rows, odd_rows)


def attn_fwd_kernel(has_bias, nparts, *refs):
    refs = list(refs)
    me_ref, src, gain = refs[:3]
    refs = refs[3:]
    ksrc = None
    if not has_bias:
        ksrc = refs.pop(0)
    segr, segc = refs[:2]
    refs = refs[2:]
    if has_bias:
        bias, far = refs[:2]
        refs = refs[2:]
    parts = refs[:nparts]
    refs = refs[nparts:]
    z, zlow, q_o, k_o, v_o, o_o, p_o, w_s, q_s, k_s, v_s, o_s, p_s, w_sem, out_sem = refs
    me = me_ref[0]

    loads = [attn_loads(me, parts, w_s, (u,), w_sem.at[u]) for u in range(4)]
    for load in loads:
        start_all(load)
    a = rms(src[...].astype(f32), gain[...]).astype(bf16)
    b = a if ksrc is None else ksrc[...]
    outs = []
    for value, weight, out, scr in ((a, 0, q_o, q_s), (b, 1, k_o, k_s), (b, 2, v_o, v_s)):
        wait_all(loads[weight])
        full = dot(value, matrix(w_s, weight)).astype(bf16)
        for p in range(PAIRS):
            scr[p] = full[:, p * TILE : (p + 1) * TILE]
        outs.append(pltpu.make_async_copy(scr, out, out_sem.at[weight]))
        outs[-1].start()

    def prob_copy(p):
        return pltpu.make_async_copy(p_s.at[pl.ds(2 * p, 2)], p_o.at[pl.ds(2 * p, 2)], out_sem.at[4])

    def pair(p, carry):
        qp, kp, vp = q_s[p], k_s[p], v_s[p]
        total = [None] * BLOCKS
        for which in range(2):
            h = 2 * p + which
            kz, vz = half_lanes(kp, which), half_lanes(vp, which)
            for bi in range(BLOCKS):
                rows = slice(bi * TILE, (bi + 1) * TILE)
                s = dot_nt(qp[rows], kz)
                if has_bias:
                    tiles = []
                    for bj in range(BLOCKS):
                        step = bi - bj
                        part = s[:, bj * TILE : (bj + 1) * TILE]
                        if abs(step) < 2:
                            part = part + bias[h, tile_of(step)]
                        else:
                            part = part + far[h, 0 if step > 0 else 1]
                        tiles.append(part)
                    s = jnp.concatenate(tiles, axis=1)
                s = jnp.where(segc[rows] == segr[...], s, MASKED)
                e = jnp.exp(s - jnp.max(s, axis=-1, keepdims=True))
                prob = (e * (1.0 / jnp.sum(e, axis=-1, keepdims=True))).astype(bf16)
                p_s[h, rows, :] = prob
                o = dot(prob, vz)
                total[bi] = o if total[bi] is None else total[bi] + o
        o_s[p] = jnp.concatenate(total, axis=0).astype(bf16)
        prob_copy(p).start()
        return carry

    lax.fori_loop(0, PAIRS, pair, 0)
    outs.append(pltpu.make_async_copy(o_s, o_o, out_sem.at[3]))
    outs[-1].start()
    mixed = jnp.concatenate([o_s[p] for p in range(PAIRS)], axis=1)
    wait_all(loads[3])
    result = src[...].astype(f32) + dot(mixed, matrix(w_s, 3))
    z[...] = result
    zlow[...] = result.astype(bf16)
    wait_all(outs)
    for p in range(PAIRS):
        prob_copy(p).wait()


VM = pl.BlockSpec(memory_space=pltpu.VMEM)
SM = pl.BlockSpec(memory_space=pltpu.SMEM)
HBM = pl.BlockSpec(memory_space=pl.ANY)
HEAD_ROWS = jax.ShapeDtypeStruct((PAIRS, LEN, TILE), bf16)
LOW_ROWS = jax.ShapeDtypeStruct((LEN, D), bf16)
FULL_ROWS = jax.ShapeDtypeStruct((LEN, D), f32)
ONE_ROW = jax.ShapeDtypeStruct((1, D), f32)
PARAMS = pltpu.CompilerParams(vmem_limit_bytes=VMEM_LIMIT)


def attn_fwd(me, src, gain, parts, segr, segc, ksrc=None, bias=None, far=None):
    has_bias = bias is not None
    args = [me, src, gain] + ([] if has_bias else [ksrc]) + [segr, segc]
    specs = [SM] + [VM] * (len(args) - 1)
    if has_bias:
        args += [bias, far]
        specs += [VM, SM]
    args += parts
    specs += [HBM] * len(parts)
    return pl.pallas_call(
        functools.partial(attn_fwd_kernel, has_bias, len(parts)),
        out_shape=(FULL_ROWS, LOW_ROWS)
        + (HEAD_ROWS,) * 4
        + (jax.ShapeDtypeStruct((HEADS, LEN, LEN), bf16),),
        in_specs=specs,
        out_specs=(VM,) * 2 + (HBM,) * 5,
        scratch_shapes=[pltpu.VMEM((4, 8, ROWS8, D), bf16)]
        + [pltpu.VMEM((PAIRS, LEN, TILE), bf16)] * 4
        + [pltpu.VMEM((HEADS, LEN, LEN), bf16)]
        + [pltpu.SemaphoreType.DMA((4,)), pltpu.SemaphoreType.DMA((5,))],
        compiler_params=PARAMS,
        name="self_fwd" if has_bias else "cross_fwd",
    )(*args)


def attn_bwd_kernel(has_bias, nparts, *refs):
    refs = list(refs)
    me_ref, gres, src, gain = refs[:4]
    refs = refs[4:]
    gother = ksrc = None
    if has_bias:
        gother = refs.pop(0)
    else:
        ksrc = refs.pop(0)
    q_i, k_i, v_i, o_i, p_i = refs[:5]
    refs = refs[5:]
    parts = refs[:nparts]
    refs = refs[nparts:]
    din, keep, send, dgain = refs[:4]
    refs = refs[4:]
    if has_bias:
        dtile, dfar = refs[:2]
        refs = refs[2:]
    else:
        dkey = refs.pop(0)
    w_s, p_s, do_s, dq_s, dk_s, dv_s, ds_s, keep_s, send_s, w_sem, p_sem, out_sem = refs
    me = me_ref[0]

    out_load = attn_loads(me, parts, w_s, (3,), w_sem.at[0])
    rest_load = attn_loads(me, parts, w_s, (0, 1, 2), w_sem.at[1])

    def prob_copy(p):
        return pltpu.make_async_copy(p_i.at[pl.ds(2 * p, 2)], p_s.at[pl.ds(2 * p, 2)], p_sem.at[p])

    start_all(out_load)
    for p in range(PAIRS):
        prob_copy(p).start()
    start_all(rest_load)
    base = gres[...].astype(f32)
    if has_bias:
        base = jnp.where(me_ref[1] == 1, gother[...].astype(f32), base)
    g = base.astype(bf16)
    wait_all(out_load)
    do = dot_nt(g, matrix(w_s, 3)).astype(bf16)
    for p in range(PAIRS):
        do_s[p] = do[:, p * TILE : (p + 1) * TILE]

    def pair(p, carry):
        qp, kp, vp, dop = q_i[p], k_i[p], v_i[p], do_s[p]
        q_t, do_t = qp.T, dop.T
        total = [None] * BLOCKS
        prob_copy(p).wait()
        for which in range(2):
            h = 2 * p + which
            kz, vz = half_lanes(kp, which), half_lanes(vp, which)
            diag = {0: None, 1: None, -1: None, 2: None, -2: None}
            for bi in range(BLOCKS):
                rows = slice(bi * TILE, (bi + 1) * TILE)
                dp = dot_nt(dop[rows], vz)
                prob = p_s[h, rows, :].astype(f32)
                t = prob * dp
                ds = t - prob * jnp.sum(t, axis=-1, keepdims=True)
                if has_bias:
                    for bj in range(BLOCKS):
                        step = max(-2, min(2, bi - bj))
                        part = ds[:, bj * TILE : (bj + 1) * TILE]
                        diag[step] = part if diag[step] is None else diag[step] + part
                low = ds.astype(bf16)
                ds_s[which, rows, :] = low
                dq = dot(low, kz)
                total[bi] = dq if total[bi] is None else total[bi] + dq
            if has_bias:
                for step in (0, 1, -1):
                    dtile[h, tile_of(step)] = diag[step].astype(bf16)
                for n, step in ((0, 2), (1, -2)):
                    dfar[h, n : n + 1, :] = jnp.sum(diag[step], axis=0, keepdims=True)
            half = slice(which * HEAD, (which + 1) * HEAD)
            dk_s[p, half, :] = dot(q_t[half], ds_s[which]).astype(bf16)
            dv_s[p, half, :] = dot(do_t[half], p_s[h]).astype(bf16)
        dq_s[p] = jnp.concatenate(total, axis=0).astype(bf16)
        return carry

    lax.fori_loop(0, PAIRS, pair, 0)
    v = src[...].astype(f32)
    a = rms(v, gain[...]).astype(bf16)
    a_t = a.T
    b_t = a_t if ksrc is None else ksrc[...].T
    dq = jnp.concatenate([dq_s[p] for p in range(PAIRS)], axis=1)
    dk_t = dk_s[...].reshape(D, LEN)
    dv_t = dv_s[...].reshape(D, LEN)
    put_blocks(me, dot(a_t, dq), 0, keep_s, send_s)
    put_blocks(me, dot_nt(b_t, dk_t), 1, keep_s, send_s)
    put_blocks(me, dot_nt(b_t, dv_t), 2, keep_s, send_s)
    mixed = jnp.concatenate([o_i[p] for p in range(PAIRS)], axis=1)
    put_blocks(me, dot(mixed.T, g), 3, keep_s, send_s)
    outs = [
        pltpu.make_async_copy(send_s, send, out_sem.at[0]),
        pltpu.make_async_copy(keep_s, keep, out_sem.at[1]),
    ]
    start_all(outs)
    wait_all(rest_load)
    query_side = dot_nt(dq, matrix(w_s, 0))
    key_side = dot_nt(dk_t.T, matrix(w_s, 1)) + dot_nt(dv_t.T, matrix(w_s, 2))
    if has_bias:
        query_side = query_side + key_side
    else:
        dkey[...] = key_side.astype(bf16)
    dv, dg = rms_back(v, gain[...], query_side)
    dgain[...] = dg
    din[...] = (base + dv).astype(din.dtype)
    wait_all(outs)


BLOCKS4 = jax.ShapeDtypeStruct((4, 4, ROWS8, D), bf16)
BLOCKS8 = jax.ShapeDtypeStruct((4, 8, ROWS8, D), bf16)


def attn_bwd(me, gres, src, gain, parts, saved, ksrc=None, gother=None):
    has_bias = ksrc is None
    args = [me, gres, src, gain, gother if has_bias else ksrc, *saved, *parts]
    specs = [SM] + [VM] * 8 + [HBM] + [HBM] * len(parts)
    outs = [LOW_ROWS if has_bias else FULL_ROWS, BLOCKS4, BLOCKS4, ONE_ROW]
    if has_bias:
        outs += [
            jax.ShapeDtypeStruct((HEADS, 3, TILE, TILE), bf16),
            jax.ShapeDtypeStruct((HEADS, 2, TILE), f32),
        ]
    else:
        outs += [LOW_ROWS]
    return pl.pallas_call(
        functools.partial(attn_bwd_kernel, has_bias, len(parts)),
        out_shape=tuple(outs),
        in_specs=specs,
        out_specs=tuple([VM, HBM, HBM] + [VM] * (len(outs) - 3)),
        scratch_shapes=[
            pltpu.VMEM((4, 8, ROWS8, D), bf16),
            pltpu.VMEM((HEADS, LEN, LEN), bf16),
            pltpu.VMEM((PAIRS, LEN, TILE), bf16),
            pltpu.VMEM((PAIRS, LEN, TILE), bf16),
            pltpu.VMEM((PAIRS, TILE, LEN), bf16),
            pltpu.VMEM((PAIRS, TILE, LEN), bf16),
            pltpu.VMEM((2, LEN, LEN), bf16),
            pltpu.VMEM((4, 4, ROWS8, D), bf16),
            pltpu.VMEM((4, 4, ROWS8, D), bf16),
            pltpu.SemaphoreType.DMA((2,)),
            pltpu.SemaphoreType.DMA((PAIRS,)),
            pltpu.SemaphoreType.DMA((2,)),
        ],
        compiler_params=PARAMS,
        name="self_bwd" if has_bias else "cross_bwd",
    )(*args)


GELU_C = float(np.sqrt(2.0 / np.pi))


def gelu_parts(u):
    square = u * u
    t = jnp.tanh(GELU_C * (u + 0.044715 * (u * square)))
    half = 0.5 + 0.5 * t
    slope = half + (half * (1.0 - t)) * (u * (GELU_C + (3 * 0.044715 * GELU_C) * square))
    return u * half, slope


def ffn_kernel(mode, nparts, *refs):
    fwd, bwd = mode != "bwd", mode != "fwd"
    refs = list(refs)
    me_ref, x, gain = refs[:3]
    refs = refs[3:]
    g = refs.pop(0) if bwd else None
    if mode == "bwd":
        h_i, slope_i = refs[:2]
        refs = refs[2:]
    parts = refs[:nparts]
    refs = refs[nparts:]
    out = refs.pop(0) if fwd else None
    if mode == "fwd":
        h_o, slope_o = refs[:2]
        refs = refs[2:]
    if bwd:
        dx, dgain, keep, send = refs[:4]
        refs = refs[4:]
    wi_s, wo_s, w_sem = refs[:3]
    refs = refs[3:]
    if fwd:
        n_s, acc = refs[:2]
        refs = refs[2:]
    if bwd:
        nt_s, dn, keep_s, send_s, out_sem = refs
    me = me_ref[0]
    step = pl.program_id(0)
    plan = part_plan(nparts, 8)

    def in_loads(unit):
        copies = []
        for part, (flip, first, count) in zip(parts, plan):
            if first == 0:
                to = wi_s.at[unit] if flip is None else wi_s.at[unit, me ^ flip]
                copies.append(pltpu.make_async_copy(part.at[unit], to, w_sem.at[unit]))
        return copies

    def out_loads():
        copies = []
        for part, (flip, first, count) in zip(parts, plan):
            if first + count == 8:
                if flip is None:
                    for k in range(4):
                        copies.append(
                            pltpu.make_async_copy(part.at[4 + k], wo_s.at[:, k], w_sem.at[4])
                        )
                else:
                    copies.append(
                        pltpu.make_async_copy(
                            part.at[pl.ds(4 - first, 4)], wo_s.at[me ^ flip], w_sem.at[4]
                        )
                    )
        return copies

    @pl.when(step == 0)
    def _():
        start_all(in_loads(0))
        start_all(out_loads())
        for unit in range(1, 4):
            start_all(in_loads(unit))
        v = x[...].astype(f32)
        n = rms(v, gain[...]).astype(bf16)
        if fwd:
            n_s[...] = n
            acc[...] = v
        if bwd:
            nt_s[...] = n.T
            dn[...] = jnp.zeros_like(dn)

    for unit in range(4):

        @pl.when(step == unit)
        def _():
            wait_all(in_loads(unit))

    wi = wi_s[step].reshape(D, D)
    if fwd:
        h, slope = gelu_parts(dot(n_s[...], wi))
        h = h.astype(bf16)
        if mode == "fwd":
            h_o[0] = h
            slope_o[0] = slope.astype(bf16)
    else:
        h, slope = h_i[0], slope_i[0].astype(f32)

    @pl.when(step == 0)
    def _():
        wait_all(out_loads())

    wo = wo_s[pl.ds(2 * step, 2)].reshape(D, D)
    if fwd:
        acc[...] += dot(h, wo)
    if bwd:
        du = (slope * dot_nt(g[...], wo)).astype(bf16)
        dn[...] += dot_nt(du, wi)
        put_blocks(me, dot(nt_s[...], du), step, keep_s, send_s)
        dwo = dot(h.T, g[...]).astype(bf16)
        odd = (me % 2) == 1
        slot = step ^ (me // 2)
        for k in range(4):
            first, second = dwo[k * ROWS8 : (k + 1) * ROWS8], dwo[(4 + k) * ROWS8 : (5 + k) * ROWS8]
            keep_s[slot, 4 + k] = jnp.where(odd, second, first)
            send_s[slot, 4 + k] = jnp.where(odd, first, second)

        def outs(c):
            slot = c ^ (me // 2)
            copies = []
            for n, (here, there) in enumerate(((send_s, send), (keep_s, keep))):
                copies.append(
                    pltpu.make_async_copy(here.at[:, c], there.at[:, c], out_sem.at[2 * n])
                )
                last = pl.ds(4, 4)
                copies.append(
                    pltpu.make_async_copy(here.at[slot, last], there.at[slot, last], out_sem.at[2 * n + 1])
                )
            return copies

        start_all(outs(step))

    @pl.when(step == pl.num_programs(0) - 1)
    def _():
        if fwd:
            out[...] = acc[...].astype(bf16)
        if bwd:
            dv, dg = rms_back(x[...].astype(f32), gain[...], dn[...])
            dgain[...] = dg
            dx[...] = (g[...].astype(f32) + dv).astype(bf16)
            for c in range(4):
                wait_all(outs(c))


def ffn(mode, me, x, gain, parts, g=None, saved=()):
    fwd, bwd = mode != "bwd", mode != "fwd"
    whole = pl.BlockSpec((LEN, D), lambda c: (0, 0))
    one = pl.BlockSpec((1, D), lambda c: (0, 0))
    hidden = pl.BlockSpec((1, LEN, D), lambda c: (c, 0, 0))
    hidden_shape = jax.ShapeDtypeStruct((4, LEN, D), bf16)
    args, specs = [me, x, gain], [SM, whole, one]
    if bwd:
        args, specs = args + [g], specs + [whole]
    args += list(saved)
    specs += [hidden] * len(saved)
    args += parts
    specs += [HBM] * len(parts)
    shapes, out_specs = [], []
    scratch = [
        pltpu.VMEM((4, 8, ROWS8, D), bf16),
        pltpu.VMEM((8, 4, ROWS8, D), bf16),
        pltpu.SemaphoreType.DMA((5,)),
    ]
    if fwd:
        shapes, out_specs = [LOW_ROWS], [whole]
        scratch += [pltpu.VMEM((LEN, D), bf16), pltpu.VMEM((LEN, D), f32)]
    if mode == "fwd":
        shapes += [hidden_shape] * 2
        out_specs += [hidden] * 2
    if bwd:
        shapes += [LOW_ROWS, ONE_ROW, BLOCKS8, BLOCKS8]
        out_specs += [whole, one, HBM, HBM]
        scratch += [
            pltpu.VMEM((D, LEN), bf16),
            pltpu.VMEM((LEN, D), f32),
            pltpu.VMEM((4, 8, ROWS8, D), bf16),
            pltpu.VMEM((4, 8, ROWS8, D), bf16),
            pltpu.SemaphoreType.DMA((4,)),
        ]
    return pl.pallas_call(
        functools.partial(ffn_kernel, mode, len(parts)),
        grid=(4,),
        out_shape=tuple(shapes),
        in_specs=specs,
        out_specs=tuple(out_specs),
        scratch_shapes=scratch,
        compiler_params=PARAMS,
        name="ffn_" + mode,
    )(*args)


def wide_add(*values):
    total = values[0].astype(f32)
    for value in values[1:]:
        total = total + value.astype(f32)
    return total.astype(bf16)


def diag_kernel(keep, recv, by_x, by_y):
    half = by_x.shape[0]
    total = wide_add(keep[0], recv[0])
    by_x[...] = total[:half]
    by_y[...] = total[half:]


def diag_add(keep, recv):
    _, k, r, c = keep.shape
    last = pl.BlockSpec((1, k, r, c), lambda i: (3, 0, 0, 0))
    half = pl.BlockSpec((k // 2, r, c), lambda i: (0, 0, 0))
    shape = jax.ShapeDtypeStruct((k // 2, r, c), bf16)
    return pl.pallas_call(
        diag_kernel,
        grid=(1,),
        out_shape=(shape, shape),
        in_specs=[last, last],
        out_specs=(half, half),
        compiler_params=PARAMS,
        name="diag_add",
    )(keep, recv)


def rest_kernel(keep, recv, from_x, from_y, own, for_x, for_y):
    half = from_x.shape[0]
    own[...] = wide_add(keep[0], recv[0])
    for_x[:half] = wide_add(keep[1, :half], recv[1, :half])
    for_x[half:] = wide_add(keep[1, half:], recv[1, half:], from_y[...])
    for_y[:half] = wide_add(keep[2, :half], recv[2, :half], from_x[...])
    for_y[half:] = wide_add(keep[2, half:], recv[2, half:])


def rest_add(keep, recv, from_x, from_y):
    _, k, r, c = keep.shape
    first = pl.BlockSpec((3, k, r, c // 2), lambda i: (0, 0, 0, i))
    half = pl.BlockSpec((k // 2, r, c // 2), lambda i: (0, 0, i))
    full = pl.BlockSpec((k, r, c // 2), lambda i: (0, 0, i))
    shape = jax.ShapeDtypeStruct((k, r, c), bf16)
    return pl.pallas_call(
        rest_kernel,
        grid=(2,),
        out_shape=(shape,) * 3,
        in_specs=[first, first, half, half],
        out_specs=(full,) * 3,
        compiler_params=PARAMS,
        name="rest_add",
    )(keep, recv, from_x, from_y)


ALL = (0, 1, 2, 3)
ENC = (1, 2)
DEC = (0, 3)


def across(x, flip, planes):
    wide, narrow = lax.axis_size("wide"), lax.axis_size("narrow")
    pairs = [(i * narrow + n, (i ^ flip) * narrow + n) for i in range(wide) for n in planes]
    return lax.ppermute(x, ("wide", "narrow"), pairs)


def between(x, pairs):
    return lax.ppermute(x, "narrow", pairs)


def in_units(local):
    return jnp.transpose(local.reshape(local.shape[0], 4, D), (1, 0, 2))


def out_units(local):
    return local.reshape(4, local.shape[0] // 4, D)


def tie(*values):
    return lax.optimization_barrier(values)


def whole_pack(shard):
    k = shard.shape[0]
    full = lax.all_gather(shard, "wide", axis=1)
    if k == 8:
        inner = full[:4].reshape(4, 8, ROWS8, D)
        outer = jnp.transpose(full[4:], (1, 0, 2, 3)).reshape(8, 4, ROWS8, D)
        return [jnp.concatenate([inner, jnp.transpose(outer, (1, 0, 2, 3))])]
    return [full.reshape(k, 8, ROWS8, D)]


def gather_near(shard, planes=ALL):
    return across(shard, 2, planes), across(shard, 4, planes), across(shard, 1, planes)


def gather_far(shard, near, planes=ALL):
    px, py, pc = near
    k = shard.shape[0]
    first = across(px[: k // 2], 4, planes)
    second = across(py[k // 2 :], 2, planes)
    parts = [px, py, first, second]
    return [shard] + parts + [pc] + [across(part, 1, planes) for part in parts]


def whole_scatter(keep, send):
    k = keep.shape[1]
    blocks = jnp.stack([keep, send], axis=1).reshape(8, k, ROWS8, D)
    inner = jnp.transpose(blocks[:, :4], (1, 0, 2, 3)).reshape(4, D, D)
    inner = lax.psum_scatter(inner, "wide", scatter_dimension=1, tiled=True)
    if k == 4:
        return inner
    outer = lax.psum_scatter(blocks[:, 4:].reshape(FF, D), "wide", scatter_dimension=0, tiled=True)
    return jnp.concatenate([inner, outer.reshape(inner.shape)])


class Scatter:
    def __init__(self, keep, send, planes=ALL):
        self.keep, self.planes = keep, planes
        self.small = lax.axis_size("wide") == 8
        self.state = (send,)
        if self.small:
            self.state = (across(send, 1, planes),)
        self.phase = 0

    def go(self):
        if not self.small:
            return self
        if self.phase == 0:
            (self.recv,) = self.state
            by_x, by_y = diag_add(self.keep, self.recv)
            self.state = across(by_x, 2, self.planes), across(by_y, 4, self.planes)
        elif self.phase == 1:
            own, for_x, for_y = rest_add(self.keep, self.recv, *self.state)
            self.state = own, across(for_x, 2, self.planes), across(for_y, 4, self.planes)
        self.phase += 1
        return self

    def result(self):
        if not self.small:
            return whole_scatter(self.keep, self.state[0])
        return wide_add(*self.state)


def tie_all(scatters, *values):
    counts = [len(s.state) for s in scatters]
    flat = tie(*[v for s in scatters for v in s.state], *values)
    for s, count in zip(scatters, counts):
        s.state, flat = flat[:count], flat[count:]
    return flat


def over_planes(share, middle):
    total = wide_add(share, between(share, [(1, 2), (2, 1)]))
    return jnp.where(middle, total, between(total, [(1, 0), (2, 3)]))


def summed(x):
    if lax.axis_size("wide") != 8:
        return lax.psum(x, ("wide", "narrow"))
    for flip in (1, 2, 4):
        x = x + across(x, flip, ALL)
    for flip in (1, 2):
        x = x + between(x, [(n, n ^ flip) for n in range(4)])
    return x


def on_device(
    enc_in,
    dec_in,
    dec_cot,
    segments,
    enc_attn_gain,
    enc_query,
    enc_key,
    enc_value,
    enc_output,
    enc_table,
    enc_ffn_gain,
    enc_ffn_in,
    enc_ffn_out,
    dec_self_gain,
    dec_query,
    dec_key,
    dec_value,
    dec_output,
    dec_table,
    dec_cross_gain,
    cross_query,
    cross_key,
    cross_value,
    cross_output,
    dec_ffn_gain,
    dec_ffn_in,
    dec_ffn_out,
):
    plane = lax.axis_index("narrow")
    is_enc = (plane == 1) | (plane == 2)
    row = plane // 2

    def own(x):
        return lax.dynamic_slice_in_dim(x, row * LEN, LEN, 0)

    def pick(enc, dec):
        return jnp.where(is_enc, enc, dec)

    def gain_of(g):
        return g.astype(f32).reshape(1, D)

    seg = lax.dynamic_slice_in_dim(segments, row, 1, 0)
    segr, segc = seg, seg.reshape(LEN, 1)
    src = pick(own(enc_in), own(dec_in))
    cot = own(dec_cot)

    me = lax.axis_index("wide") if lax.axis_size("wide") == 8 else 0
    me = jnp.stack([jnp.asarray(me, jnp.int32), is_enc.astype(jnp.int32)])

    pack_a = jnp.stack(
        [
            pick(enc_query, dec_query),
            pick(enc_key, dec_key),
            pick(enc_value, dec_value),
            pick(enc_output, dec_output),
        ]
    )
    pack_f = jnp.concatenate(
        [in_units(pick(enc_ffn_in, dec_ffn_in)), out_units(pick(enc_ffn_out, dec_ffn_out))]
    )
    pack_c = jnp.stack([cross_query, cross_key, cross_value, cross_output])
    small = lax.axis_size("wide") == 8
    if small:
        near_a = gather_near(pack_a)

    enc_ids, enc_far = tile_ids(True)
    dec_ids, dec_far = tile_ids(False)
    ids = pick(jnp.asarray(enc_ids), jnp.asarray(dec_ids))
    far_ids = pick(jnp.asarray(enc_far), jnp.asarray(dec_far))
    buckets = jnp.arange(BUCKETS + 1, dtype=jnp.int32)
    hot = (ids[None] == buckets[:, None, None, None]).astype(bf16)
    far_hot = (far_ids[None] == buckets[:, None]).astype(bf16)
    table = jnp.concatenate([pick(enc_table, dec_table), jnp.full((1, HEADS), MASKED, bf16)])
    bias = jnp.einsum("bh,bsij->hsij", table, hot, preferred_element_type=f32)
    far = jnp.einsum("bh,bs->hs", table, far_hot, preferred_element_type=f32)

    gain_a = pick(gain_of(enc_attn_gain), gain_of(dec_self_gain))
    enc_gain = gain_of(enc_ffn_gain)
    gain_c = gain_of(dec_cross_gain)
    if small:
        *near_a, pack_f, bias, far, src, cot, segc, me = tie(
            *near_a, pack_f, bias, far, src, cot, segc, me
        )
        w_attn = gather_far(pack_a, near_a)
        near_f = gather_near(pack_f)
    else:
        w_attn, w_ffn, w_cross = whole_pack(pack_a), whole_pack(pack_f), whole_pack(pack_c)
    z1, x1, *saved = attn_fwd(me, src, gain_a, w_attn, segr, segc, bias=bias, far=far)
    if small:
        z1, x1, *near_f, pack_c = tie(z1, x1, *near_f, pack_c)
        w_ffn = gather_far(pack_f, near_f)
        near_c = gather_near(pack_c, DEC)
    enc_out, *saved_f = ffn("fwd", me, x1, enc_gain, w_ffn)
    if small:
        enc_out, *near_c = tie(enc_out, *near_c)
    memory = between(enc_out, [(1, 0), (2, 3)])
    if small:
        w_cross = gather_far(pack_c, near_c, DEC)
    _, z2, *saved_c = attn_fwd(me, z1, gain_c, w_cross, segr, segc, ksrc=memory)

    def by_columns(x):
        return lax.all_to_all(x, "narrow", split_axis=1, concat_axis=0, tiled=True)

    def rows_by_block(parts):
        rows = [parts[n * LEN : (n + 1) * LEN] for n in range(4)]
        return jnp.concatenate([rows[1], rows[2]]), jnp.concatenate([rows[0], rows[3]])

    dec_out, gz2, dgain_df, *blocks = ffn("both", me, z2, gain_of(dec_ffn_gain), w_ffn, cot)
    sum_df = Scatter(*blocks, DEC)
    out_cols = by_columns(pick(enc_out, dec_out))
    gz1, *blocks, dgain_c, genc_out = attn_bwd(me, gz2, z1, gain_c, w_cross, saved_c, ksrc=memory)
    genc_out, gz1, out_cols, *blocks = tie_all([sum_df], genc_out, gz1, out_cols, *blocks)
    genc = between(genc_out, [(0, 1), (3, 2)])
    sum_c = Scatter(*blocks, DEC)
    sum_df.go()
    (genc,) = tie_all([sum_df, sum_c], genc)
    sum_df.go()
    sum_c.go()
    gx1, dgain_ef, *blocks = ffn("bwd", me, x1, enc_gain, w_ffn, genc, saved_f)
    gx1, *blocks = tie_all([sum_df, sum_c], gx1, *blocks)
    sum_ef = Scatter(*blocks, ENC)
    s_df = sum_df.result()
    part_df = between(s_df, [(0, 1), (3, 2)])
    sum_c.go()
    din, *blocks, dgain_a, dtile, dfar = attn_bwd(
        me, gz1, src, gain_a, w_attn, saved, gother=gx1
    )
    din, dgain_a, dtile, dfar, part_df, *blocks = tie_all(
        [sum_ef, sum_c], din, dgain_a, dtile, dfar, part_df, *blocks
    )
    sum_a = Scatter(*blocks)
    grad_cols = by_columns(din)
    sum_ef.go()
    s_c = sum_c.result()
    part_c = between(s_c, [(0, 1), (3, 2)])
    tie_all([sum_ef, sum_a])
    sum_ef.go()
    sum_a.go()
    s_ef = sum_ef.result()
    s_a = sum_a.go().result()
    part_s = between(s_a, [(0, 1), (3, 2)])

    def rows_of(f):
        return jnp.transpose(f[:4], (1, 0, 2)).reshape(-1, FF), f[4:].reshape(-1, D)

    g_df, g_c, g_s, g_ef, g_e = (
        over_planes(s, is_enc).astype(f32) for s in (part_df, part_c, part_s, s_ef, s_a)
    )
    gi_d, go_d = rows_of(g_df)
    gi_e, go_e = rows_of(g_ef)

    dtable = jnp.einsum("hsij,bsij->bh", dtile, hot, preferred_element_type=f32)
    dtable = dtable + jnp.einsum("hsj,bs->bh", dfar, far_hot.astype(f32))
    dtable = jnp.pad(dtable[:BUCKETS].reshape(1, BUCKETS * HEADS), ((0, 0), (0, D - BUCKETS * HEADS)))
    none = jnp.zeros((1, D), f32)

    def when_enc(x):
        return jnp.where(is_enc, x, 0.0)

    def when_dec(x):
        return jnp.where(is_enc, 0.0, x)

    sums = jnp.concatenate(
        [
            when_enc(dgain_a),
            when_enc(dgain_ef),
            when_dec(dgain_a),
            when_dec(dgain_c),
            when_dec(dgain_df),
            when_enc(dtable),
            when_dec(dtable),
            none,
        ]
    )
    sums = summed(sums)
    tables = sums[5:7, : BUCKETS * HEADS].reshape(2, BUCKETS, HEADS)

    enc_cols, dec_cols = rows_by_block(out_cols)
    enc_grad_cols, dec_grad_cols = rows_by_block(grad_cols)
    return (
        enc_cols,
        dec_cols,
        enc_grad_cols,
        dec_grad_cols,
        sums[0],
        g_e[0],
        g_e[1],
        g_e[2],
        g_e[3],
        tables[0],
        sums[1],
        gi_e,
        go_e,
        sums[2],
        g_s[0],
        g_s[1],
        g_s[2],
        g_s[3],
        tables[1],
        sums[3],
        g_c[0],
        g_c[1],
        g_c[2],
        g_c[3],
        sums[4],
        gi_d,
        go_d,
    )


def solution(mesh):
    rows, copied = P("wide", None), P()
    block = P("wide", "narrow")
    gains = (copied,)
    attention = (rows,) * 4
    placed = (
        (rows,) * 4
        + gains
        + attention
        + (copied,)
        + gains
        + (rows,) * 2
        + gains
        + attention
        + (copied,)
        + gains
        + attention
        + gains
        + (rows,) * 2
    )
    return jax.shard_map(
        on_device,
        mesh=mesh,
        in_specs=placed,
        out_specs=(block,) * 4 + placed[4:],
        check_vma=False,
    )
```

time: 738 us -> 547 us (0.74)
  starting transfers between devices: 235 us -> 148 us
  local copies, waits for them, and re-layouts: 91.7 us -> 35.3 us
  other arithmetic: 70.3 us -> 32.1 us
  waiting for transfers between devices: 174 us -> 137 us
  Pallas kernels: 151 us -> 177 us
    ppermute x83 -> x50, starting transfers between devices: 135 us -> 78.8 us  [across(): return lax.ppermute(x, ('wide', 'narrow'), pairs)]
    ppermute x22 -> x17, waiting for transfers between devices: 119 us -> 78.1 us  [between(): return lax.ppermute(x, 'narrow', pairs)]
    ppermute x22 -> x17, starting transfers between devices: 89.2 us -> 50.7 us  [between(): return lax.ppermute(x, 'narrow', pairs)]
    dynamic_update_slice x28 -> x0, local copies, waits for them, and re-layouts: 33.9 us -> none  [gathered(): full = lax.dynamic_update_slice(full, piece[:, None], (0, me ^ flip, 0, 0))]
    pallas_call x7 -> x15, Pallas kernels: 151 us -> 177 us  [the longest x3 57.5 us: ffn(): pl.pallas_call(functools.partial(ffn_kernel, mode, len(parts)), grid=(4,)...]
    convert_element_type x37 -> x12, other arithmetic: 36 us -> 20.8 us  [the longest x9 17.9 us: wide_add(): return total.astype(bf16)]
    squeeze x6 -> x0, local copies, waits for them, and re-layouts: 13.7 us -> none  [block(): return lax.dynamic_slice(blocks, (0, me ^ flip, 0, 0), (k, 1, r, c))[:, 0]]
    all_to_all x2, starting transfers between devices: 10.5 us -> 18.7 us  [by_columns(): return lax.all_to_all(x, 'narrow', split_axis=1, concat_axis=0, tiled=True)]
  transfers between devices with their start and end apart: 107 -> 69, of which waited for: 27 -> 23; matrix products, arithmetic and copies ran while one was open for 20% -> 10% of each run, Pallas kernels for 15% -> 23%
where the time goes in v2:
time: 547 us; the launch traced here: 537 us
  Pallas kernels  177 us (32%)
  starting transfers between devices  148 us (27%)
  waiting for transfers between devices  137 us (25%)
  local copies, waits for them, and re-layouts  35.3 us (6%)
  other arithmetic  32.1 us (6%)
    ppermute x50, starting transfers between devices, across(): return lax.ppermute(x, ('wide', 'narrow'), pairs)  78.8 us
    ppermute x17, waiting for transfers between devices, between(): return lax.ppermute(x, 'narrow', pairs)  78.1 us
    ppermute x50, waiting for transfers between devices, across(): return lax.ppermute(x, ('wide', 'narrow'), pairs)  59.4 us
    pallas_call x3, Pallas kernels, ffn(): pl.pallas_call(functools.partial(ffn_kernel, mode, len(parts)), grid=(4,)...  57.5 us
    pallas_call x2, Pallas kernels, attn_bwd(): pl.pallas_call(functools.partial(attn_bwd_kernel, has_bias, len(parts)),...  51.2 us
    ppermute x17, starting transfers between devices, between(): return lax.ppermute(x, 'narrow', pairs)  50.7 us
    pallas_call x2, Pallas kernels, attn_fwd(): pl.pallas_call(functools.partial(attn_fwd_kernel, has_bias, len(parts)),...  42 us
    all_to_all x2, starting transfers between devices, by_columns(): return lax.all_to_all(x, 'narrow', split_axis=1, concat_axis=0, tiled=True)  18.7 us
  transfers between devices with their start and end apart: 69, of which 23 were waited for; matrix products, arithmetic and copies ran while one was open for 10% of the time, Pallas kernels for 23%

profile of v2, /device:TPU:0, one launch (start us, length us, event | category | flops | bytes accessed | tf_op | source)
XLA Modules:
  0.0 537.5 jit_solution(6658833104787283184)
XLA Ops:
  25.9 5.7 %collective-permute-done.3.refs_10_.refs_13_ = bf16[2,96,768]{2,1,0:T(8,128)(2,1)S(1)} collective-permute-done((bf16[2,96,768]{2,1,0:T(8,128)(2,1)S(1)}, bf16[2,96,768]{2,1,0:T(8,128)(2,1)S(1)}, u32[]{:S(2)}, u32[]{:S(2)}) %collective-permute-start.3) | collective-permute-done | bytes 294944 | tf_op jit(solution)/shard_map/ppermute | solution.py:650
  41.5 21.2 %self_fwd.1 = (f32[512,768]{1,0:T(8,128)}, bf16[512,768]{1,0:T(8,128)(2,1)}, bf16[6,512,128]{2,1,0:T(8,128)(2,1)}, bf16[6,512,128]{2,1,0:T(8,128)(2,1)}, bf16[6,...) custom-call(s32[2]{0:T(128)} %pad_add_fusion.refs_0_, ...), custom_call_target="tpu_custom_call" | custom-call | tf_op jit(solution)/shard_map/self_fwd/pallas_call | solution.py:233
  65.4 13.1 %collective-permute-done.12.refs_6_.refs_7_.refs_9_ = bf16[4,96,768]{2,1,0:T(8,128)(2,1)S(1)} collective-permute-done((bf16[4,96,768]{2,1,0:T(8,128)(2,1)S(1)}, bf16[4,96,768]{2,1,0:T(8,128)(2,1)S(1)}, u32[]{:S(2)}, u32[]{:S(2)}) %collective-permute-start.12) | collective-permute-done | bytes 589856 | tf_op jit(solution)/shard_map/ppermute | solution.py:650
  89.4 13.7 %ffn_fwd.1 = (bf16[512,768]{1,0:T(8,128)(2,1)}, bf16[4,512,768]{2,1,0:T(8,128)(2,1)}, bf16[4,512,768]{2,1,0:T(8,128)(2,1)}) custom-call(s32[2]{0:T(128)} %pad_add_fusion.refs_0_, bf16[512,768]{1,0:T(8,128)(2,1)} %get-tuple-element.147.refs_1_, f32[1,768]{1,0:T(1,128)} %reshape.131.refs_2_, bf16[8,96,768]{2,1,0:T(8,128)(2,1)} %copy-done.2, ...), custom_call_target="tpu_custom_call" | custom-call | tf_op jit(solution)/shard_map/ffn_fwd/pallas_call | solution.py:574
  107.8 3.2 collective-permute-start.22
  114.0 3.4 collective-permute-start.23
  120.6 4.7 collective-permute-done.23.refs_10_.refs_14_
  130.5 20.8 %cross_fwd.1 = (f32[512,768]{1,0:T(8,128)}, bf16[512,768]{1,0:T(8,128)(2,1)}, bf16[6,512,128]{2,1,0:T(8,128)(2,1)}, bf16[6,512,128]{2,1,0:T(8,128)(2,1)}, bf16[6...) custom-call(s32[2]{0:T(128)} %pad_add_fusion.refs_0_, ...), custom_call_target="tpu_custom_call" | custom-call | tf_op jit(solution)/shard_map/cross_fwd/pallas_call | solution.py:233
  151.3 24.8 %ffn_both.1 = (bf16[512,768]{1,0:T(8,128)(2,1)}, bf16[512,768]{1,0:T(8,128)(2,1)}, f32[1,768]{1,0:T(1,128)}, bf16[4,8,96,768]{3,2,1,0:T(8,128)(2,1)}, bf16[4,8,96,768]{3,2,1,0:T(8,128)(2,1)}) custom-call(s32[2]{0:T(128)} %pad_add_fusion.refs_0_, bf16[512,768]{1,0:T(8,128)(2,1)} %get-tuple-element.157.refs_1_, f32[1,768]{1,0:T(1,128)} %reshape.133.refs_2_, ...), custom_call_target="tpu_custom_call" | custom-call | tf_op jit(solution)/shard_map/ffn_both/pallas_call | solution.py:574
  180.9 14.8 %all-to-all-start = ((bf16[512,4,192]{0,2,1:T(8,128)(2,1)}), bf16[512,4,192]{0,2,1:T(8,128)(2,1)S(1)}, u32[]{:S(2)}, u32[]{:S(2)}) async-start(bf16[512,4,192]{0,2,1:T(8,128)(2,1)} %bitcast.15), calls=%async_computation | async-start | bytes 1572864 | tf_op jit(solution)/shard_map/all_to_all | solution.py:856
  195.7 25.0 %cross_bwd.1 = (f32[512,768]{1,0:T(8,128)}, bf16[4,4,96,768]{3,2,1,0:T(8,128)(2,1)}, bf16[4,4,96,768]{3,2,1,0:T(8,128)(2,1)}, f32[1,768]{1,0:T(1,128)}, bf16[512,768]{1,0:T(8,128)(2,1)}) custom-call(s32[2]{0:T(128)} %pad_add_fusion.refs_0_, bf16[512,768]{1,0:T(8,128)(2,1)} %get-tuple-element.160.refs_1_, f32[512,768]{1,0:T(8,128)} %get-tuple-element.146.refs_1_.refs_2_, ...), custom_call_target="tpu_custom_call" | custom-call | tf_op jit(solution)/shard_map/cross_bwd/pallas_call | solution.py:373
  222.7 3.7 collective-permute-start.32
  229.2 3.4 collective-permute-start.29
  235.3 10.5 %collective-permute-done.29.from_x = bf16[4,96,768]{2,1,0:T(8,128)(2,1)S(1)} collective-permute-done((bf16[4,96,768]{2,1,0:T(8,128)(2,1)}, bf16[4,96,768]{2,1,0:T(8,128)(2,1)S(1)}, u32[]{:S(2)}, u32[]{:S(2)}) %collective-permute-start.29) | collective-permute-done | bytes 589856 | tf_op jit(solution)/shard_map/ppermute | solution.py:650
  245.7 3.1 collective-permute-done.30.from_y
  249.7 6.0 %rest_add.4 = (bf16[8,96,768]{2,1,0:T(8,128)(2,1)}, bf16[8,96,768]{2,1,0:T(8,128)(2,1)}, bf16[8,96,768]{2,1,0:T(8,128)(2,1)}) custom-call(bf16[4,8,96,768]{3,2,1,0:T(8,128)(2,1)} %get-tuple-element.172.keep, bf16[4,8,96,768]{3,2,1,0:T(8,128)(2,1)} %collective-permute-done.28.recv, bf16[4,96,768]{2,1,0:T(8,128)(2,1)} %copy-done.39, bf16[4,96,768]{2,1,0:T(8,128)(2,1)} %copy-done.40), custom_call_target="tpu_custom_call" | custom-call | tf_op jit(solution)/shard_map/rest_add/pallas_call | solution.py:631
  262.9 3.4 collective-permute-start.35
  266.3 3.2 collective-permute-start.36
  269.5 19.0 %ffn_bwd.1 = (bf16[512,768]{1,0:T(8,128)(2,1)}, f32[1,768]{1,0:T(1,128)}, bf16[4,8,96,768]{3,2,1,0:T(8,128)(2,1)}, bf16[4,8,96,768]{3,2,1,0:T(8,128)(2,1)}) custom-call(s32[2]{0:T(128)} %pad_add_fusion.refs_0_, bf16[512,768]{1,0:T(8,128)(2,1)} %get-tuple-element.147.refs_1_, f32[1,768]{1,0:T(1,128)} %reshape.131.refs_2_, ...), custom_call_target="tpu_custom_call" | custom-call | tf_op jit(solution)/shard_map/ffn_bwd/pallas_call | solution.py:574
  299.0 3.1 rest_add.5
  302.1 3.4 collective-permute-start.38
  308.4 26.2 %self_bwd.1 = (bf16[512,768]{1,0:T(8,128)(2,1)}, bf16[4,4,96,768]{3,2,1,0:T(8,128)(2,1)}, bf16[4,4,96,768]{3,2,1,0:T(8,128)(2,1)}, f32[1,768]{1,0:T(1,128)}, bf1...) custom-call(s32[2]{0:T(128)} %pad_add_fusion.refs_0_, f32[512,768]{1,0:T(8,128)} %get-tuple-element.199.refs_1_, ...), custom_call_target="tpu_custom_call" | custom-call | tf_op jit(solution)/shard_map/self_bwd/pallas_call | solution.py:373
  349.9 9.6 %collective-permute-done.62 = bf16[4,96,768]{2,1,0:T(8,128)(2,1)} collective-permute-done((bf16[4,96,768]{2,1,0:T(8,128)(2,1)}, bf16[4,96,768]{2,1,0:T(8,128)(2,1)}, u32[]{:S(2)}, u32[]{:S(2)}) %collective-permute-start.62) | collective-permute-done | bytes 589856 | tf_op jit(solution)/shard_map/ppermute | solution.py:654
  367.8 6.2 %collective-permute-done.42 = f32[8,768]{1,0:T(8,128)S(1)} collective-permute-done((f32[8,768]{1,0:T(8,128)S(1)}, f32[8,768]{1,0:T(8,128)S(1)}, u32[]{:S(2)}, u32[]{:S(2)}) %collective-permute-start.42) | collective-permute-done | bytes 24608 | tf_op jit(solution)/shard_map/ppermute | solution.py:650
  377.9 6.8 %collective-permute-start.44 = (f32[8,768]{1,0:T(8,128)S(1)}, f32[8,768]{1,0:T(8,128)S(1)}, u32[]{:S(2)}, u32[]{:S(2)}) collective-permute-start(f32[8,768]{1,0:T(8,128)S(1)} %add.77), channel_id=1, source_target_pairs={{0,1},{1,0},{2,3},{3,2},{4,5},{5,4},{6,7},{7,6},{8,9},{9,8},{10,11... | collective-permute-start | bytes 73736 | tf_op jit(solution)/shard_map/ppermute | solution.py:654
  385.9 4.7 rest_add.7
  397.6 3.2 rest_add.6
  406.5 3.9 all-to-all-start.1
  418.6 19.6 %collective-permute-start.59 = (bf16[4,96,768]{2,1,0:T(8,128)(2,1)}, bf16[4,96,768]{2,1,0:T(8,128)(2,1)}, u32[]{:S(2)}, u32[]{:S(2)}) collective-permute-start(bf16[4,96,768]{2,1,0:T(8,128)(2,1)} %add_convert_fusion.8), channel_id=1, source_target_pairs={{0,1},{3,2},{4,5},{7,6},{8,9},{11,10},{12,13},{15,14},{16,17},{19,... | collective-permute-start | bytes 1769480 | tf_op jit(solution)/shard_map/ppermute | solution.py:654
  457.7 26.8 %collective-permute-done.54 = bf16[4,96,768]{2,1,0:T(8,128)(2,1)S(1)} collective-permute-done((bf16[4,96,768]{2,1,0:T(8,128)(2,1)S(1)}, bf16[4,96,768]{2,1,0:T(8,128)(2,1)S(1)}, u32[]{:S(2)}, u32[]{:S(2)}) %collective-permute-start.54) | collective-permute-done | bytes 589856 | tf_op jit(solution)/shard_map/ppermute | solution.py:654
  485.6 22.9 %collective-permute-done.61 = bf16[4,96,768]{2,1,0:T(8,128)(2,1)S(1)} collective-permute-done((bf16[4,96,768]{2,1,0:T(8,128)(2,1)S(1)}, bf16[4,96,768]{2,1,0:T(8,128)(2,1)S(1)}, u32[]{:S(2)}, u32[]{:S(2)}) %collective-permute-start.61) | collective-permute-done | bytes 589856 | tf_op jit(solution)/shard_map/ppermute | solution.py:654
  511.8 18.4 %collective-permute-done.58 = bf16[8,96,768]{2,1,0:T(8,128)(2,1)S(1)} collective-permute-done((bf16[8,96,768]{2,1,0:T(8,128)(2,1)S(1)}, bf16[8,96,768]{2,1,0:T(8,128)(2,1)S(1)}, u32[]{:S(2)}, u32[]{:S(2)}) %collective-permute-start.58) | collective-permute-done | bytes 1179680 | tf_op jit(solution)/shard_map/ppermute | solution.py:654
  (348 shorter events, 177.5 us)
Async XLA Ops:
  23.9 38.9 %collective-permute-start.10 = (bf16[8,96,768]{2,1,0:T(8,128)(2,1)S(1)}, bf16[8,96,768]{2,1,0:T(8,128)(2,1)S(1)}, u32[]{:S(2)}, u32[]{:S(2)}) collective-permute-start(bf16[8,96,768]{2,1,0:T(8,128)(2,1)S(1)} %pad_maximum_fusion.refs_3_.refs_4_.refs_6_), channel_id=1, source_target_pairs={{0,16},{1,17},{2,18},{3,19},{4,20},{5,21},{6,22},{7,23},{8,24},{9,... | collective-permute-start | bytes 3538952 | tf_op jit(solution)/shard_map/ppermute | solution.py:650
  24.2 38.5 %collective-permute-start.11 = (bf16[8,96,768]{2,1,0:T(8,128)(2,1)S(1)}, bf16[8,96,768]{2,1,0:T(8,128)(2,1)}, u32[]{:S(2)}, u32[]{:S(2)}) collective-permute-start(bf16[8,96,768]{2,1,0:T(8,128)(2,1)S(1)} %pad_maximum_fusion.refs_3_.refs_4_.refs_6_), channel_id=1, source_target_pairs={{0,4},{1,5},{2,6},{3,7},{4,0},{5,1},{6,2},{7,3},{8,12},{9,13},{10,... | collective-permute-start | bytes 3538952 | tf_op jit(solution)/shard_map/ppermute | solution.py:650
  24.2 38.5 %collective-permute-start.9 = (bf16[8,96,768]{2,1,0:T(8,128)(2,1)S(1)}, bf16[8,96,768]{2,1,0:T(8,128)(2,1)S(1)}, u32[]{:S(2)}, u32[]{:S(2)}) collective-permute-start(bf16[8,96,768]{2,1,0:T(8,128)(2,1)S(1)} %pad_maximum_fusion.refs_3_.refs_4_.refs_6_), channel_id=1, source_target_pairs={{0,8},{1,9},{2,10},{3,11},{4,12},{5,13},{6,14},{7,15},{8,0},{9,1},... | collective-permute-start | bytes 3538952 | tf_op jit(solution)/shard_map/ppermute | solution.py:650
  64.9 23.5 %collective-permute-start.14 = (bf16[8,96,768]{2,1,0:T(8,128)(2,1)S(1)}, bf16[8,96,768]{2,1,0:T(8,128)(2,1)S(1)}, u32[]{:S(2)}, u32[]{:S(2)}) collective-permute-start(bf16[8,96,768]{2,1,0:T(8,128)(2,1)S(1)} %collective-permute-done.9.refs_4_.refs_5_.refs_7_), channel_id=1, source_target_pairs={{0,4},{1,5},{2,6},{3,7},{4,0},{5,1},{6,2},{7,3},{8,12},{9,13},{10,... | collective-permute-start | bytes 3538952 | tf_op jit(solution)/shard_map/ppermute | solution.py:650
  64.9 23.5 %collective-permute-start.15 = (bf16[8,96,768]{2,1,0:T(8,128)(2,1)S(1)}, bf16[8,96,768]{2,1,0:T(8,128)(2,1)}, u32[]{:S(2)}, u32[]{:S(2)}) collective-permute-start(bf16[8,96,768]{2,1,0:T(8,128)(2,1)S(1)} %collective-permute-done.10.refs_5_.refs_6_.refs_8_), channel_id=1, source_target_pairs={{0,4},{1,5},{2,6},{3,7},{4,0},{5,1},{6,2},{7,3},{8,12},{9,13},{10,... | collective-permute-start | bytes 3538952 | tf_op jit(solution)/shard_map/ppermute | solution.py:650
  79.7 23.4 %collective-permute-start.18 = (bf16[4,96,768]{2,1,0:T(8,128)(2,1)}, bf16[4,96,768]{2,1,0:T(8,128)(2,1)}, u32[]{:S(2)}, u32[]{:S(2)}) collective-permute-start(bf16[4,96,768]{2,1,0:T(8,128)(2,1)} %pad_maximum_fusion.2.refs_6_.refs_10_), channel_id=1, source_target_pairs={{0,8},{3,11},{4,12},{7,15},{8,0},{11,3},{12,4},{15,7},{16,24},{19,... | collective-permute-start | bytes 1769480 | tf_op jit(solution)/shard_map/ppermute | solution.py:650
  103.1 25.6 %collective-permute-start.21 = (bf16[512,768]{1,0:T(8,128)(2,1)}, bf16[512,768]{1,0:T(8,128)(2,1)S(1)}, u32[]{:S(2)}, u32[]{:S(2)}) collective-permute-start(bf16[512,768]{1,0:T(8,128)(2,1)} %get-tuple-element.153), channel_id=1, source_target_pairs={{1,0},{2,3},{5,4},{6,7},{9,8},{10,11},{13,12},{14,15},{17,16},{18,... | collective-permute-start | bytes 2359304 | tf_op jit(solution)/shard_map/ppermute | solution.py:654
  176.1 44.7 %collective-permute-start.28 = (bf16[4,8,96,768]{3,2,1,0:T(8,128)(2,1)}, bf16[4,8,96,768]{3,2,1,0:T(8,128)(2,1)}, u32[]{:S(2)}, u32[]{:S(2)}) collective-permute-start(bf16[4,8,96,768]{3,2,1,0:T(8,128)(2,1)} %get-tuple-element.159), channel_id=1, source_target_pairs={{0,4},{3,7},{4,0},{7,3},{8,12},{11,15},{12,8},{15,11},{16,20},{19,... | collective-permute-start | bytes 14155784 | tf_op jit(solution)/shard_map/ppermute | solution.py:650
  180.9 39.8 %all-to-all-start = ((bf16[512,4,192]{0,2,1:T(8,128)(2,1)}), bf16[512,4,192]{0,2,1:T(8,128)(2,1)S(1)}, u32[]{:S(2)}, u32[]{:S(2)}) async-start(bf16[512,4,192]{0,2,1:T(8,128)(2,1)} %bitcast.15), calls=%async_computation | async-start | bytes 1572864 | tf_op jit(solution)/shard_map/all_to_all | solution.py:856
  220.8 28.9 %collective-permute-start.31 = (bf16[4,4,96,768]{3,2,1,0:T(8,128)(2,1)}, bf16[4,4,96,768]{3,2,1,0:T(8,128)(2,1)S(1)}, u32[]{:S(2)}, u32[]{:S(2)}) collective-permute-start(bf16[4,4,96,768]{3,2,1,0:T(8,128)(2,1)} %get-tuple-element.176), channel_id=1, source_target_pairs={{0,4},{3,7},{4,0},{7,3},{8,12},{11,15},{12,8},{15,11},{16,20},{19,... | collective-permute-start | bytes 7077896 | tf_op jit(solution)/shard_map/ppermute | solution.py:650
  222.7 26.1 %collective-permute-start.32 = (bf16[512,768]{1,0:T(8,128)(2,1)}, bf16[512,768]{1,0:T(8,128)(2,1)}, u32[]{:S(2)}, u32[]{:S(2)}) collective-permute-start(bf16[512,768]{1,0:T(8,128)(2,1)} %get-tuple-element.177), channel_id=1, source_target_pairs={{0,1},{3,2},{4,5},{7,6},{8,9},{11,10},{12,13},{15,14},{16,17},{19,... | collective-permute-start | bytes 2359304 | tf_op jit(solution)/shard_map/ppermute | solution.py:654
  255.7 36.4 %collective-permute-start.33 = (bf16[8,96,768]{2,1,0:T(8,128)(2,1)}, bf16[8,96,768]{2,1,0:T(8,128)(2,1)S(1)}, u32[]{:S(2)}, u32[]{:S(2)}) collective-permute-start(bf16[8,96,768]{2,1,0:T(8,128)(2,1)} %get-tuple-element.181), channel_id=1, source_target_pairs={{0,8},{3,11},{4,12},{7,15},{8,0},{11,3},{12,4},{15,7},{16,24},{19,... | collective-permute-start | bytes 3538952 | tf_op jit(solution)/shard_map/ppermute | solution.py:650
  258.1 34.0 %collective-permute-start.34 = (bf16[8,96,768]{2,1,0:T(8,128)(2,1)}, bf16[8,96,768]{2,1,0:T(8,128)(2,1)}, u32[]{:S(2)}, u32[]{:S(2)}) collective-permute-start(bf16[8,96,768]{2,1,0:T(8,128)(2,1)} %get-tuple-element.182), channel_id=1, source_target_pairs={{0,16},{3,19},{4,20},{7,23},{8,24},{11,27},{12,28},{15,31},{16,0},... | collective-permute-start | bytes 3538952 | tf_op jit(solution)/shard_map/ppermute | solution.py:650
  262.9 27.1 %collective-permute-start.35 = (bf16[2,96,768]{2,1,0:T(8,128)(2,1)}, bf16[2,96,768]{2,1,0:T(8,128)(2,1)S(1)}, u32[]{:S(2)}, u32[]{:S(2)}) collective-permute-start(bf16[2,96,768]{2,1,0:T(8,128)(2,1)} %get-tuple-element.185), channel_id=1, source_target_pairs={{0,8},{3,11},{4,12},{7,15},{8,0},{11,3},{12,4},{15,7},{16,24},{19,... | collective-permute-start | bytes 884744 | tf_op jit(solution)/shard_map/ppermute | solution.py:650
  266.3 25.8 %collective-permute-start.36 = (bf16[2,96,768]{2,1,0:T(8,128)(2,1)}, bf16[2,96,768]{2,1,0:T(8,128)(2,1)S(1)}, u32[]{:S(2)}, u32[]{:S(2)}) collective-permute-start(bf16[2,96,768]{2,1,0:T(8,128)(2,1)} %get-tuple-element.186), channel_id=1, source_target_pairs={{0,16},{3,19},{4,20},{7,23},{8,24},{11,27},{12,28},{15,31},{16,0},... | collective-permute-start | bytes 884744 | tf_op jit(solution)/shard_map/ppermute | solution.py:650
  292.1 42.5 %collective-permute-start.37 = (bf16[4,8,96,768]{3,2,1,0:T(8,128)(2,1)}, bf16[4,8,96,768]{3,2,1,0:T(8,128)(2,1)}, u32[]{:S(2)}, u32[]{:S(2)}) collective-permute-start(bf16[4,8,96,768]{3,2,1,0:T(8,128)(2,1)} %get-tuple-element.193), channel_id=1, source_target_pairs={{1,5},{2,6},{5,1},{6,2},{9,13},{10,14},{13,9},{14,10},{17,21},{18,... | collective-permute-start | bytes 14155784 | tf_op jit(solution)/shard_map/ppermute | solution.py:650
  297.6 37.0 %collective-permute-start.40 = (bf16[8,96,768]{2,1,0:T(8,128)(2,1)}, bf16[8,96,768]{2,1,0:T(8,128)(2,1)S(1)}, u32[]{:S(2)}, u32[]{:S(2)}) collective-permute-start(bf16[8,96,768]{2,1,0:T(8,128)(2,1)} %add_convert_fusion.3), channel_id=1, source_target_pairs={{0,1},{3,2},{4,5},{7,6},{8,9},{11,10},{12,13},{15,14},{16,17},{19,... | collective-permute-start | bytes 3538952 | tf_op jit(solution)/shard_map/ppermute | solution.py:654
  302.1 32.5 %collective-permute-start.38 = (bf16[4,96,768]{2,1,0:T(8,128)(2,1)}, bf16[4,96,768]{2,1,0:T(8,128)(2,1)S(1)}, u32[]{:S(2)}, u32[]{:S(2)}) collective-permute-start(bf16[4,96,768]{2,1,0:T(8,128)(2,1)} %get-tuple-element.197), channel_id=1, source_target_pairs={{0,8},{3,11},{4,12},{7,15},{8,0},{11,3},{12,4},{15,7},{16,24},{19,... | collective-permute-start | bytes 1769480 | tf_op jit(solution)/shard_map/ppermute | solution.py:650
  305.5 29.1 %collective-permute-start.39 = (bf16[4,96,768]{2,1,0:T(8,128)(2,1)}, bf16[4,96,768]{2,1,0:T(8,128)(2,1)S(1)}, u32[]{:S(2)}, u32[]{:S(2)}) collective-permute-start(bf16[4,96,768]{2,1,0:T(8,128)(2,1)} %get-tuple-element.198), channel_id=1, source_target_pairs={{0,16},{3,19},{4,20},{7,23},{8,24},{11,27},{12,28},{15,31},{16,0},... | collective-permute-start | bytes 1769480 | tf_op jit(solution)/shard_map/ppermute | solution.py:650
  336.0 24.9 %collective-permute-start.48 = (bf16[4,4,96,768]{3,2,1,0:T(8,128)(2,1)}, bf16[4,4,96,768]{3,2,1,0:T(8,128)(2,1)S(1)}, u32[]{:S(2)}, u32[]{:S(2)}) collective-permute-start(bf16[4,4,96,768]{3,2,1,0:T(8,128)(2,1)} %get-tuple-element.227), channel_id=1, source_target_pairs={{0,4},{1,5},{2,6},{3,7},{4,0},{5,1},{6,2},{7,3},{8,12},{9,13},{10,... | collective-permute-start | bytes 7077896 | tf_op jit(solution)/shard_map/ppermute | solution.py:650
  359.4 43.0 %collective-permute-start.63 = (bf16[4,96,768]{2,1,0:T(8,128)(2,1)}, bf16[4,96,768]{2,1,0:T(8,128)(2,1)}, u32[]{:S(2)}, u32[]{:S(2)}) collective-permute-start(bf16[4,96,768]{2,1,0:T(8,128)(2,1)} %collective-permute-done.62), channel_id=1, source_target_pairs={{1,2},{2,1},{5,6},{6,5},{9,10},{10,9},{13,14},{14,13},{17,18},{18,... | collective-permute-start | bytes 1769480 | tf_op jit(solution)/shard_map/ppermute | solution.py:654
  364.4 29.8 %collective-permute-start.49 = (bf16[2,96,768]{2,1,0:T(8,128)(2,1)}, bf16[2,96,768]{2,1,0:T(8,128)(2,1)S(1)}, u32[]{:S(2)}, u32[]{:S(2)}) collective-permute-start(bf16[2,96,768]{2,1,0:T(8,128)(2,1)} %get-tuple-element.229), channel_id=1, source_target_pairs={{0,8},{1,9},{2,10},{3,11},{4,12},{5,13},{6,14},{7,15},{8,0},{9,1},... | collective-permute-start | bytes 884744 | tf_op jit(solution)/shard_map/ppermute | solution.py:650
  390.7 47.5 %collective-permute-start.55 = (bf16[8,96,768]{2,1,0:T(8,128)(2,1)}, bf16[8,96,768]{2,1,0:T(8,128)(2,1)}, u32[]{:S(2)}, u32[]{:S(2)}) collective-permute-start(bf16[8,96,768]{2,1,0:T(8,128)(2,1)} %get-tuple-element.237), channel_id=1, source_target_pairs={{1,9},{2,10},{5,13},{6,14},{9,1},{10,2},{13,5},{14,6},{17,25},{18,... | collective-permute-start | bytes 3538952 | tf_op jit(solution)/shard_map/ppermute | solution.py:650
  392.3 47.3 %collective-permute-start.56 = (bf16[8,96,768]{2,1,0:T(8,128)(2,1)}, bf16[8,96,768]{2,1,0:T(8,128)(2,1)}, u32[]{:S(2)}, u32[]{:S(2)}) collective-permute-start(bf16[8,96,768]{2,1,0:T(8,128)(2,1)} %get-tuple-element.238), channel_id=1, source_target_pairs={{1,17},{2,18},{5,21},{6,22},{9,25},{10,26},{13,29},{14,30},{17,1},... | collective-permute-start | bytes 3538952 | tf_op jit(solution)/shard_map/ppermute | solution.py:650
  396.0 47.6 %collective-permute-start.65 = (bf16[8,96,768]{2,1,0:T(8,128)(2,1)S(1)}, bf16[8,96,768]{2,1,0:T(8,128)(2,1)}, u32[]{:S(2)}, u32[]{:S(2)}) collective-permute-start(bf16[8,96,768]{2,1,0:T(8,128)(2,1)S(1)} %copy-done.20), channel_id=1, source_target_pairs={{1,2},{2,1},{5,6},{6,5},{9,10},{10,9},{13,14},{14,13},{17,18},{18,... | collective-permute-start | bytes 3538952 | tf_op jit(solution)/shard_map/ppermute | solution.py:654
  406.5 41.9 %all-to-all-start.1 = ((bf16[512,4,192]{0,2,1:T(8,128)(2,1)}), bf16[512,4,192]{0,2,1:T(8,128)(2,1)S(1)}, u32[]{:S(2)}, u32[]{:S(2)}) async-start(bf16[512,4,192]{0,2,1:T(8,128)(2,1)} %bitcast.17), calls=%async_computation.1 | async-start | bytes 1572864 | tf_op jit(solution)/shard_map/all_to_all | solution.py:856
  414.8 70.8 %collective-permute-start.64 = (bf16[4,96,768]{2,1,0:T(8,128)(2,1)}, bf16[4,96,768]{2,1,0:T(8,128)(2,1)}, u32[]{:S(2)}, u32[]{:S(2)}) collective-permute-start(bf16[4,96,768]{2,1,0:T(8,128)(2,1)} %add_convert_fusion.4), channel_id=1, source_target_pairs={{1,0},{2,3},{5,4},{6,7},{9,8},{10,11},{13,12},{14,15},{17,16},{18,... | collective-permute-start | bytes 1769480 | tf_op jit(solution)/shard_map/ppermute | solution.py:654
  418.6 28.3 %collective-permute-start.59 = (bf16[4,96,768]{2,1,0:T(8,128)(2,1)}, bf16[4,96,768]{2,1,0:T(8,128)(2,1)}, u32[]{:S(2)}, u32[]{:S(2)}) collective-permute-start(bf16[4,96,768]{2,1,0:T(8,128)(2,1)} %add_convert_fusion.8), channel_id=1, source_target_pairs={{0,1},{3,2},{4,5},{7,6},{8,9},{11,10},{12,13},{15,14},{16,17},{19,... | collective-permute-start | bytes 1769480 | tf_op jit(solution)/shard_map/ppermute | solution.py:654
  445.2 66.6 %collective-permute-start.66 = (bf16[8,96,768]{2,1,0:T(8,128)(2,1)S(1)}, bf16[8,96,768]{2,1,0:T(8,128)(2,1)}, u32[]{:S(2)}, u32[]{:S(2)}) collective-permute-start(bf16[8,96,768]{2,1,0:T(8,128)(2,1)S(1)} %add_convert_fusion), channel_id=1, source_target_pairs={{1,0},{2,3},{5,4},{6,7},{9,8},{10,11},{13,12},{14,15},{17,16},{18,... | collective-permute-start | bytes 3538952 | tf_op jit(solution)/shard_map/ppermute | solution.py:654
  449.8 34.7 %collective-permute-start.54 = (bf16[4,96,768]{2,1,0:T(8,128)(2,1)S(1)}, bf16[4,96,768]{2,1,0:T(8,128)(2,1)S(1)}, u32[]{:S(2)}, u32[]{:S(2)}) collective-permute-start(bf16[4,96,768]{2,1,0:T(8,128)(2,1)S(1)} %add_convert_fusion.7), channel_id=1, source_target_pairs={{1,0},{2,3},{5,4},{6,7},{9,8},{10,11},{13,12},{14,15},{17,16},{18,... | collective-permute-start | bytes 1769480 | tf_op jit(solution)/shard_map/ppermute | solution.py:654
  453.5 55.0 %collective-permute-start.61 = (bf16[4,96,768]{2,1,0:T(8,128)(2,1)S(1)}, bf16[4,96,768]{2,1,0:T(8,128)(2,1)S(1)}, u32[]{:S(2)}, u32[]{:S(2)}) collective-permute-start(bf16[4,96,768]{2,1,0:T(8,128)(2,1)S(1)} %add_convert_fusion.6), channel_id=1, source_target_pairs={{1,0},{2,3},{5,4},{6,7},{9,8},{10,11},{13,12},{14,15},{17,16},{18,... | collective-permute-start | bytes 1769480 | tf_op jit(solution)/shard_map/ppermute | solution.py:654
  456.4 73.8 %collective-permute-start.58 = (bf16[8,96,768]{2,1,0:T(8,128)(2,1)S(1)}, bf16[8,96,768]{2,1,0:T(8,128)(2,1)S(1)}, u32[]{:S(2)}, u32[]{:S(2)}) collective-permute-start(bf16[8,96,768]{2,1,0:T(8,128)(2,1)S(1)} %add_convert_fusion.1), channel_id=1, source_target_pairs={{1,0},{2,3},{5,4},{6,7},{9,8},{10,11},{13,12},{14,15},{17,16},{18,... | collective-permute-start | bytes 3538952 | tf_op jit(solution)/shard_map/ppermute | solution.py:654
  (108 other events, 935.4 us)

commit v3 on v2

--- a/solution.py
+++ b/solution.py
@@ -19,6 +19,7 @@
 TILE = 128
 BLOCKS = LEN // TILE
 ROWS8 = D // 8
+EXTRA = 16
 
 EPSILON = 1e-06
 MASKED = -1000000000.0
@@ -62,6 +63,18 @@
     return np.stack(tiles).astype(np.int32), far.astype(np.int32)
 
 
+def sum_ids(both_ways):
+    p = np.arange(2 * TILE)
+    parts = []
+    for step in (0, 1, -1):
+        n = TILE - 1 - p + step * TILE
+        ids = bucket_of(n, both_ways)
+        parts.append(np.where((p == 2 * TILE - 1) | ((n < 0) & (not both_ways)), TILE, ids))
+    far = tile_ids(both_ways)[1]
+    parts += [np.full(TILE, b if b < BUCKETS else TILE) for b in far]
+    return np.concatenate(parts).astype(np.int32)
+
+
 def dot(a, b):
     return jnp.dot(a, b, preferred_element_type=f32)
 
@@ -109,6 +122,18 @@
     return copies
 
 
+def only(role, kernel):
+    if role is None:
+        return kernel
+
+    def guarded(me_ref, *refs):
+        @pl.when(me_ref[1] == role)
+        def _():
+            kernel(me_ref, *refs)
+
+    return guarded
+
+
 def start_all(copies):
     for copy in copies:
         copy.start()
@@ -130,8 +155,9 @@
         even_rows = value[2 * i * ROWS8 : (2 * i + 1) * ROWS8]
         odd_rows = value[(2 * i + 1) * ROWS8 : (2 * i + 2) * ROWS8]
         slot = i ^ (me // 2)
-        keep[slot, unit] = jnp.where(odd, odd_rows, even_rows)
-        send[slot, unit] = jnp.where(odd, even_rows, odd_rows)
+        rows = slice(unit * ROWS8, (unit + 1) * ROWS8) if isinstance(unit, int) else unit
+        keep[slot, rows, :] = jnp.where(odd, odd_rows, even_rows)
+        send[slot, rows, :] = jnp.where(odd, even_rows, odd_rows)
 
 
 def attn_fwd_kernel(has_bias, nparts, *refs):
@@ -231,7 +257,10 @@
     args += parts
     specs += [HBM] * len(parts)
     return pl.pallas_call(
-        functools.partial(attn_fwd_kernel, has_bias, len(parts)),
+        only(
+            None if has_bias else 0,
+            functools.partial(attn_fwd_kernel, has_bias, len(parts)),
+        ),
         out_shape=(FULL_ROWS, LOW_ROWS)
         + (HEAD_ROWS,) * 4
         + (jax.ShapeDtypeStruct((HEADS, LEN, LEN), bf16),),
@@ -252,20 +281,21 @@
     refs = refs[4:]
     gother = ksrc = None
     if has_bias:
-        gother = refs.pop(0)
+        gother, gains, hot = refs[:3]
+        refs = refs[3:]
     else:
         ksrc = refs.pop(0)
     q_i, k_i, v_i, o_i, p_i = refs[:5]
     refs = refs[5:]
     parts = refs[:nparts]
     refs = refs[nparts:]
-    din, keep, send, dgain = refs[:4]
-    refs = refs[4:]
+    din, keep, send = refs[:3]
+    refs = refs[3:]
     if has_bias:
-        dtile, dfar = refs[:2]
+        vec_s = refs.pop()
+    else:
+        dgain, dkey = refs[:2]
         refs = refs[2:]
-    else:
-        dkey = refs.pop(0)
     w_s, p_s, do_s, dq_s, dk_s, dv_s, ds_s, keep_s, send_s, w_sem, p_sem, out_sem = refs
     me = me_ref[0]
 
@@ -287,6 +317,11 @@
     do = dot_nt(g, matrix(w_s, 3)).astype(bf16)
     for p in range(PAIRS):
         do_s[p] = do[:, p * TILE : (p + 1) * TILE]
+
+    if has_bias:
+        down = lax.broadcasted_iota(jnp.int32, (TILE, TILE), 0)
+        along = lax.broadcasted_iota(jnp.int32, (TILE, TILE), 1)
+        mirror = (down + along == TILE - 1).astype(bf16)
 
     def pair(p, carry):
         qp, kp, vp, dop = q_i[p], k_i[p], v_i[p], do_s[p]
@@ -313,10 +348,21 @@
                 dq = dot(low, kz)
                 total[bi] = dq if total[bi] is None else total[bi] + dq
             if has_bias:
-                for step in (0, 1, -1):
-                    dtile[h, tile_of(step)] = diag[step].astype(bf16)
-                for n, step in ((0, 2), (1, -2)):
-                    dfar[h, n : n + 1, :] = jnp.sum(diag[step], axis=0, keepdims=True)
+                near = jnp.concatenate([diag[step] for step in (0, 1, -1)], axis=1)
+                near = dot(mirror, near.astype(bf16))
+                nothing = jnp.zeros((TILE, TILE), f32)
+                for t in range(3):
+                    part = near[:, t * TILE : (t + 1) * TILE]
+                    part = pltpu.roll(
+                        jnp.concatenate([part, nothing], axis=1), 0, 1, stride=1, stride_axis=0
+                    )
+                    vec_s[h, :, 2 * t * TILE : 2 * (t + 1) * TILE] = jnp.sum(
+                        part, axis=0, keepdims=True
+                    )
+                for n, step in ((6, 2), (7, -2)):
+                    vec_s[h, :, n * TILE : (n + 1) * TILE] = jnp.sum(
+                        diag[step], axis=0, keepdims=True
+                    )
             half = slice(which * HEAD, (which + 1) * HEAD)
             dk_s[p, half, :] = dot(q_t[half], ds_s[which]).astype(bf16)
             dv_s[p, half, :] = dot(do_t[half], p_s[h]).astype(bf16)
@@ -331,6 +377,24 @@
     dq = jnp.concatenate([dq_s[p] for p in range(PAIRS)], axis=1)
     dk_t = dk_s[...].reshape(D, LEN)
     dv_t = dv_s[...].reshape(D, LEN)
+    wait_all(rest_load)
+    query_side = dot_nt(dq, matrix(w_s, 0))
+    key_side = dot_nt(dk_t.T, matrix(w_s, 1)) + dot_nt(dv_t.T, matrix(w_s, 2))
+    if has_bias:
+        query_side = query_side + key_side
+    else:
+        dkey[...] = key_side.astype(bf16)
+    dv, dg = rms_back(v, gain[...], query_side)
+    din[...] = (base + dv).astype(din.dtype)
+    if has_bias:
+        table = dot(vec_s[...].reshape(HEADS, 8 * TILE).astype(bf16), hot[...])
+        table = jnp.concatenate([table, jnp.zeros((HEADS, D - TILE), f32)], axis=1)
+        rows = jnp.concatenate([table, dg, gains[...], jnp.zeros((1, D), f32)], axis=0)
+        for slot in range(4):
+            keep_s[slot, D // 2 :, :] = rows.astype(bf16)
+            send_s[slot, D // 2 :, :] = rows.astype(bf16)
+    else:
+        dgain[...] = dg
     put_blocks(me, dot(a_t, dq), 0, keep_s, send_s)
     put_blocks(me, dot_nt(b_t, dk_t), 1, keep_s, send_s)
     put_blocks(me, dot_nt(b_t, dv_t), 2, keep_s, send_s)
@@ -341,37 +405,24 @@
         pltpu.make_async_copy(keep_s, keep, out_sem.at[1]),
     ]
     start_all(outs)
-    wait_all(rest_load)
-    query_side = dot_nt(dq, matrix(w_s, 0))
-    key_side = dot_nt(dk_t.T, matrix(w_s, 1)) + dot_nt(dv_t.T, matrix(w_s, 2))
-    if has_bias:
-        query_side = query_side + key_side
-    else:
-        dkey[...] = key_side.astype(bf16)
-    dv, dg = rms_back(v, gain[...], query_side)
-    dgain[...] = dg
-    din[...] = (base + dv).astype(din.dtype)
     wait_all(outs)
 
 
-BLOCKS4 = jax.ShapeDtypeStruct((4, 4, ROWS8, D), bf16)
-BLOCKS8 = jax.ShapeDtypeStruct((4, 8, ROWS8, D), bf16)
-
-
-def attn_bwd(me, gres, src, gain, parts, saved, ksrc=None, gother=None):
+BLOCKS8 = jax.ShapeDtypeStruct((4, D, D), bf16)
+
+
+def attn_bwd(me, gres, src, gain, parts, saved, ksrc=None, others=()):
     has_bias = ksrc is None
-    args = [me, gres, src, gain, gother if has_bias else ksrc, *saved, *parts]
-    specs = [SM] + [VM] * 8 + [HBM] + [HBM] * len(parts)
-    outs = [LOW_ROWS if has_bias else FULL_ROWS, BLOCKS4, BLOCKS4, ONE_ROW]
-    if has_bias:
-        outs += [
-            jax.ShapeDtypeStruct((HEADS, 3, TILE, TILE), bf16),
-            jax.ShapeDtypeStruct((HEADS, 2, TILE), f32),
-        ]
-    else:
-        outs += [LOW_ROWS]
+    args = [me, gres, src, gain] + (list(others) if has_bias else [ksrc]) + [*saved, *parts]
+    specs = [SM] + [VM] * (len(args) - 2 - len(parts)) + [HBM] * (1 + len(parts))
+    rows = D // 2 + (EXTRA if has_bias else 0)
+    pack = jax.ShapeDtypeStruct((4, rows, D), bf16)
+    outs = [LOW_ROWS, pack, pack] if has_bias else [FULL_ROWS, pack, pack, ONE_ROW, LOW_ROWS]
     return pl.pallas_call(
-        functools.partial(attn_bwd_kernel, has_bias, len(parts)),
+        only(
+            None if has_bias else 0,
+            functools.partial(attn_bwd_kernel, has_bias, len(parts)),
+        ),
         out_shape=tuple(outs),
         in_specs=specs,
         out_specs=tuple([VM, HBM, HBM] + [VM] * (len(outs) - 3)),
@@ -383,12 +434,13 @@
             pltpu.VMEM((PAIRS, TILE, LEN), bf16),
             pltpu.VMEM((PAIRS, TILE, LEN), bf16),
             pltpu.VMEM((2, LEN, LEN), bf16),
-            pltpu.VMEM((4, 4, ROWS8, D), bf16),
-            pltpu.VMEM((4, 4, ROWS8, D), bf16),
+            pltpu.VMEM((4, rows, D), bf16),
+            pltpu.VMEM((4, rows, D), bf16),
             pltpu.SemaphoreType.DMA((2,)),
             pltpu.SemaphoreType.DMA((PAIRS,)),
             pltpu.SemaphoreType.DMA((2,)),
-        ],
+        ]
+        + ([pltpu.VMEM((HEADS, 1, 8 * TILE), f32)] if has_bias else []),
         compiler_params=PARAMS,
         name="self_bwd" if has_bias else "cross_bwd",
     )(*args)
@@ -500,23 +552,26 @@
     if bwd:
         du = (slope * dot_nt(g[...], wo)).astype(bf16)
         dn[...] += dot_nt(du, wi)
-        put_blocks(me, dot(nt_s[...], du), step, keep_s, send_s)
+        in_rows = pl.ds(pl.multiple_of(step * ROWS8, 32), ROWS8)
+        put_blocks(me, dot(nt_s[...], du), in_rows, keep_s, send_s)
         dwo = dot(h.T, g[...]).astype(bf16)
         odd = (me % 2) == 1
         slot = step ^ (me // 2)
         for k in range(4):
             first, second = dwo[k * ROWS8 : (k + 1) * ROWS8], dwo[(4 + k) * ROWS8 : (5 + k) * ROWS8]
-            keep_s[slot, 4 + k] = jnp.where(odd, second, first)
-            send_s[slot, 4 + k] = jnp.where(odd, first, second)
+            rows = slice((4 + k) * ROWS8, (5 + k) * ROWS8)
+            keep_s[slot, rows, :] = jnp.where(odd, second, first)
+            send_s[slot, rows, :] = jnp.where(odd, first, second)
 
         def outs(c):
             slot = c ^ (me // 2)
             copies = []
             for n, (here, there) in enumerate(((send_s, send), (keep_s, keep))):
+                part = pl.ds(pl.multiple_of(c * ROWS8, 32), ROWS8)
                 copies.append(
-                    pltpu.make_async_copy(here.at[:, c], there.at[:, c], out_sem.at[2 * n])
+                    pltpu.make_async_copy(here.at[:, part], there.at[:, part], out_sem.at[2 * n])
                 )
-                last = pl.ds(4, 4)
+                last = pl.ds(D // 2, D // 2)
                 copies.append(
                     pltpu.make_async_copy(here.at[slot, last], there.at[slot, last], out_sem.at[2 * n + 1])
                 )
@@ -567,12 +622,12 @@
         scratch += [
             pltpu.VMEM((D, LEN), bf16),
             pltpu.VMEM((LEN, D), f32),
-            pltpu.VMEM((4, 8, ROWS8, D), bf16),
-            pltpu.VMEM((4, 8, ROWS8, D), bf16),
+            pltpu.VMEM((4, D, D), bf16),
+            pltpu.VMEM((4, D, D), bf16),
             pltpu.SemaphoreType.DMA((4,)),
         ]
     return pl.pallas_call(
-        functools.partial(ffn_kernel, mode, len(parts)),
+        only(0 if mode == "both" else 1, functools.partial(ffn_kernel, mode, len(parts))),
         grid=(4,),
         out_shape=tuple(shapes),
         in_specs=specs,
@@ -590,53 +645,78 @@
     return total.astype(bf16)
 
 
-def diag_kernel(keep, recv, by_x, by_y):
+def diag_kernel(me_ref, keep, recv, by_x, by_y, keep_s, recv_s, sem):
     half = by_x.shape[0]
-    total = wide_add(keep[0], recv[0])
-    by_x[...] = total[:half]
-    by_y[...] = total[half:]
-
-
-def diag_add(keep, recv):
-    _, k, r, c = keep.shape
-    last = pl.BlockSpec((1, k, r, c), lambda i: (3, 0, 0, 0))
-    half = pl.BlockSpec((k // 2, r, c), lambda i: (0, 0, 0))
-    shape = jax.ShapeDtypeStruct((k // 2, r, c), bf16)
+    loads = [
+        pltpu.make_async_copy(keep.at[3], keep_s, sem.at[0]),
+        pltpu.make_async_copy(recv.at[3], recv_s, sem.at[1]),
+    ]
+    start_all(loads)
+    wait_all(loads)
+    keep_s[...] = wide_add(keep_s[...], recv_s[...])
+    stores = [
+        pltpu.make_async_copy(keep_s.at[:half], by_x, sem.at[0]),
+        pltpu.make_async_copy(keep_s.at[half:], by_y, sem.at[1]),
+    ]
+    start_all(stores)
+    wait_all(stores)
+
+
+def diag_add(role, me, keep, recv):
+    _, r, c = keep.shape
+    half = r // 32 * 16
     return pl.pallas_call(
-        diag_kernel,
-        grid=(1,),
-        out_shape=(shape, shape),
-        in_specs=[last, last],
-        out_specs=(half, half),
+        only(role, diag_kernel),
+        out_shape=tuple(jax.ShapeDtypeStruct((n, c), bf16) for n in (half, r - half)),
+        in_specs=[SM, HBM, HBM],
+        out_specs=(HBM, HBM),
+        scratch_shapes=[pltpu.VMEM((r, c), bf16)] * 2 + [pltpu.SemaphoreType.DMA((2,))],
         compiler_params=PARAMS,
         name="diag_add",
-    )(keep, recv)
-
-
-def rest_kernel(keep, recv, from_x, from_y, own, for_x, for_y):
+    )(me, keep, recv)
+
+
+def rest_kernel(
+    me_ref, keep, recv, from_x, from_y, own, for_x, for_y, keep_s, recv_s, x_s, y_s, sem
+):
     half = from_x.shape[0]
-    own[...] = wide_add(keep[0], recv[0])
-    for_x[:half] = wide_add(keep[1, :half], recv[1, :half])
-    for_x[half:] = wide_add(keep[1, half:], recv[1, half:], from_y[...])
-    for_y[:half] = wide_add(keep[2, :half], recv[2, :half], from_x[...])
-    for_y[half:] = wide_add(keep[2, half:], recv[2, half:])
-
-
-def rest_add(keep, recv, from_x, from_y):
-    _, k, r, c = keep.shape
-    first = pl.BlockSpec((3, k, r, c // 2), lambda i: (0, 0, 0, i))
-    half = pl.BlockSpec((k // 2, r, c // 2), lambda i: (0, 0, i))
-    full = pl.BlockSpec((k, r, c // 2), lambda i: (0, 0, i))
-    shape = jax.ShapeDtypeStruct((k, r, c), bf16)
+    loads = []
+    for slot in range(3):
+        loads.append(pltpu.make_async_copy(keep.at[slot], keep_s.at[slot], sem.at[2 * slot]))
+        loads.append(pltpu.make_async_copy(recv.at[slot], recv_s.at[slot], sem.at[2 * slot + 1]))
+    loads.append(pltpu.make_async_copy(from_x, x_s, sem.at[6]))
+    loads.append(pltpu.make_async_copy(from_y, y_s, sem.at[7]))
+    start_all(loads[2:4] + loads[6:] + loads[4:6] + loads[:2])
+    stores = []
+    for slot, out in ((1, for_x), (2, for_y), (0, own)):
+        wait_all(loads[2 * slot : 2 * slot + 2])
+        if slot == 1:
+            wait_all(loads[6:])
+            top, low = (), (y_s[...],)
+        else:
+            top, low = ((x_s[...],), ()) if slot == 2 else ((), ())
+        keep_s[slot, :half] = wide_add(keep_s[slot, :half], recv_s[slot, :half], *top)
+        keep_s[slot, half:] = wide_add(keep_s[slot, half:], recv_s[slot, half:], *low)
+        stores.append(pltpu.make_async_copy(keep_s.at[slot], out, sem.at[8 + slot]))
+        stores[-1].start()
+    wait_all(stores)
+
+
+def rest_add(role, me, keep, recv, from_x, from_y):
+    _, r, c = keep.shape
+    half = r // 32 * 16
+    shape = jax.ShapeDtypeStruct((r, c), bf16)
     return pl.pallas_call(
-        rest_kernel,
-        grid=(2,),
+        only(role, rest_kernel),
         out_shape=(shape,) * 3,
-        in_specs=[first, first, half, half],
-        out_specs=(full,) * 3,
+        in_specs=[SM] + [HBM] * 4,
+        out_specs=(HBM,) * 3,
+        scratch_shapes=[pltpu.VMEM((3, r, c), bf16)] * 2
+        + [pltpu.VMEM((half, c), bf16), pltpu.VMEM((r - half, c), bf16)]
+        + [pltpu.SemaphoreType.DMA((11,))],
         compiler_params=PARAMS,
         name="rest_add",
-    )(keep, recv, from_x, from_y)
+    )(me, keep, recv, from_x, from_y)
 
 
 ALL = (0, 1, 2, 3)
@@ -690,34 +770,40 @@
 
 
 def whole_scatter(keep, send):
-    k = keep.shape[1]
-    blocks = jnp.stack([keep, send], axis=1).reshape(8, k, ROWS8, D)
-    inner = jnp.transpose(blocks[:, :4], (1, 0, 2, 3)).reshape(4, D, D)
-    inner = lax.psum_scatter(inner, "wide", scatter_dimension=1, tiled=True)
-    if k == 4:
-        return inner
-    outer = lax.psum_scatter(blocks[:, 4:].reshape(FF, D), "wide", scatter_dimension=0, tiled=True)
-    return jnp.concatenate([inner, outer.reshape(inner.shape)])
+    blocks = jnp.stack([keep, send], axis=1).reshape(8, -1, D)
+    k = blocks.shape[1] // ROWS8
+    weights = blocks[:, : k * ROWS8].reshape(8, k, ROWS8, D)
+    inner = jnp.transpose(weights[:, :4], (1, 0, 2, 3)).reshape(4, D, D)
+    inner = lax.psum_scatter(inner, "wide", scatter_dimension=1, tiled=True).reshape(-1, D)
+    if k == 8:
+        last = weights[:, 4:].reshape(FF, D)
+        last = lax.psum_scatter(last, "wide", scatter_dimension=0, tiled=True)
+    else:
+        last = lax.psum(blocks[0, k * ROWS8 :], "wide")
+    return jnp.concatenate([inner, last])
 
 
 class Scatter:
-    def __init__(self, keep, send, planes=ALL):
-        self.keep, self.planes = keep, planes
+    def __init__(self, me, keep, send, planes):
+        self.me, self.keep, self.planes = me, keep, planes
+        self.role = {ENC: 1, DEC: 0, ALL: None}[planes]
         self.small = lax.axis_size("wide") == 8
         self.state = (send,)
         if self.small:
             self.state = (across(send, 1, planes),)
-        self.phase = 0
+        self.phase, self.token = 0, keep
 
     def go(self):
         if not self.small:
             return self
         if self.phase == 0:
             (self.recv,) = self.state
-            by_x, by_y = diag_add(self.keep, self.recv)
+            by_x, by_y = diag_add(self.role, self.me, self.keep, self.recv)
+            self.token = by_x
             self.state = across(by_x, 2, self.planes), across(by_y, 4, self.planes)
         elif self.phase == 1:
-            own, for_x, for_y = rest_add(self.keep, self.recv, *self.state)
+            own, for_x, for_y = rest_add(self.role, self.me, self.keep, self.recv, *self.state)
+            self.token = own
             self.state = own, across(for_x, 2, self.planes), across(for_y, 4, self.planes)
         self.phase += 1
         return self
@@ -736,19 +822,35 @@
     return flat
 
 
-def over_planes(share, middle):
-    total = wide_add(share, between(share, [(1, 2), (2, 1)]))
-    return jnp.where(middle, total, between(total, [(1, 0), (2, 3)]))
-
-
-def summed(x):
-    if lax.axis_size("wide") != 8:
-        return lax.psum(x, ("wide", "narrow"))
-    for flip in (1, 2, 4):
-        x = x + across(x, flip, ALL)
-    for flip in (1, 2):
-        x = x + between(x, [(n, n ^ flip) for n in range(4)])
-    return x
+class FromMiddle:
+    def __init__(self, share, middle):
+        self.share, self.middle = share, middle
+        self.state = (between(share, [(1, 2), (2, 1)]),)
+
+    def go(self):
+        self.total = wide_add(self.share, *self.state)
+        self.state = (between(self.total, [(1, 0), (2, 3)]),)
+        return self
+
+    def result(self):
+        return jnp.where(self.middle, self.total, *self.state).astype(f32)
+
+
+class FromEnds:
+    def __init__(self, share, middle):
+        self.share, self.middle = share, middle
+        self.got, self.state = [], (between(share, [(0, 1), (3, 2)]),)
+
+    def go(self):
+        self.got.append(self.state[0])
+        pairs = [(1, 2), (2, 1)] if len(self.got) == 1 else [(1, 0), (2, 3)]
+        self.state = (between(self.state[0], pairs),)
+        return self
+
+    def result(self):
+        near, far = self.got
+        first = jnp.where(self.middle, near, self.share).astype(f32)
+        return first + jnp.where(self.middle, far, *self.state).astype(f32)
 
 
 def on_device(
@@ -813,6 +915,7 @@
         [in_units(pick(enc_ffn_in, dec_ffn_in)), out_units(pick(enc_ffn_out, dec_ffn_out))]
     )
     pack_c = jnp.stack([cross_query, cross_key, cross_value, cross_output])
+    shard_rows = enc_query.shape[0]
     small = lax.axis_size("wide") == 8
     if small:
         near_a = gather_near(pack_a)
@@ -827,6 +930,9 @@
     table = jnp.concatenate([pick(enc_table, dec_table), jnp.full((1, HEADS), MASKED, bf16)])
     bias = jnp.einsum("bh,bsij->hsij", table, hot, preferred_element_type=f32)
     far = jnp.einsum("bh,bs->hs", table, far_hot, preferred_element_type=f32)
+    enc_sums, dec_sums = sum_ids(True), sum_ids(False)
+    sums_of = pick(jnp.asarray(enc_sums), jnp.asarray(dec_sums))
+    sum_hot = (sums_of[:, None] == jnp.arange(TILE, dtype=jnp.int32)).astype(bf16)
 
     gain_a = pick(gain_of(enc_attn_gain), gain_of(dec_self_gain))
     enc_gain = gain_of(enc_ffn_gain)
@@ -860,75 +966,73 @@
         return jnp.concatenate([rows[1], rows[2]]), jnp.concatenate([rows[0], rows[3]])
 
     dec_out, gz2, dgain_df, *blocks = ffn("both", me, z2, gain_of(dec_ffn_gain), w_ffn, cot)
-    sum_df = Scatter(*blocks, DEC)
+    sum_df = Scatter(me, *blocks, DEC)
     out_cols = by_columns(pick(enc_out, dec_out))
-    gz1, *blocks, dgain_c, genc_out = attn_bwd(me, gz2, z1, gain_c, w_cross, saved_c, ksrc=memory)
+    gz1, *blocks, dgain_c, genc_out = attn_bwd(
+        me, gz2, z1, gain_c, w_cross, saved_c, ksrc=memory
+    )
     genc_out, gz1, out_cols, *blocks = tie_all([sum_df], genc_out, gz1, out_cols, *blocks)
     genc = between(genc_out, [(0, 1), (3, 2)])
-    sum_c = Scatter(*blocks, DEC)
+    sum_c = Scatter(me, *blocks, DEC)
     sum_df.go()
-    (genc,) = tie_all([sum_df, sum_c], genc)
+    (gz1,) = tie_all([sum_df, sum_c], gz1)
     sum_df.go()
     sum_c.go()
     gx1, dgain_ef, *blocks = ffn("bwd", me, x1, enc_gain, w_ffn, genc, saved_f)
-    gx1, *blocks = tie_all([sum_df, sum_c], gx1, *blocks)
-    sum_ef = Scatter(*blocks, ENC)
-    s_df = sum_df.result()
-    part_df = between(s_df, [(0, 1), (3, 2)])
+    gx1, *blocks = tie_all([sum_c], gx1, *blocks)
+    sum_ef = Scatter(me, *blocks, ENC)
+    gains = jnp.concatenate([pick(dgain_ef, dgain_df), dgain_c])
+    din, *blocks = attn_bwd(
+        me, gz1, src, gain_a, w_attn, saved, others=(gx1, gains, sum_hot)
+    )
+    din, *blocks = tie_all([sum_ef, sum_c, sum_df], din, *blocks)
+    sum_a = Scatter(me, *blocks, ALL)
+    sum_ef.go()
+    tie_all([sum_df, sum_c], sum_ef.token)
+    all_df = FromEnds(sum_df.result(), is_enc)
+    tie_all([sum_c], all_df.share)
     sum_c.go()
-    din, *blocks, dgain_a, dtile, dfar = attn_bwd(
-        me, gz1, src, gain_a, w_attn, saved, gother=gx1
+    tie_all([sum_ef, sum_a], all_df.share)
+    sum_ef.go()
+    tie_all([sum_a], sum_ef.token)
+    sum_a.go()
+    tie_all([sum_c], sum_a.token)
+    all_c = FromEnds(sum_c.result(), is_enc)
+    tie_all([all_df], all_c.share)
+    all_df.go()
+    din, _ = tie(din, sum_a.token)
+    grad_cols = by_columns(din)
+    tie_all([sum_a, all_c])
+    sum_a.go()
+    all_c.go()
+    tie_all([sum_ef, all_df], sum_a.token)
+    all_ef = FromMiddle(sum_ef.result(), is_enc)
+    all_df.go()
+    tie_all([sum_a, all_c], all_ef.share)
+    s_a = sum_a.result()
+    all_e = FromMiddle(s_a, is_enc)
+    all_s = FromEnds(s_a, is_enc)
+    all_c.go()
+    tie_all([all_ef], s_a)
+    all_ef.go()
+    tie_all([all_e, all_s], all_ef.total)
+    all_e.go()
+    all_s.go()
+    tie_all([all_s], all_e.total)
+    all_s.go()
+
+    def split(f):
+        return f[: 4 * shard_rows].reshape(4, shard_rows, D), f[4 * shard_rows :]
+
+    g_df, g_c, g_s, g_ef, g_e = (
+        split(p.result()) for p in (all_df, all_c, all_s, all_ef, all_e)
     )
-    din, dgain_a, dtile, dfar, part_df, *blocks = tie_all(
-        [sum_ef, sum_c], din, dgain_a, dtile, dfar, part_df, *blocks
-    )
-    sum_a = Scatter(*blocks)
-    grad_cols = by_columns(din)
-    sum_ef.go()
-    s_c = sum_c.result()
-    part_c = between(s_c, [(0, 1), (3, 2)])
-    tie_all([sum_ef, sum_a])
-    sum_ef.go()
-    sum_a.go()
-    s_ef = sum_ef.result()
-    s_a = sum_a.go().result()
-    part_s = between(s_a, [(0, 1), (3, 2)])
-
-    def rows_of(f):
-        return jnp.transpose(f[:4], (1, 0, 2)).reshape(-1, FF), f[4:].reshape(-1, D)
-
-    g_df, g_c, g_s, g_ef, g_e = (
-        over_planes(s, is_enc).astype(f32) for s in (part_df, part_c, part_s, s_ef, s_a)
-    )
-    gi_d, go_d = rows_of(g_df)
-    gi_e, go_e = rows_of(g_ef)
-
-    dtable = jnp.einsum("hsij,bsij->bh", dtile, hot, preferred_element_type=f32)
-    dtable = dtable + jnp.einsum("hsj,bs->bh", dfar, far_hot.astype(f32))
-    dtable = jnp.pad(dtable[:BUCKETS].reshape(1, BUCKETS * HEADS), ((0, 0), (0, D - BUCKETS * HEADS)))
-    none = jnp.zeros((1, D), f32)
-
-    def when_enc(x):
-        return jnp.where(is_enc, x, 0.0)
-
-    def when_dec(x):
-        return jnp.where(is_enc, 0.0, x)
-
-    sums = jnp.concatenate(
-        [
-            when_enc(dgain_a),
-            when_enc(dgain_ef),
-            when_dec(dgain_a),
-            when_dec(dgain_c),
-            when_dec(dgain_df),
-            when_enc(dtable),
-            when_dec(dtable),
-            none,
-        ]
-    )
-    sums = summed(sums)
-    tables = sums[5:7, : BUCKETS * HEADS].reshape(2, BUCKETS, HEADS)
-
+    gi_e, gi_d = (jnp.transpose(g[0], (1, 0, 2)).reshape(-1, FF) for g in (g_ef, g_df))
+    go_e, go_d = g_ef[1], g_df[1]
+    more_e, more_s = g_e[1], g_s[1]
+    g_e, g_s, g_c = g_e[0], g_s[0], g_c[0]
+    tables = [jnp.transpose(m[:HEADS, :BUCKETS]) for m in (more_e, more_s)]
+    sums = [more_e[HEADS], more_e[HEADS + 1], more_s[HEADS], more_s[HEADS + 2], more_s[HEADS + 1]]
     enc_cols, dec_cols = rows_by_block(out_cols)
     enc_grad_cols, dec_grad_cols = rows_by_block(grad_cols)
     return (

time: 547 us -> 498 us (0.910)
  Pallas kernels: 177 us -> 156 us
  waiting for transfers between devices: 137 us -> 119 us
  other arithmetic: 32.1 us -> 25.7 us
    ppermute x17 -> x15, waiting for transfers between devices: 78.1 us -> 49.8 us  [between(): return lax.ppermute(x, 'narrow', pairs)]
    pallas_call x15, Pallas kernels: 177 us -> 156 us  [the longest x2 55.1 us: attn_bwd(): pl.pallas_call(only(None if has_bias else 0, functools.partial(attn_bwd_k...]
    ppermute x17 -> x15, starting transfers between devices: 50.7 us -> 62.7 us  [between(): return lax.ppermute(x, 'narrow', pairs)]
    all_to_all x2, starting transfers between devices: 18.7 us -> 8.58 us  [by_columns(): return lax.all_to_all(x, 'narrow', split_axis=1, concat_axis=0, tiled=True)]
    ppermute x50 -> x47, waiting for transfers between devices: 59.4 us -> 69.1 us  [across(): return lax.ppermute(x, ('wide', 'narrow'), pairs)]
    convert_element_type x9 -> x6, other arithmetic: 17.9 us -> 8.9 us  [wide_add(): return total.astype(bf16)]
    ppermute x50 -> x47, starting transfers between devices: 78.8 us -> 77.2 us  [across(): return lax.ppermute(x, ('wide', 'narrow'), pairs)]
    unnamed x144 -> x142, local copies, waits for them, and re-layouts: 12.7 us -> 13.7 us
  transfers between devices with their start and end apart: 69 -> 64, of which waited for: 23 -> 25; matrix products, arithmetic and copies ran while one was open for 10% -> 9% of each run, Pallas kernels for 23% -> 22%
where the time goes in v3:
time: 498 us; the launch traced here: 489 us
  Pallas kernels  156 us (31%)
  starting transfers between devices  149 us (30%)
  waiting for transfers between devices  119 us (24%)
  local copies, waits for them, and re-layouts  36.7 us (7%)
  other arithmetic  25.7 us (5%)
    ppermute x47, starting transfers between devices, across(): return lax.ppermute(x, ('wide', 'narrow'), pairs)  77.2 us
    ppermute x47, waiting for transfers between devices, across(): return lax.ppermute(x, ('wide', 'narrow'), pairs)  69.1 us
    ppermute x15, starting transfers between devices, between(): return lax.ppermute(x, 'narrow', pairs)  62.7 us
    pallas_call x2, Pallas kernels, attn_bwd(): pl.pallas_call(only(None if has_bias else 0, functools.partial(attn_bwd_k...  55.1 us
    ppermute x15, waiting for transfers between devices, between(): return lax.ppermute(x, 'narrow', pairs)  49.8 us
    pallas_call x2, Pallas kernels, attn_fwd(): pl.pallas_call(only(None if has_bias else 0, functools.partial(attn_fwd_k...  42.1 us
    pallas_call x3, Pallas kernels, ffn(): pl.pallas_call(only(0 if mode == 'both' else 1, functools.partial(ffn_ker...  34.2 us
    pallas_call x4, Pallas kernels, rest_add(): pl.pallas_call(only(role, rest_kernel), out_shape=(shape,) * 3, in_specs=...  14.3 us
  transfers between devices with their start and end apart: 64, of which 25 were waited for; matrix products, arithmetic and copies ran while one was open for 9% of the time, Pallas kernels for 22%

profile of v3, /device:TPU:0, one launch (start us, length us, event | category | flops | bytes accessed | tf_op | source)
XLA Modules:
  0.0 489.3 jit_solution(15371283763173320931)
XLA Ops:
  25.1 5.7 %collective-permute-done.3.refs_10_.refs_15_ = bf16[2,96,768]{2,1,0:T(8,128)(2,1)S(1)} collective-permute-done((bf16[2,96,768]{2,1,0:T(8,128)(2,1)S(1)}, bf16[2,96,768]{2,1,0:T(8,128)(2,1)S(1)}, u32[]{:S(2)}, u32[]{:S(2)}) %collective-permute-start.3) | collective-permute-done | bytes 294944 | tf_op jit(solution)/shard_map/ppermute | solution.py:730
  40.7 21.2 %self_fwd.1 = (f32[512,768]{1,0:T(8,128)}, bf16[512,768]{1,0:T(8,128)(2,1)}, bf16[6,512,128]{2,1,0:T(8,128)(2,1)}, bf16[6,512,128]{2,1,0:T(8,128)(2,1)}, bf16[6,...) custom-call(s32[2]{0:T(128)} %pad_add_fusion.refs_0_.me_ref, ...), custom_call_target="tpu_custom_call" | custom-call | tf_op jit(solution)/shard_map/self_fwd/pallas_call | solution.py:259
  64.6 13.1 %collective-permute-done.12.refs_5_.refs_6_.refs_8_ = bf16[4,96,768]{2,1,0:T(8,128)(2,1)S(1)} collective-permute-done((bf16[4,96,768]{2,1,0:T(8,128)(2,1)S(1)}, bf16[4,96,768]{2,1,0:T(8,128)(2,1)S(1)}, u32[]{:S(2)}, u32[]{:S(2)}) %collective-permute-start.12) | collective-permute-done | bytes 589856 | tf_op jit(solution)/shard_map/ppermute | solution.py:730
  88.8 4.3 ffn_fwd.1
  93.2 3.6 collective-permute-done.18.refs_6_.refs_10_
  108.7 3.6 collective-permute-start.23
  116.4 3.4 collective-permute-done.23.refs_9_.refs_13_
  125.0 20.9 %cross_fwd.1 = (f32[512,768]{1,0:T(8,128)}, bf16[512,768]{1,0:T(8,128)(2,1)}, bf16[6,512,128]{2,1,0:T(8,128)(2,1)}, bf16[6,512,128]{2,1,0:T(8,128)(2,1)}, bf16[6...) custom-call(s32[2]{0:T(128)} %pad_add_fusion.refs_0_.me_ref, ...), custom_call_target="tpu_custom_call" | custom-call | tf_op jit(solution)/shard_map/cross_fwd/pallas_call | solution.py:259
  145.9 25.0 %ffn_both.1 = (bf16[512,768]{1,0:T(8,128)(2,1)}, bf16[512,768]{1,0:T(8,128)(2,1)}, f32[1,768]{1,0:T(1,128)}, bf16[4,768,768]{2,1,0:T(8,128)(2,1)}, bf16[4,768,768]{2,1,0:T(8,128)(2,1)}) custom-call(s32[2]{0:T(128)} %pad_add_fusion.refs_0_.me_ref, bf16[512,768]{1,0:T(8,128)(2,1)} %get-tuple-element.177.refs_0_, f32[1,768]{1,0:T(1,128)} %reshape.152.refs_1_, ...), custom_call_target="tpu_custom_call" | custom-call | tf_op jit(solution)/shard_map/ffn_both/pallas_call | solution.py:629
  175.8 4.9 %all-to-all-start = ((bf16[512,4,192]{0,2,1:T(8,128)(2,1)}), bf16[512,4,192]{0,2,1:T(8,128)(2,1)S(1)}, u32[]{:S(2)}, u32[]{:S(2)}) async-start(bf16[512,4,192]{0,2,1:T(8,128)(2,1)} %bitcast.15), calls=%async_computation | async-start | bytes 1572864 | tf_op jit(solution)/shard_map/all_to_all | solution.py:962
  180.7 27.4 %cross_bwd.1 = (f32[512,768]{1,0:T(8,128)}, bf16[4,384,768]{2,1,0:T(8,128)(2,1)}, bf16[4,384,768]{2,1,0:T(8,128)(2,1)}, f32[1,768]{1,0:T(1,128)}, bf16[512,768]{1,0:T(8,128)(2,1)}) custom-call(s32[2]{0:T(128)} %pad_add_fusion.refs_0_.me_ref, bf16[512,768]{1,0:T(8,128)(2,1)} %get-tuple-element.180.refs_0_, f32[512,768]{1,0:T(8,128)} %get-tuple-element.166.refs_0_.refs_1_, ...), custom_call_target="tpu_custom_call" | custom-call | tf_op jit(solution)/shard_map/cross_bwd/pallas_call | solution.py:421
  210.1 3.6 diag_add.4
  213.8 3.6 collective-permute-start.29
  222.0 9.6 %collective-permute-done.29.refs_2_ = bf16[384,768]{1,0:T(8,128)(2,1)S(1)} collective-permute-done((bf16[384,768]{1,0:T(8,128)(2,1)}, bf16[384,768]{1,0:T(8,128)(2,1)S(1)}, u32[]{:S(2)}, u32[]{:S(2)}) %collective-permute-start.29) | collective-permute-done | bytes 589856 | tf_op jit(solution)/shard_map/ppermute | solution.py:730
  242.3 3.7 collective-permute-start.33
  246.9 4.9 ffn_bwd.1
  255.5 5.7 %rest_add.4 = (bf16[768,768]{1,0:T(8,128)(2,1)}, bf16[768,768]{1,0:T(8,128)(2,1)}, bf16[768,768]{1,0:T(8,128)(2,1)}) custom-call(s32[2]{0:T(128)} %pad_add_fusion.refs_0_.me_ref, bf16[4,768,768]{2,1,0:T(8,128)(2,1)} %get-tuple-element.193.refs_0_, bf16[4,768,768]{2,1,0:T(8,128)(2,1)} %collective-permute-done.28.refs_1_, bf16[384,768]{1,0:T(8,128)(2,1)} %copy-done.44, ...), custom_call_target="tpu_custom_call" | custom-call | tf_op jit(solution)/shard_map/rest_add/pallas_call | solution.py:709
  261.2 3.6 collective-permute-start.36
  264.8 3.7 collective-permute-start.37
  270.1 27.7 %self_bwd.1 = (bf16[512,768]{1,0:T(8,128)(2,1)}, bf16[4,400,768]{2,1,0:T(8,128)(2,1)}, bf16[4,400,768]{2,1,0:T(8,128)(2,1)}) custom-call(s32[2]{0:T(128)} %pad_add_fusion.refs_0_.me_ref, f32[512,768]{1,0:T(8,128)} %get-tuple-element.216.refs_1_, bf16[512,768]{1,0:T(8,128)(2,1)} %get-tuple-element.156.refs_1_.refs_2_, f32[1,768]{1,0:T(1,128)} %select_n.171.refs_2_.refs_3_, ...), custom_call_target="tpu_custom_call" | custom-call | tf_op jit(solution)/shard_map/self_bwd/pallas_call | solution.py:421
  300.6 3.4 add_convert_fusion.2
  304.1 6.1 %collective-permute-start.51 = (bf16[768,768]{1,0:T(8,128)(2,1)}, bf16[768,768]{1,0:T(8,128)(2,1)}, u32[]{:S(2)}, u32[]{:S(2)}) collective-permute-start(bf16[768,768]{1,0:T(8,128)(2,1)} %add_convert_fusion.2), channel_id=1, source_target_pairs={{0,1},{3,2},{4,5},{7,6},{8,9},{11,10},{12,13},{15,14},{16,17},{19,... | collective-permute-start | bytes 3538952 | tf_op jit(solution)/shard_map/ppermute | solution.py:734
  311.6 3.9 rest_add.6
  315.5 3.5 collective-permute-start.43
  326.1 6.3 %collective-permute-done.43 = bf16[384,768]{1,0:T(8,128)(2,1)} collective-permute-done((bf16[384,768]{1,0:T(8,128)(2,1)}, bf16[384,768]{1,0:T(8,128)(2,1)}, u32[]{:S(2)}, u32[]{:S(2)}) %collective-permute-start.43) | collective-permute-done | bytes 589856 | tf_op jit(solution)/shard_map/ppermute | solution.py:730
  342.7 8.2 %collective-permute-start.45 = (bf16[384,768]{1,0:T(8,128)(2,1)S(1)}, bf16[384,768]{1,0:T(8,128)(2,1)}, u32[]{:S(2)}, u32[]{:S(2)}) collective-permute-start(bf16[384,768]{1,0:T(8,128)(2,1)S(1)} %add_convert_fusion.5), channel_id=1, source_target_pairs={{0,1},{3,2},{4,5},{7,6},{8,9},{11,10},{12,13},{15,14},{16,17},{19,... | collective-permute-start | bytes 1769480 | tf_op jit(solution)/shard_map/ppermute | solution.py:734
  352.1 3.7 all-to-all-start.1
  358.2 4.9 %collective-permute-done.42.from_y = bf16[208,768]{1,0:T(8,128)(2,1)S(1)} collective-permute-done((bf16[208,768]{1,0:T(8,128)(2,1)}, bf16[208,768]{1,0:T(8,128)(2,1)S(1)}, u32[]{:S(2)}, u32[]{:S(2)}) %collective-permute-start.42) | collective-permute-done | bytes 319520 | tf_op jit(solution)/shard_map/ppermute | solution.py:730
  363.9 3.9 rest_add.7
  386.6 33.0 %collective-permute-start.54 = (bf16[400,768]{1,0:T(8,128)(2,1)S(1)}, bf16[400,768]{1,0:T(8,128)(2,1)S(1)}, u32[]{:S(2)}, u32[]{:S(2)}) collective-permute-start(bf16[400,768]{1,0:T(8,128)(2,1)S(1)} %add_convert_fusion.4), channel_id=1, source_target_pairs={{0,1},{3,2},{4,5},{7,6},{8,9},{11,10},{12,13},{15,14},{16,17},{19,... | collective-permute-start | bytes 1843208 | tf_op jit(solution)/shard_map/ppermute | solution.py:734
  419.6 11.3 %collective-permute-done.60 = bf16[384,768]{1,0:T(8,128)(2,1)} collective-permute-done((bf16[384,768]{1,0:T(8,128)(2,1)}, bf16[384,768]{1,0:T(8,128)(2,1)}, u32[]{:S(2)}, u32[]{:S(2)}) %collective-permute-start.60) | collective-permute-done | bytes 589856 | tf_op jit(solution)/shard_map/ppermute | solution.py:734
  444.1 34.7 %collective-permute-done.56 = bf16[400,768]{1,0:T(8,128)(2,1)S(1)} collective-permute-done((bf16[400,768]{1,0:T(8,128)(2,1)S(1)}, bf16[400,768]{1,0:T(8,128)(2,1)S(1)}, u32[]{:S(2)}, u32[]{:S(2)}) %collective-permute-start.56) | collective-permute-done | bytes 614432 | tf_op jit(solution)/shard_map/ppermute | solution.py:734
  (320 shorter events, 164.9 us)
Async XLA Ops:
  23.0 38.9 %collective-permute-start.10 = (bf16[8,96,768]{2,1,0:T(8,128)(2,1)S(1)}, bf16[8,96,768]{2,1,0:T(8,128)(2,1)S(1)}, u32[]{:S(2)}, u32[]{:S(2)}) collective-permute-start(bf16[8,96,768]{2,1,0:T(8,128)(2,1)S(1)} %pad_maximum_fusion.refs_2_.refs_3_.refs_5_), channel_id=1, source_target_pairs={{0,16},{1,17},{2,18},{3,19},{4,20},{5,21},{6,22},{7,23},{8,24},{9,... | collective-permute-start | bytes 3538952 | tf_op jit(solution)/shard_map/ppermute | solution.py:730
  23.4 38.5 %collective-permute-start.11 = (bf16[8,96,768]{2,1,0:T(8,128)(2,1)S(1)}, bf16[8,96,768]{2,1,0:T(8,128)(2,1)}, u32[]{:S(2)}, u32[]{:S(2)}) collective-permute-start(bf16[8,96,768]{2,1,0:T(8,128)(2,1)S(1)} %pad_maximum_fusion.refs_2_.refs_3_.refs_5_), channel_id=1, source_target_pairs={{0,4},{1,5},{2,6},{3,7},{4,0},{5,1},{6,2},{7,3},{8,12},{9,13},{10,... | collective-permute-start | bytes 3538952 | tf_op jit(solution)/shard_map/ppermute | solution.py:730
  23.4 38.5 %collective-permute-start.9 = (bf16[8,96,768]{2,1,0:T(8,128)(2,1)S(1)}, bf16[8,96,768]{2,1,0:T(8,128)(2,1)S(1)}, u32[]{:S(2)}, u32[]{:S(2)}) collective-permute-start(bf16[8,96,768]{2,1,0:T(8,128)(2,1)S(1)} %pad_maximum_fusion.refs_2_.refs_3_.refs_5_), channel_id=1, source_target_pairs={{0,8},{1,9},{2,10},{3,11},{4,12},{5,13},{6,14},{7,15},{8,0},{9,1},... | collective-permute-start | bytes 3538952 | tf_op jit(solution)/shard_map/ppermute | solution.py:730
  64.0 23.8 %collective-permute-start.14 = (bf16[8,96,768]{2,1,0:T(8,128)(2,1)S(1)}, bf16[8,96,768]{2,1,0:T(8,128)(2,1)S(1)}, u32[]{:S(2)}, u32[]{:S(2)}) collective-permute-start(bf16[8,96,768]{2,1,0:T(8,128)(2,1)S(1)} %collective-permute-done.9.refs_3_.refs_4_.refs_6_), channel_id=1, source_target_pairs={{0,4},{1,5},{2,6},{3,7},{4,0},{5,1},{6,2},{7,3},{8,12},{9,13},{10,... | collective-permute-start | bytes 3538952 | tf_op jit(solution)/shard_map/ppermute | solution.py:730
  64.0 23.8 %collective-permute-start.15 = (bf16[8,96,768]{2,1,0:T(8,128)(2,1)S(1)}, bf16[8,96,768]{2,1,0:T(8,128)(2,1)}, u32[]{:S(2)}, u32[]{:S(2)}) collective-permute-start(bf16[8,96,768]{2,1,0:T(8,128)(2,1)S(1)} %collective-permute-done.10.refs_4_.refs_5_.refs_7_), channel_id=1, source_target_pairs={{0,4},{1,5},{2,6},{3,7},{4,0},{5,1},{6,2},{7,3},{8,12},{9,13},{10,... | collective-permute-start | bytes 3538952 | tf_op jit(solution)/shard_map/ppermute | solution.py:730
  78.8 17.9 %collective-permute-start.18 = (bf16[4,96,768]{2,1,0:T(8,128)(2,1)}, bf16[4,96,768]{2,1,0:T(8,128)(2,1)}, u32[]{:S(2)}, u32[]{:S(2)}) collective-permute-start(bf16[4,96,768]{2,1,0:T(8,128)(2,1)} %pad_maximum_fusion.2.refs_5_.refs_9_), channel_id=1, source_target_pairs={{0,8},{3,11},{4,12},{7,15},{8,0},{11,3},{12,4},{15,7},{16,24},{19,... | collective-permute-start | bytes 1769480 | tf_op jit(solution)/shard_map/ppermute | solution.py:730
  99.0 24.3 %collective-permute-start.21 = (bf16[512,768]{1,0:T(8,128)(2,1)}, bf16[512,768]{1,0:T(8,128)(2,1)S(1)}, u32[]{:S(2)}, u32[]{:S(2)}) collective-permute-start(bf16[512,768]{1,0:T(8,128)(2,1)} %get-tuple-element.173), channel_id=1, source_target_pairs={{1,0},{2,3},{5,4},{6,7},{9,8},{10,11},{13,12},{14,15},{17,16},{18,... | collective-permute-start | bytes 2359304 | tf_op jit(solution)/shard_map/ppermute | solution.py:734
  101.2 21.6 %collective-permute-start.24 = (bf16[4,96,768]{2,1,0:T(8,128)(2,1)}, bf16[4,96,768]{2,1,0:T(8,128)(2,1)S(1)}, u32[]{:S(2)}, u32[]{:S(2)}) collective-permute-start(bf16[4,96,768]{2,1,0:T(8,128)(2,1)} %collective-permute-done.18.refs_6_.refs_10_), channel_id=1, source_target_pairs={{0,4},{3,7},{4,0},{7,3},{8,12},{11,15},{12,8},{15,11},{16,20},{19,... | collective-permute-start | bytes 1769480 | tf_op jit(solution)/shard_map/ppermute | solution.py:730
  170.9 37.3 %collective-permute-start.28 = (bf16[4,768,768]{2,1,0:T(8,128)(2,1)}, bf16[4,768,768]{2,1,0:T(8,128)(2,1)}, u32[]{:S(2)}, u32[]{:S(2)}) collective-permute-start(bf16[4,768,768]{2,1,0:T(8,128)(2,1)} %get-tuple-element.179), channel_id=1, source_target_pairs={{0,4},{3,7},{4,0},{7,3},{8,12},{11,15},{12,8},{15,11},{16,20},{19,... | collective-permute-start | bytes 14155784 | tf_op jit(solution)/shard_map/ppermute | solution.py:730
  175.8 32.4 %all-to-all-start = ((bf16[512,4,192]{0,2,1:T(8,128)(2,1)}), bf16[512,4,192]{0,2,1:T(8,128)(2,1)S(1)}, u32[]{:S(2)}, u32[]{:S(2)}) async-start(bf16[512,4,192]{0,2,1:T(8,128)(2,1)} %bitcast.15), calls=%async_computation | async-start | bytes 1572864 | tf_op jit(solution)/shard_map/all_to_all | solution.py:962
  208.2 27.6 %collective-permute-start.31 = (bf16[4,384,768]{2,1,0:T(8,128)(2,1)}, bf16[4,384,768]{2,1,0:T(8,128)(2,1)S(1)}, u32[]{:S(2)}, u32[]{:S(2)}) collective-permute-start(bf16[4,384,768]{2,1,0:T(8,128)(2,1)} %get-tuple-element.197), channel_id=1, source_target_pairs={{0,4},{3,7},{4,0},{7,3},{8,12},{11,15},{12,8},{15,11},{16,20},{19,... | collective-permute-start | bytes 7077896 | tf_op jit(solution)/shard_map/ppermute | solution.py:730
  213.8 17.8 %collective-permute-start.29 = (bf16[384,768]{1,0:T(8,128)(2,1)}, bf16[384,768]{1,0:T(8,128)(2,1)S(1)}, u32[]{:S(2)}, u32[]{:S(2)}) collective-permute-start(bf16[384,768]{1,0:T(8,128)(2,1)} %get-tuple-element.195), channel_id=1, source_target_pairs={{0,8},{3,11},{4,12},{7,15},{8,0},{11,3},{12,4},{15,7},{16,24},{19,... | collective-permute-start | bytes 1769480 | tf_op jit(solution)/shard_map/ppermute | solution.py:730
  220.7 25.4 %collective-permute-start.34 = (bf16[512,768]{1,0:T(8,128)(2,1)}, bf16[512,768]{1,0:T(8,128)(2,1)S(1)}, u32[]{:S(2)}, u32[]{:S(2)}) collective-permute-start(bf16[512,768]{1,0:T(8,128)(2,1)} %get-tuple-element.202), channel_id=1, source_target_pairs={{0,1},{3,2},{4,5},{7,6},{8,9},{11,10},{12,13},{15,14},{16,17},{19,... | collective-permute-start | bytes 2359304 | tf_op jit(solution)/shard_map/ppermute | solution.py:734
  252.5 45.4 %collective-permute-start.35 = (bf16[4,768,768]{2,1,0:T(8,128)(2,1)}, bf16[4,768,768]{2,1,0:T(8,128)(2,1)}, u32[]{:S(2)}, u32[]{:S(2)}) collective-permute-start(bf16[4,768,768]{2,1,0:T(8,128)(2,1)} %get-tuple-element.208), channel_id=1, source_target_pairs={{1,5},{2,6},{5,1},{6,2},{9,13},{10,14},{13,9},{14,10},{17,21},{18,... | collective-permute-start | bytes 14155784 | tf_op jit(solution)/shard_map/ppermute | solution.py:730
  261.2 36.6 %collective-permute-start.36 = (bf16[768,768]{1,0:T(8,128)(2,1)}, bf16[768,768]{1,0:T(8,128)(2,1)S(1)}, u32[]{:S(2)}, u32[]{:S(2)}) collective-permute-start(bf16[768,768]{1,0:T(8,128)(2,1)} %get-tuple-element.214), channel_id=1, source_target_pairs={{0,8},{3,11},{4,12},{7,15},{8,0},{11,3},{12,4},{15,7},{16,24},{19,... | collective-permute-start | bytes 3538952 | tf_op jit(solution)/shard_map/ppermute | solution.py:730
  264.8 33.0 %collective-permute-start.37 = (bf16[768,768]{1,0:T(8,128)(2,1)}, bf16[768,768]{1,0:T(8,128)(2,1)S(1)}, u32[]{:S(2)}, u32[]{:S(2)}) collective-permute-start(bf16[768,768]{1,0:T(8,128)(2,1)} %get-tuple-element.215), channel_id=1, source_target_pairs={{0,16},{3,19},{4,20},{7,23},{8,24},{11,27},{12,28},{15,31},{16,0},... | collective-permute-start | bytes 3538952 | tf_op jit(solution)/shard_map/ppermute | solution.py:730
  299.2 22.3 %collective-permute-start.40 = (bf16[4,400,768]{2,1,0:T(8,128)(2,1)}, bf16[4,400,768]{2,1,0:T(8,128)(2,1)S(1)}, u32[]{:S(2)}, u32[]{:S(2)}) collective-permute-start(bf16[4,400,768]{2,1,0:T(8,128)(2,1)} %get-tuple-element.235), channel_id=1, source_target_pairs={{0,4},{1,5},{2,6},{3,7},{4,0},{5,1},{6,2},{7,3},{8,12},{9,13},{10,... | collective-permute-start | bytes 7372808 | tf_op jit(solution)/shard_map/ppermute | solution.py:730
  299.9 19.1 %collective-permute-start.38 = (bf16[384,768]{1,0:T(8,128)(2,1)}, bf16[384,768]{1,0:T(8,128)(2,1)S(1)}, u32[]{:S(2)}, u32[]{:S(2)}) collective-permute-start(bf16[384,768]{1,0:T(8,128)(2,1)} %get-tuple-element.233), channel_id=1, source_target_pairs={{1,9},{2,10},{5,13},{6,14},{9,1},{10,2},{13,5},{14,6},{17,25},{18,... | collective-permute-start | bytes 1769480 | tf_op jit(solution)/shard_map/ppermute | solution.py:730
  304.1 33.1 %collective-permute-start.51 = (bf16[768,768]{1,0:T(8,128)(2,1)}, bf16[768,768]{1,0:T(8,128)(2,1)}, u32[]{:S(2)}, u32[]{:S(2)}) collective-permute-start(bf16[768,768]{1,0:T(8,128)(2,1)} %add_convert_fusion.2), channel_id=1, source_target_pairs={{0,1},{3,2},{4,5},{7,6},{8,9},{11,10},{12,13},{15,14},{16,17},{19,... | collective-permute-start | bytes 3538952 | tf_op jit(solution)/shard_map/ppermute | solution.py:734
  337.1 33.9 %collective-permute-start.52 = (bf16[768,768]{1,0:T(8,128)(2,1)}, bf16[768,768]{1,0:T(8,128)(2,1)}, u32[]{:S(2)}, u32[]{:S(2)}) collective-permute-start(bf16[768,768]{1,0:T(8,128)(2,1)} %collective-permute-done.51), channel_id=1, source_target_pairs={{1,2},{2,1},{5,6},{6,5},{9,10},{10,9},{13,14},{14,13},{17,18},{18,... | collective-permute-start | bytes 3538952 | tf_op jit(solution)/shard_map/ppermute | solution.py:734
  338.9 34.6 %collective-permute-start.49 = (bf16[768,768]{1,0:T(8,128)(2,1)}, bf16[768,768]{1,0:T(8,128)(2,1)}, u32[]{:S(2)}, u32[]{:S(2)}) collective-permute-start(bf16[768,768]{1,0:T(8,128)(2,1)} %get-tuple-element.268), channel_id=1, source_target_pairs={{1,9},{2,10},{5,13},{6,14},{9,1},{10,2},{13,5},{14,6},{17,25},{18,... | collective-permute-start | bytes 3538952 | tf_op jit(solution)/shard_map/ppermute | solution.py:730
  340.6 32.8 %collective-permute-start.50 = (bf16[768,768]{1,0:T(8,128)(2,1)}, bf16[768,768]{1,0:T(8,128)(2,1)}, u32[]{:S(2)}, u32[]{:S(2)}) collective-permute-start(bf16[768,768]{1,0:T(8,128)(2,1)} %get-tuple-element.269), channel_id=1, source_target_pairs={{1,17},{2,18},{5,21},{6,22},{9,25},{10,26},{13,29},{14,30},{17,1},... | collective-permute-start | bytes 3538952 | tf_op jit(solution)/shard_map/ppermute | solution.py:730
  342.7 21.2 %collective-permute-start.45 = (bf16[384,768]{1,0:T(8,128)(2,1)S(1)}, bf16[384,768]{1,0:T(8,128)(2,1)}, u32[]{:S(2)}, u32[]{:S(2)}) collective-permute-start(bf16[384,768]{1,0:T(8,128)(2,1)S(1)} %add_convert_fusion.5), channel_id=1, source_target_pairs={{0,1},{3,2},{4,5},{7,6},{8,9},{11,10},{12,13},{15,14},{16,17},{19,... | collective-permute-start | bytes 1769480 | tf_op jit(solution)/shard_map/ppermute | solution.py:734
  352.1 31.8 %all-to-all-start.1 = ((bf16[512,4,192]{0,2,1:T(8,128)(2,1)}), bf16[512,4,192]{0,2,1:T(8,128)(2,1)S(1)}, u32[]{:S(2)}, u32[]{:S(2)}) async-start(bf16[512,4,192]{0,2,1:T(8,128)(2,1)} %bitcast.17), calls=%async_computation.1 | async-start | bytes 1572864 | tf_op jit(solution)/shard_map/all_to_all | solution.py:962
  373.4 64.9 %collective-permute-start.61 = (bf16[768,768]{1,0:T(8,128)(2,1)}, bf16[768,768]{1,0:T(8,128)(2,1)}, u32[]{:S(2)}, u32[]{:S(2)}) collective-permute-start(bf16[768,768]{1,0:T(8,128)(2,1)} %collective-permute-done.52), channel_id=1, source_target_pairs={{1,0},{2,3},{5,4},{6,7},{9,8},{10,11},{13,12},{14,15},{17,16},{18,... | collective-permute-start | bytes 3538952 | tf_op jit(solution)/shard_map/ppermute | solution.py:734
  376.8 56.5 %collective-permute-start.55 = (bf16[768,768]{1,0:T(8,128)(2,1)S(1)}, bf16[768,768]{1,0:T(8,128)(2,1)}, u32[]{:S(2)}, u32[]{:S(2)}) collective-permute-start(bf16[768,768]{1,0:T(8,128)(2,1)S(1)} %add_convert_fusion.1), channel_id=1, source_target_pairs={{1,2},{2,1},{5,6},{6,5},{9,10},{10,9},{13,14},{14,13},{17,18},{18,... | collective-permute-start | bytes 3538952 | tf_op jit(solution)/shard_map/ppermute | solution.py:734
  382.6 48.3 %collective-permute-start.60 = (bf16[384,768]{1,0:T(8,128)(2,1)}, bf16[384,768]{1,0:T(8,128)(2,1)}, u32[]{:S(2)}, u32[]{:S(2)}) collective-permute-start(bf16[384,768]{1,0:T(8,128)(2,1)} %collective-permute-done.48), channel_id=1, source_target_pairs={{1,0},{2,3},{5,4},{6,7},{9,8},{10,11},{13,12},{14,15},{17,16},{18,... | collective-permute-start | bytes 1769480 | tf_op jit(solution)/shard_map/ppermute | solution.py:734
  385.9 50.3 %collective-permute-start.53 = (bf16[400,768]{1,0:T(8,128)(2,1)S(1)}, bf16[400,768]{1,0:T(8,128)(2,1)S(1)}, u32[]{:S(2)}, u32[]{:S(2)}) collective-permute-start(bf16[400,768]{1,0:T(8,128)(2,1)S(1)} %add_convert_fusion.4), channel_id=1, source_target_pairs={{1,2},{2,1},{5,6},{6,5},{9,10},{10,9},{13,14},{14,13},{17,18},{18,... | collective-permute-start | bytes 1843208 | tf_op jit(solution)/shard_map/ppermute | solution.py:734
  386.6 49.6 %collective-permute-start.54 = (bf16[400,768]{1,0:T(8,128)(2,1)S(1)}, bf16[400,768]{1,0:T(8,128)(2,1)S(1)}, u32[]{:S(2)}, u32[]{:S(2)}) collective-permute-start(bf16[400,768]{1,0:T(8,128)(2,1)S(1)} %add_convert_fusion.4), channel_id=1, source_target_pairs={{0,1},{3,2},{4,5},{7,6},{8,9},{11,10},{12,13},{15,14},{16,17},{19,... | collective-permute-start | bytes 1843208 | tf_op jit(solution)/shard_map/ppermute | solution.py:734
  434.9 46.3 %collective-permute-start.57 = (bf16[768,768]{1,0:T(8,128)(2,1)S(1)}, bf16[768,768]{1,0:T(8,128)(2,1)S(1)}, u32[]{:S(2)}, u32[]{:S(2)}) collective-permute-start(bf16[768,768]{1,0:T(8,128)(2,1)S(1)} %add_convert_fusion), channel_id=1, source_target_pairs={{1,0},{2,3},{5,4},{6,7},{9,8},{10,11},{13,12},{14,15},{17,16},{18,... | collective-permute-start | bytes 3538952 | tf_op jit(solution)/shard_map/ppermute | solution.py:734
  437.1 41.8 %collective-permute-start.56 = (bf16[400,768]{1,0:T(8,128)(2,1)S(1)}, bf16[400,768]{1,0:T(8,128)(2,1)S(1)}, u32[]{:S(2)}, u32[]{:S(2)}) collective-permute-start(bf16[400,768]{1,0:T(8,128)(2,1)S(1)} %add_convert_fusion.3), channel_id=1, source_target_pairs={{1,0},{2,3},{5,4},{6,7},{9,8},{10,11},{13,12},{14,15},{17,16},{18,... | collective-permute-start | bytes 1843208 | tf_op jit(solution)/shard_map/ppermute | solution.py:734
  442.8 43.7 %collective-permute-start.59 = (bf16[400,768]{1,0:T(8,128)(2,1)S(1)}, bf16[400,768]{1,0:T(8,128)(2,1)S(1)}, u32[]{:S(2)}, u32[]{:S(2)}) collective-permute-start(bf16[400,768]{1,0:T(8,128)(2,1)S(1)} %collective-permute-done.58), channel_id=1, source_target_pairs={{1,0},{2,3},{5,4},{6,7},{9,8},{10,11},{13,12},{14,15},{17,16},{18,... | collective-permute-start | bytes 1843208 | tf_op jit(solution)/shard_map/ppermute | solution.py:734
  (103 other events, 913.7 us)

commit v4 on v3

--- a/solution.py
+++ b/solution.py
@@ -813,6 +813,12 @@
             return whole_scatter(self.keep, self.state[0])
         return wide_add(*self.state)
 
+    def halves(self):
+        if not self.small:
+            return jnp.split(self.result(), 2)
+        half = self.state[0].shape[0] // 2
+        return wide_add(*[v[:half] for v in self.state]), wide_add(*[v[half:] for v in self.state])
+
 
 def tie_all(scatters, *values):
     counts = [len(s.state) for s in scatters]
@@ -967,68 +973,82 @@
 
     dec_out, gz2, dgain_df, *blocks = ffn("both", me, z2, gain_of(dec_ffn_gain), w_ffn, cot)
     sum_df = Scatter(me, *blocks, DEC)
-    out_cols = by_columns(pick(enc_out, dec_out))
-    gz1, *blocks, dgain_c, genc_out = attn_bwd(
+    gz1, *blocks_c, dgain_c, genc_out = attn_bwd(
         me, gz2, z1, gain_c, w_cross, saved_c, ksrc=memory
     )
-    genc_out, gz1, out_cols, *blocks = tie_all([sum_df], genc_out, gz1, out_cols, *blocks)
     genc = between(genc_out, [(0, 1), (3, 2)])
-    sum_c = Scatter(me, *blocks, DEC)
+    sum_c = Scatter(me, *blocks_c, DEC)
+    out_rows = pick(enc_out, dec_out)
+    (out_rows,) = tie_all([sum_df, sum_c], out_rows)
     sum_df.go()
-    (gz1,) = tie_all([sum_df, sum_c], gz1)
+    genc, out_rows, _ = tie(genc, out_rows, sum_df.token)
+    gx1, dgain_ef, *blocks = ffn("bwd", me, x1, enc_gain, w_ffn, genc, saved_f)
+    gx1, out_rows, *blocks = tie_all([sum_df], gx1, out_rows, *blocks)
+    sum_ef = Scatter(me, *blocks, ENC)
     sum_df.go()
+    out_rows, _ = tie_all([sum_c], out_rows, sum_df.token)
+    out_cols = by_columns(out_rows)
     sum_c.go()
-    gx1, dgain_ef, *blocks = ffn("bwd", me, x1, enc_gain, w_ffn, genc, saved_f)
-    gx1, *blocks = tie_all([sum_c], gx1, *blocks)
-    sum_ef = Scatter(me, *blocks, ENC)
     gains = jnp.concatenate([pick(dgain_ef, dgain_df), dgain_c])
     din, *blocks = attn_bwd(
         me, gz1, src, gain_a, w_attn, saved, others=(gx1, gains, sum_hot)
     )
-    din, *blocks = tie_all([sum_ef, sum_c, sum_df], din, *blocks)
+    din, out_cols, *blocks = tie_all([sum_ef, sum_c, sum_df], din, out_cols, *blocks)
     sum_a = Scatter(me, *blocks, ALL)
     sum_ef.go()
     tie_all([sum_df, sum_c], sum_ef.token)
-    all_df = FromEnds(sum_df.result(), is_enc)
-    tie_all([sum_c], all_df.share)
+    first, last = sum_df.halves()
+    all_d1 = FromEnds(first, is_enc)
+    last = tie(last, first)[0]
+    all_d2 = FromEnds(last, is_enc)
+    tie_all([sum_c], last)
     sum_c.go()
-    tie_all([sum_ef, sum_a], all_df.share)
+    tie_all([sum_ef, sum_a], last)
     sum_ef.go()
+    tie_all([all_d1], sum_ef.token)
+    all_d1.go()
     tie_all([sum_a], sum_ef.token)
     sum_a.go()
-    tie_all([sum_c], sum_a.token)
+    tie_all([all_d2, sum_c], sum_a.token)
+    all_d2.go()
     all_c = FromEnds(sum_c.result(), is_enc)
-    tie_all([all_df], all_c.share)
-    all_df.go()
     din, _ = tie(din, sum_a.token)
     grad_cols = by_columns(din)
-    tie_all([sum_a, all_c])
+    tie_all([sum_a, all_d1])
     sum_a.go()
+    all_d1.go()
+    tie_all([sum_ef, all_c, all_d2], sum_a.token)
+    first, last = sum_ef.halves()
+    all_f1 = FromMiddle(first, is_enc)
+    last = tie(last, first)[0]
+    all_f2 = FromMiddle(last, is_enc)
+    all_d2.go()
     all_c.go()
-    tie_all([sum_ef, all_df], sum_a.token)
-    all_ef = FromMiddle(sum_ef.result(), is_enc)
-    all_df.go()
-    tie_all([sum_a, all_c], all_ef.share)
+    tie_all([sum_a], last)
     s_a = sum_a.result()
     all_e = FromMiddle(s_a, is_enc)
     all_s = FromEnds(s_a, is_enc)
-    all_c.go()
-    tie_all([all_ef], s_a)
-    all_ef.go()
-    tie_all([all_e, all_s], all_ef.total)
+    tie_all([all_f1], s_a)
+    all_f1.go()
+    tie_all([all_f2], all_f1.total)
+    all_f2.go()
+    tie_all([all_e, all_s, all_c], all_f2.total)
     all_e.go()
     all_s.go()
+    all_c.go()
     tie_all([all_s], all_e.total)
     all_s.go()
 
     def split(f):
         return f[: 4 * shard_rows].reshape(4, shard_rows, D), f[4 * shard_rows :]
 
-    g_df, g_c, g_s, g_ef, g_e = (
-        split(p.result()) for p in (all_df, all_c, all_s, all_ef, all_e)
-    )
-    gi_e, gi_d = (jnp.transpose(g[0], (1, 0, 2)).reshape(-1, FF) for g in (g_ef, g_df))
-    go_e, go_d = g_ef[1], g_df[1]
+    g_c, g_s, g_e = (split(p.result()) for p in (all_c, all_s, all_e))
+
+    def in_rows(f):
+        return jnp.transpose(f.result().reshape(4, shard_rows, D), (1, 0, 2)).reshape(-1, FF)
+
+    gi_e, gi_d = in_rows(all_f1), in_rows(all_d1)
+    go_e, go_d = all_f2.result(), all_d2.result()
     more_e, more_s = g_e[1], g_s[1]
     g_e, g_s, g_c = g_e[0], g_s[0], g_c[0]
     tables = [jnp.transpose(m[:HEADS, :BUCKETS]) for m in (more_e, more_s)]

time: 498 us -> 485 us (0.974)
  starting transfers between devices: 149 us -> 133 us
  local copies, waits for them, and re-layouts: 36.7 us -> 30.5 us
    ppermute x15 -> x20, starting transfers between devices: 62.7 us -> 41.5 us  [between(): return lax.ppermute(x, 'narrow', pairs)]
    ppermute x15 -> x20, waiting for transfers between devices: 49.8 us -> 68 us  [between(): return lax.ppermute(x, 'narrow', pairs)]
    ppermute x47, waiting for transfers between devices: 69.1 us -> 54.9 us  [across(): return lax.ppermute(x, ('wide', 'narrow'), pairs)]
    all_to_all x2, starting transfers between devices: 8.58 us -> 16.1 us  [by_columns(): return lax.all_to_all(x, 'narrow', split_axis=1, concat_axis=0, tiled=True)]
    unnamed x142 -> x128, local copies, waits for them, and re-layouts: 13.7 us -> 9.87 us
    convert_element_type x6 -> x7, other arithmetic: 8.9 us -> 10.9 us  [wide_add(): return total.astype(bf16)]
  transfers between devices with their start and end apart: 64 -> 69, of which waited for: 25 -> 28; matrix products, arithmetic and copies ran while one was open for 9% -> 10% of each run, Pallas kernels for 22% -> 23%
where the time goes in v4:
time: 485 us; the launch traced here: 476 us
  Pallas kernels  156 us (32%)
  starting transfers between devices  133 us (27%)
  waiting for transfers between devices  123 us (25%)
  local copies, waits for them, and re-layouts  30.5 us (6%)
  other arithmetic  29.5 us (6%)
    ppermute x47, starting transfers between devices, across(): return lax.ppermute(x, ('wide', 'narrow'), pairs)  75.7 us
    ppermute x20, waiting for transfers between devices, between(): return lax.ppermute(x, 'narrow', pairs)  68 us
    pallas_call x2, Pallas kernels, attn_bwd(): pl.pallas_call(only(None if has_bias else 0, functools.partial(attn_bwd_k...  55.3 us
    ppermute x47, waiting for transfers between devices, across(): return lax.ppermute(x, ('wide', 'narrow'), pairs)  54.9 us
    pallas_call x2, Pallas kernels, attn_fwd(): pl.pallas_call(only(None if has_bias else 0, functools.partial(attn_fwd_k...  41.9 us
    ppermute x20, starting transfers between devices, between(): return lax.ppermute(x, 'narrow', pairs)  41.5 us
    pallas_call x3, Pallas kernels, ffn(): pl.pallas_call(only(0 if mode == 'both' else 1, functools.partial(ffn_ker...  34.1 us
    all_to_all x2, starting transfers between devices, by_columns(): return lax.all_to_all(x, 'narrow', split_axis=1, concat_axis=0, tiled=True)  16.1 us
  transfers between devices with their start and end apart: 69, of which 28 were waited for; matrix products, arithmetic and copies ran while one was open for 10% of the time, Pallas kernels for 23%

profile of v4, /device:TPU:0, one launch (start us, length us, event | category | flops | bytes accessed | tf_op | source)
XLA Modules:
  0.0 476.3 jit_solution(12162362249524139040)
XLA Ops:
  25.1 5.7 %collective-permute-done.3.refs_10_.refs_15_ = bf16[2,96,768]{2,1,0:T(8,128)(2,1)S(1)} collective-permute-done((bf16[2,96,768]{2,1,0:T(8,128)(2,1)S(1)}, bf16[2,96,768]{2,1,0:T(8,128)(2,1)S(1)}, u32[]{:S(2)}, u32[]{:S(2)}) %collective-permute-start.3) | collective-permute-done | bytes 294944 | tf_op jit(solution)/shard_map/ppermute | solution.py:730
  40.7 21.1 %self_fwd.1 = (f32[512,768]{1,0:T(8,128)}, bf16[512,768]{1,0:T(8,128)(2,1)}, bf16[6,512,128]{2,1,0:T(8,128)(2,1)}, bf16[6,512,128]{2,1,0:T(8,128)(2,1)}, bf16[6,...) custom-call(s32[2]{0:T(128)} %pad_add_fusion.refs_0_.me_ref, ...), custom_call_target="tpu_custom_call" | custom-call | tf_op jit(solution)/shard_map/self_fwd/pallas_call | solution.py:259
  64.5 13.1 %collective-permute-done.12.refs_5_.refs_6_.refs_8_ = bf16[4,96,768]{2,1,0:T(8,128)(2,1)S(1)} collective-permute-done((bf16[4,96,768]{2,1,0:T(8,128)(2,1)S(1)}, bf16[4,96,768]{2,1,0:T(8,128)(2,1)S(1)}, u32[]{:S(2)}, u32[]{:S(2)}) %collective-permute-start.12) | collective-permute-done | bytes 589856 | tf_op jit(solution)/shard_map/ppermute | solution.py:730
  88.4 4.4 ffn_fwd.1
  92.8 3.9 collective-permute-done.18.refs_6_.refs_10_
  108.6 3.6 collective-permute-start.23
  116.4 3.4 collective-permute-done.23.refs_9_.refs_13_
  125.0 20.8 %cross_fwd.1 = (f32[512,768]{1,0:T(8,128)}, bf16[512,768]{1,0:T(8,128)(2,1)}, bf16[6,512,128]{2,1,0:T(8,128)(2,1)}, bf16[6,512,128]{2,1,0:T(8,128)(2,1)}, bf16[6...) custom-call(s32[2]{0:T(128)} %pad_add_fusion.refs_0_.me_ref, ...), custom_call_target="tpu_custom_call" | custom-call | tf_op jit(solution)/shard_map/cross_fwd/pallas_call | solution.py:259
  145.7 24.9 %ffn_both.1 = (bf16[512,768]{1,0:T(8,128)(2,1)}, bf16[512,768]{1,0:T(8,128)(2,1)}, f32[1,768]{1,0:T(1,128)}, bf16[4,768,768]{2,1,0:T(8,128)(2,1)}, bf16[4,768,768]{2,1,0:T(8,128)(2,1)}) custom-call(s32[2]{0:T(128)} %pad_add_fusion.refs_0_.me_ref, bf16[512,768]{1,0:T(8,128)(2,1)} %get-tuple-element.181.refs_0_, f32[1,768]{1,0:T(1,128)} %reshape.157.refs_1_, ...), custom_call_target="tpu_custom_call" | custom-call | tf_op jit(solution)/shard_map/ffn_both/pallas_call | solution.py:629
  173.1 27.6 %cross_bwd.1 = (f32[512,768]{1,0:T(8,128)}, bf16[4,384,768]{2,1,0:T(8,128)(2,1)}, bf16[4,384,768]{2,1,0:T(8,128)(2,1)}, f32[1,768]{1,0:T(1,128)}, bf16[512,768]{1,0:T(8,128)(2,1)}) custom-call(s32[2]{0:T(128)} %pad_add_fusion.refs_0_.me_ref, bf16[512,768]{1,0:T(8,128)(2,1)} %get-tuple-element.185.refs_0_, f32[512,768]{1,0:T(8,128)} %get-tuple-element.170.refs_0_.refs_1_, ...), custom_call_target="tpu_custom_call" | custom-call | tf_op jit(solution)/shard_map/cross_bwd/pallas_call | solution.py:421
  207.4 3.7 diag_add.4
  211.1 3.7 collective-permute-start.30
  218.0 4.0 collective-permute-done.32.refs_2_
  222.9 4.9 %ffn_bwd.1 = (bf16[512,768]{1,0:T(8,128)(2,1)}, f32[1,768]{1,0:T(1,128)}, bf16[4,768,768]{2,1,0:T(8,128)(2,1)}, bf16[4,768,768]{2,1,0:T(8,128)(2,1)}) custom-call(s32[2]{0:T(128)} %pad_add_fusion.refs_0_.me_ref, bf16[512,768]{1,0:T(8,128)(2,1)} %get-tuple-element.171.refs_0_, f32[1,768]{1,0:T(1,128)} %reshape.155.refs_1_, bf16[512,768]{1,0:T(8,128)(2,1)} %copy-done.31, ...), custom_call_target="tpu_custom_call" | custom-call | tf_op jit(solution)/shard_map/ffn_bwd/pallas_call | solution.py:629
  228.6 3.4 collective-permute-done.31.refs_3_
  234.8 5.9 %rest_add.4 = (bf16[768,768]{1,0:T(8,128)(2,1)}, bf16[768,768]{1,0:T(8,128)(2,1)}, bf16[768,768]{1,0:T(8,128)(2,1)}) custom-call(s32[2]{0:T(128)} %pad_add_fusion.refs_0_.me_ref, bf16[4,768,768]{2,1,0:T(8,128)(2,1)} %get-tuple-element.183.refs_0_, bf16[4,768,768]{2,1,0:T(8,128)(2,1)} %collective-permute-done.28.refs_1_, bf16[384,768]{1,0:T(8,128)(2,1)} %copy-done.38, ...), custom_call_target="tpu_custom_call" | custom-call | tf_op jit(solution)/shard_map/rest_add/pallas_call | solution.py:709
  241.9 10.1 %all-to-all-start = ((bf16[512,4,192]{0,2,1:T(8,128)(2,1)}), bf16[512,4,192]{0,2,1:T(8,128)(2,1)S(1)}, u32[]{:S(2)}, u32[]{:S(2)}) async-start(bf16[512,4,192]{0,2,1:T(8,128)(2,1)} %bitcast.15), calls=%async_computation | async-start | bytes 1572864 | tf_op jit(solution)/shard_map/all_to_all | solution.py:968
  252.0 3.5 collective-permute-start.36
  255.5 3.3 collective-permute-start.37
  268.3 27.7 %self_bwd.1 = (bf16[512,768]{1,0:T(8,128)(2,1)}, bf16[4,400,768]{2,1,0:T(8,128)(2,1)}, bf16[4,400,768]{2,1,0:T(8,128)(2,1)}) custom-call(s32[2]{0:T(128)} %pad_add_fusion.refs_0_.me_ref, f32[512,768]{1,0:T(8,128)} %get-tuple-element.217.refs_1_, bf16[512,768]{1,0:T(8,128)(2,1)} %get-tuple-element.160.refs_1_.refs_2_, f32[1,768]{1,0:T(1,128)} %select_n.179.refs_2_.refs_3_, ...), custom_call_target="tpu_custom_call" | custom-call | tf_op jit(solution)/shard_map/self_bwd/pallas_call | solution.py:421
  306.2 3.9 rest_add.7
  310.1 3.3 collective-permute-start.50
  337.2 5.9 %all-to-all-start.1 = ((bf16[512,4,192]{0,2,1:T(8,128)(2,1)}), bf16[512,4,192]{0,2,1:T(8,128)(2,1)S(1)}, u32[]{:S(2)}, u32[]{:S(2)}) async-start(bf16[512,4,192]{0,2,1:T(8,128)(2,1)} %bitcast.17), calls=%async_computation.1 | async-start | bytes 1572864 | tf_op jit(solution)/shard_map/all_to_all | solution.py:968
  346.9 6.2 %collective-permute-start.52 = (bf16[384,768]{1,0:T(8,128)(2,1)S(1)}, bf16[384,768]{1,0:T(8,128)(2,1)}, u32[]{:S(2)}, u32[]{:S(2)}) collective-permute-start(bf16[384,768]{1,0:T(8,128)(2,1)S(1)} %add_convert_fusion.6), channel_id=1, source_target_pairs={{0,1},{3,2},{4,5},{7,6},{8,9},{11,10},{12,13},{15,14},{16,17},{19,... | collective-permute-start | bytes 1769480 | tf_op jit(solution)/shard_map/ppermute | solution.py:734
  355.4 4.0 rest_add.6
  359.4 11.3 %collective-permute-done.65 = bf16[384,768]{1,0:T(8,128)(2,1)} collective-permute-done((bf16[384,768]{1,0:T(8,128)(2,1)}, bf16[384,768]{1,0:T(8,128)(2,1)}, u32[]{:S(2)}, u32[]{:S(2)}) %collective-permute-start.65) | collective-permute-done | bytes 589856 | tf_op jit(solution)/shard_map/ppermute | solution.py:734
  391.2 11.2 %collective-permute-start.55 = (bf16[400,768]{1,0:T(8,128)(2,1)S(1)}, bf16[400,768]{1,0:T(8,128)(2,1)S(1)}, u32[]{:S(2)}, u32[]{:S(2)}) collective-permute-start(bf16[400,768]{1,0:T(8,128)(2,1)S(1)} %add_convert_fusion.1), channel_id=1, source_target_pairs={{0,1},{3,2},{4,5},{7,6},{8,9},{11,10},{12,13},{15,14},{16,17},{19,... | collective-permute-start | bytes 1843208 | tf_op jit(solution)/shard_map/ppermute | solution.py:734
  413.5 14.2 %collective-permute-done.60 = bf16[384,768]{1,0:T(8,128)(2,1)S(1)} collective-permute-done((bf16[384,768]{1,0:T(8,128)(2,1)S(1)}, bf16[384,768]{1,0:T(8,128)(2,1)S(1)}, u32[]{:S(2)}, u32[]{:S(2)}) %collective-permute-start.60) | collective-permute-done | bytes 589856 | tf_op jit(solution)/shard_map/ppermute | solution.py:734
  427.8 6.3 %collective-permute-done.61 = bf16[384,768]{1,0:T(8,128)(2,1)S(1)} collective-permute-done((bf16[384,768]{1,0:T(8,128)(2,1)S(1)}, bf16[384,768]{1,0:T(8,128)(2,1)S(1)}, u32[]{:S(2)}, u32[]{:S(2)}) %collective-permute-start.61) | collective-permute-done | bytes 589856 | tf_op jit(solution)/shard_map/ppermute | solution.py:734
  436.4 14.7 %collective-permute-done.64 = bf16[384,768]{1,0:T(8,128)(2,1)S(1)} collective-permute-done((bf16[384,768]{1,0:T(8,128)(2,1)S(1)}, bf16[384,768]{1,0:T(8,128)(2,1)S(1)}, u32[]{:S(2)}, u32[]{:S(2)}) %collective-permute-start.64) | collective-permute-done | bytes 589856 | tf_op jit(solution)/shard_map/ppermute | solution.py:734
  453.7 10.5 %collective-permute-done.59 = bf16[400,768]{1,0:T(8,128)(2,1)S(1)} collective-permute-done((bf16[400,768]{1,0:T(8,128)(2,1)S(1)}, bf16[400,768]{1,0:T(8,128)(2,1)S(1)}, u32[]{:S(2)}, u32[]{:S(2)}) %collective-permute-start.59) | collective-permute-done | bytes 614432 | tf_op jit(solution)/shard_map/ppermute | solution.py:734
  466.6 6.9 %collective-permute-done.63 = bf16[400,768]{1,0:T(8,128)(2,1)S(1)} collective-permute-done((bf16[400,768]{1,0:T(8,128)(2,1)S(1)}, bf16[400,768]{1,0:T(8,128)(2,1)S(1)}, u32[]{:S(2)}, u32[]{:S(2)}) %collective-permute-start.63) | collective-permute-done | bytes 614432 | tf_op jit(solution)/shard_map/ppermute | solution.py:734
  (318 shorter events, 177.1 us)
Async XLA Ops:
  23.0 38.8 %collective-permute-start.10 = (bf16[8,96,768]{2,1,0:T(8,128)(2,1)S(1)}, bf16[8,96,768]{2,1,0:T(8,128)(2,1)S(1)}, u32[]{:S(2)}, u32[]{:S(2)}) collective-permute-start(bf16[8,96,768]{2,1,0:T(8,128)(2,1)S(1)} %pad_maximum_fusion.refs_2_.refs_3_.refs_5_), channel_id=1, source_target_pairs={{0,16},{1,17},{2,18},{3,19},{4,20},{5,21},{6,22},{7,23},{8,24},{9,... | collective-permute-start | bytes 3538952 | tf_op jit(solution)/shard_map/ppermute | solution.py:730
  23.4 38.5 %collective-permute-start.11 = (bf16[8,96,768]{2,1,0:T(8,128)(2,1)S(1)}, bf16[8,96,768]{2,1,0:T(8,128)(2,1)}, u32[]{:S(2)}, u32[]{:S(2)}) collective-permute-start(bf16[8,96,768]{2,1,0:T(8,128)(2,1)S(1)} %pad_maximum_fusion.refs_2_.refs_3_.refs_5_), channel_id=1, source_target_pairs={{0,4},{1,5},{2,6},{3,7},{4,0},{5,1},{6,2},{7,3},{8,12},{9,13},{10,... | collective-permute-start | bytes 3538952 | tf_op jit(solution)/shard_map/ppermute | solution.py:730
  23.4 38.5 %collective-permute-start.9 = (bf16[8,96,768]{2,1,0:T(8,128)(2,1)S(1)}, bf16[8,96,768]{2,1,0:T(8,128)(2,1)S(1)}, u32[]{:S(2)}, u32[]{:S(2)}) collective-permute-start(bf16[8,96,768]{2,1,0:T(8,128)(2,1)S(1)} %pad_maximum_fusion.refs_2_.refs_3_.refs_5_), channel_id=1, source_target_pairs={{0,8},{1,9},{2,10},{3,11},{4,12},{5,13},{6,14},{7,15},{8,0},{9,1},... | collective-permute-start | bytes 3538952 | tf_op jit(solution)/shard_map/ppermute | solution.py:730
  64.0 23.4 %collective-permute-start.14 = (bf16[8,96,768]{2,1,0:T(8,128)(2,1)S(1)}, bf16[8,96,768]{2,1,0:T(8,128)(2,1)S(1)}, u32[]{:S(2)}, u32[]{:S(2)}) collective-permute-start(bf16[8,96,768]{2,1,0:T(8,128)(2,1)S(1)} %collective-permute-done.9.refs_3_.refs_4_.refs_6_), channel_id=1, source_target_pairs={{0,4},{1,5},{2,6},{3,7},{4,0},{5,1},{6,2},{7,3},{8,12},{9,13},{10,... | collective-permute-start | bytes 3538952 | tf_op jit(solution)/shard_map/ppermute | solution.py:730
  64.0 23.4 %collective-permute-start.15 = (bf16[8,96,768]{2,1,0:T(8,128)(2,1)S(1)}, bf16[8,96,768]{2,1,0:T(8,128)(2,1)}, u32[]{:S(2)}, u32[]{:S(2)}) collective-permute-start(bf16[8,96,768]{2,1,0:T(8,128)(2,1)S(1)} %collective-permute-done.10.refs_4_.refs_5_.refs_7_), channel_id=1, source_target_pairs={{0,4},{1,5},{2,6},{3,7},{4,0},{5,1},{6,2},{7,3},{8,12},{9,13},{10,... | collective-permute-start | bytes 3538952 | tf_op jit(solution)/shard_map/ppermute | solution.py:730
  98.9 24.3 %collective-permute-start.21 = (bf16[512,768]{1,0:T(8,128)(2,1)}, bf16[512,768]{1,0:T(8,128)(2,1)S(1)}, u32[]{:S(2)}, u32[]{:S(2)}) collective-permute-start(bf16[512,768]{1,0:T(8,128)(2,1)} %get-tuple-element.177), channel_id=1, source_target_pairs={{1,0},{2,3},{5,4},{6,7},{9,8},{10,11},{13,12},{14,15},{17,16},{18,... | collective-permute-start | bytes 2359304 | tf_op jit(solution)/shard_map/ppermute | solution.py:734
  101.2 21.6 %collective-permute-start.24 = (bf16[4,96,768]{2,1,0:T(8,128)(2,1)}, bf16[4,96,768]{2,1,0:T(8,128)(2,1)S(1)}, u32[]{:S(2)}, u32[]{:S(2)}) collective-permute-start(bf16[4,96,768]{2,1,0:T(8,128)(2,1)} %collective-permute-done.18.refs_6_.refs_10_), channel_id=1, source_target_pairs={{0,4},{3,7},{4,0},{7,3},{8,12},{11,15},{12,8},{15,11},{16,20},{19,... | collective-permute-start | bytes 1769480 | tf_op jit(solution)/shard_map/ppermute | solution.py:730
  170.7 36.7 %collective-permute-start.28 = (bf16[4,768,768]{2,1,0:T(8,128)(2,1)}, bf16[4,768,768]{2,1,0:T(8,128)(2,1)}, u32[]{:S(2)}, u32[]{:S(2)}) collective-permute-start(bf16[4,768,768]{2,1,0:T(8,128)(2,1)} %get-tuple-element.184), channel_id=1, source_target_pairs={{0,4},{3,7},{4,0},{7,3},{8,12},{11,15},{12,8},{15,11},{16,20},{19,... | collective-permute-start | bytes 14155784 | tf_op jit(solution)/shard_map/ppermute | solution.py:730
  232.0 64.2 %collective-permute-start.33 = (bf16[4,768,768]{2,1,0:T(8,128)(2,1)}, bf16[4,768,768]{2,1,0:T(8,128)(2,1)}, u32[]{:S(2)}, u32[]{:S(2)}) collective-permute-start(bf16[4,768,768]{2,1,0:T(8,128)(2,1)} %get-tuple-element.205), channel_id=1, source_target_pairs={{1,5},{2,6},{5,1},{6,2},{9,13},{10,14},{13,9},{14,10},{17,21},{18,... | collective-permute-start | bytes 14155784 | tf_op jit(solution)/shard_map/ppermute | solution.py:730
  241.9 54.2 %all-to-all-start = ((bf16[512,4,192]{0,2,1:T(8,128)(2,1)}), bf16[512,4,192]{0,2,1:T(8,128)(2,1)S(1)}, u32[]{:S(2)}, u32[]{:S(2)}) async-start(bf16[512,4,192]{0,2,1:T(8,128)(2,1)} %bitcast.15), calls=%async_computation | async-start | bytes 1572864 | tf_op jit(solution)/shard_map/all_to_all | solution.py:968
  252.0 44.2 %collective-permute-start.36 = (bf16[768,768]{1,0:T(8,128)(2,1)}, bf16[768,768]{1,0:T(8,128)(2,1)}, u32[]{:S(2)}, u32[]{:S(2)}) collective-permute-start(bf16[768,768]{1,0:T(8,128)(2,1)} %get-tuple-element.215), channel_id=1, source_target_pairs={{0,8},{3,11},{4,12},{7,15},{8,0},{11,3},{12,4},{15,7},{16,24},{19,... | collective-permute-start | bytes 3538952 | tf_op jit(solution)/shard_map/ppermute | solution.py:730
  255.5 40.7 %collective-permute-start.37 = (bf16[768,768]{1,0:T(8,128)(2,1)}, bf16[768,768]{1,0:T(8,128)(2,1)}, u32[]{:S(2)}, u32[]{:S(2)}) collective-permute-start(bf16[768,768]{1,0:T(8,128)(2,1)} %get-tuple-element.216), channel_id=1, source_target_pairs={{0,16},{3,19},{4,20},{7,23},{8,24},{11,27},{12,28},{15,31},{16,0},... | collective-permute-start | bytes 3538952 | tf_op jit(solution)/shard_map/ppermute | solution.py:730
  262.8 33.3 %collective-permute-start.34 = (bf16[192,768]{1,0:T(8,128)(2,1)}, bf16[192,768]{1,0:T(8,128)(2,1)S(1)}, u32[]{:S(2)}, u32[]{:S(2)}) collective-permute-start(bf16[192,768]{1,0:T(8,128)(2,1)} %get-tuple-element.213), channel_id=1, source_target_pairs={{0,8},{3,11},{4,12},{7,15},{8,0},{11,3},{12,4},{15,7},{16,24},{19,... | collective-permute-start | bytes 884744 | tf_op jit(solution)/shard_map/ppermute | solution.py:730
  265.3 30.9 %collective-permute-start.35 = (bf16[192,768]{1,0:T(8,128)(2,1)}, bf16[192,768]{1,0:T(8,128)(2,1)S(1)}, u32[]{:S(2)}, u32[]{:S(2)}) collective-permute-start(bf16[192,768]{1,0:T(8,128)(2,1)} %get-tuple-element.214), channel_id=1, source_target_pairs={{0,16},{3,19},{4,20},{7,23},{8,24},{11,27},{12,28},{15,31},{16,0},... | collective-permute-start | bytes 884744 | tf_op jit(solution)/shard_map/ppermute | solution.py:730
  296.9 21.9 %collective-permute-start.40 = (bf16[4,400,768]{2,1,0:T(8,128)(2,1)}, bf16[4,400,768]{2,1,0:T(8,128)(2,1)S(1)}, u32[]{:S(2)}, u32[]{:S(2)}) collective-permute-start(bf16[4,400,768]{2,1,0:T(8,128)(2,1)} %get-tuple-element.238), channel_id=1, source_target_pairs={{0,4},{1,5},{2,6},{3,7},{4,0},{5,1},{6,2},{7,3},{8,12},{9,13},{10,... | collective-permute-start | bytes 7372808 | tf_op jit(solution)/shard_map/ppermute | solution.py:730
  320.3 22.8 %collective-permute-start.44 = (bf16[384,768]{1,0:T(8,128)(2,1)}, bf16[384,768]{1,0:T(8,128)(2,1)}, u32[]{:S(2)}, u32[]{:S(2)}) collective-permute-start(bf16[384,768]{1,0:T(8,128)(2,1)} %collective-permute-done.43), channel_id=1, source_target_pairs={{1,2},{2,1},{5,6},{6,5},{9,10},{10,9},{13,14},{14,13},{17,18},{18,... | collective-permute-start | bytes 1769480 | tf_op jit(solution)/shard_map/ppermute | solution.py:734
  331.8 43.6 %collective-permute-start.47 = (bf16[768,768]{1,0:T(8,128)(2,1)}, bf16[768,768]{1,0:T(8,128)(2,1)}, u32[]{:S(2)}, u32[]{:S(2)}) collective-permute-start(bf16[768,768]{1,0:T(8,128)(2,1)} %get-tuple-element.262), channel_id=1, source_target_pairs={{1,9},{2,10},{5,13},{6,14},{9,1},{10,2},{13,5},{14,6},{17,25},{18,... | collective-permute-start | bytes 3538952 | tf_op jit(solution)/shard_map/ppermute | solution.py:730
  333.5 41.9 %collective-permute-start.48 = (bf16[768,768]{1,0:T(8,128)(2,1)}, bf16[768,768]{1,0:T(8,128)(2,1)}, u32[]{:S(2)}, u32[]{:S(2)}) collective-permute-start(bf16[768,768]{1,0:T(8,128)(2,1)} %get-tuple-element.263), channel_id=1, source_target_pairs={{1,17},{2,18},{5,21},{6,22},{9,25},{10,26},{13,29},{14,30},{17,1},... | collective-permute-start | bytes 3538952 | tf_op jit(solution)/shard_map/ppermute | solution.py:730
  337.2 44.6 %all-to-all-start.1 = ((bf16[512,4,192]{0,2,1:T(8,128)(2,1)}), bf16[512,4,192]{0,2,1:T(8,128)(2,1)S(1)}, u32[]{:S(2)}, u32[]{:S(2)}) async-start(bf16[512,4,192]{0,2,1:T(8,128)(2,1)} %bitcast.17), calls=%async_computation.1 | async-start | bytes 1572864 | tf_op jit(solution)/shard_map/all_to_all | solution.py:968
  343.9 26.7 %collective-permute-start.65 = (bf16[384,768]{1,0:T(8,128)(2,1)}, bf16[384,768]{1,0:T(8,128)(2,1)}, u32[]{:S(2)}, u32[]{:S(2)}) collective-permute-start(bf16[384,768]{1,0:T(8,128)(2,1)} %collective-permute-done.44), channel_id=1, source_target_pairs={{1,0},{2,3},{5,4},{6,7},{9,8},{10,11},{13,12},{14,15},{17,16},{18,... | collective-permute-start | bytes 1769480 | tf_op jit(solution)/shard_map/ppermute | solution.py:734
  346.9 27.9 %collective-permute-start.52 = (bf16[384,768]{1,0:T(8,128)(2,1)S(1)}, bf16[384,768]{1,0:T(8,128)(2,1)}, u32[]{:S(2)}, u32[]{:S(2)}) collective-permute-start(bf16[384,768]{1,0:T(8,128)(2,1)S(1)} %add_convert_fusion.6), channel_id=1, source_target_pairs={{0,1},{3,2},{4,5},{7,6},{8,9},{11,10},{12,13},{15,14},{16,17},{19,... | collective-permute-start | bytes 1769480 | tf_op jit(solution)/shard_map/ppermute | solution.py:734
  353.1 22.3 %collective-permute-start.53 = (bf16[384,768]{1,0:T(8,128)(2,1)}, bf16[384,768]{1,0:T(8,128)(2,1)}, u32[]{:S(2)}, u32[]{:S(2)}) collective-permute-start(bf16[384,768]{1,0:T(8,128)(2,1)} %collective-permute-done.49), channel_id=1, source_target_pairs={{1,2},{2,1},{5,6},{6,5},{9,10},{10,9},{13,14},{14,13},{17,18},{18,... | collective-permute-start | bytes 1769480 | tf_op jit(solution)/shard_map/ppermute | solution.py:734
  375.4 30.8 %collective-permute-start.66 = (bf16[384,768]{1,0:T(8,128)(2,1)}, bf16[384,768]{1,0:T(8,128)(2,1)}, u32[]{:S(2)}, u32[]{:S(2)}) collective-permute-start(bf16[384,768]{1,0:T(8,128)(2,1)} %collective-permute-done.53), channel_id=1, source_target_pairs={{1,0},{2,3},{5,4},{6,7},{9,8},{10,11},{13,12},{14,15},{17,16},{18,... | collective-permute-start | bytes 1769480 | tf_op jit(solution)/shard_map/ppermute | solution.py:734
  380.3 23.4 %collective-permute-start.57 = (bf16[384,768]{1,0:T(8,128)(2,1)S(1)}, bf16[384,768]{1,0:T(8,128)(2,1)}, u32[]{:S(2)}, u32[]{:S(2)}) collective-permute-start(bf16[384,768]{1,0:T(8,128)(2,1)S(1)} %get-tuple-element.278), channel_id=1, source_target_pairs={{1,2},{2,1},{5,6},{6,5},{9,10},{10,9},{13,14},{14,13},{17,18},{18,... | collective-permute-start | bytes 1769480 | tf_op jit(solution)/shard_map/ppermute | solution.py:734
  385.2 24.7 %collective-permute-start.56 = (bf16[384,768]{1,0:T(8,128)(2,1)}, bf16[384,768]{1,0:T(8,128)(2,1)S(1)}, u32[]{:S(2)}, u32[]{:S(2)}) collective-permute-start(bf16[384,768]{1,0:T(8,128)(2,1)} %collective-permute-done.52), channel_id=1, source_target_pairs={{1,2},{2,1},{5,6},{6,5},{9,10},{10,9},{13,14},{14,13},{17,18},{18,... | collective-permute-start | bytes 1769480 | tf_op jit(solution)/shard_map/ppermute | solution.py:734
  390.5 19.3 %collective-permute-start.54 = (bf16[400,768]{1,0:T(8,128)(2,1)S(1)}, bf16[400,768]{1,0:T(8,128)(2,1)S(1)}, u32[]{:S(2)}, u32[]{:S(2)}) collective-permute-start(bf16[400,768]{1,0:T(8,128)(2,1)S(1)} %add_convert_fusion.1), channel_id=1, source_target_pairs={{1,2},{2,1},{5,6},{6,5},{9,10},{10,9},{13,14},{14,13},{17,18},{18,... | collective-permute-start | bytes 1843208 | tf_op jit(solution)/shard_map/ppermute | solution.py:734
  403.7 24.1 %collective-permute-start.60 = (bf16[384,768]{1,0:T(8,128)(2,1)S(1)}, bf16[384,768]{1,0:T(8,128)(2,1)S(1)}, u32[]{:S(2)}, u32[]{:S(2)}) collective-permute-start(bf16[384,768]{1,0:T(8,128)(2,1)S(1)} %add_convert_fusion.3), channel_id=1, source_target_pairs={{1,0},{2,3},{5,4},{6,7},{9,8},{10,11},{13,12},{14,15},{17,16},{18,... | collective-permute-start | bytes 1769480 | tf_op jit(solution)/shard_map/ppermute | solution.py:734
  406.2 27.9 %collective-permute-start.61 = (bf16[384,768]{1,0:T(8,128)(2,1)S(1)}, bf16[384,768]{1,0:T(8,128)(2,1)S(1)}, u32[]{:S(2)}, u32[]{:S(2)}) collective-permute-start(bf16[384,768]{1,0:T(8,128)(2,1)S(1)} %add_convert_fusion.2), channel_id=1, source_target_pairs={{1,0},{2,3},{5,4},{6,7},{9,8},{10,11},{13,12},{14,15},{17,16},{18,... | collective-permute-start | bytes 1769480 | tf_op jit(solution)/shard_map/ppermute | solution.py:734
  410.0 41.0 %collective-permute-start.64 = (bf16[384,768]{1,0:T(8,128)(2,1)S(1)}, bf16[384,768]{1,0:T(8,128)(2,1)S(1)}, u32[]{:S(2)}, u32[]{:S(2)}) collective-permute-start(bf16[384,768]{1,0:T(8,128)(2,1)S(1)} %collective-permute-done.56), channel_id=1, source_target_pairs={{1,0},{2,3},{5,4},{6,7},{9,8},{10,11},{13,12},{14,15},{17,16},{18,... | collective-permute-start | bytes 1769480 | tf_op jit(solution)/shard_map/ppermute | solution.py:734
  411.3 41.1 %collective-permute-start.62 = (bf16[400,768]{1,0:T(8,128)(2,1)S(1)}, bf16[400,768]{1,0:T(8,128)(2,1)S(1)}, u32[]{:S(2)}, u32[]{:S(2)}) collective-permute-start(bf16[400,768]{1,0:T(8,128)(2,1)S(1)} %collective-permute-done.55), channel_id=1, source_target_pairs={{1,2},{2,1},{5,6},{6,5},{9,10},{10,9},{13,14},{14,13},{17,18},{18,... | collective-permute-start | bytes 1843208 | tf_op jit(solution)/shard_map/ppermute | solution.py:734
  412.2 52.0 %collective-permute-start.59 = (bf16[400,768]{1,0:T(8,128)(2,1)S(1)}, bf16[400,768]{1,0:T(8,128)(2,1)S(1)}, u32[]{:S(2)}, u32[]{:S(2)}) collective-permute-start(bf16[400,768]{1,0:T(8,128)(2,1)S(1)} %add_convert_fusion), channel_id=1, source_target_pairs={{1,0},{2,3},{5,4},{6,7},{9,8},{10,11},{13,12},{14,15},{17,16},{18,... | collective-permute-start | bytes 1843208 | tf_op jit(solution)/shard_map/ppermute | solution.py:734
  452.4 21.1 %collective-permute-start.63 = (bf16[400,768]{1,0:T(8,128)(2,1)S(1)}, bf16[400,768]{1,0:T(8,128)(2,1)S(1)}, u32[]{:S(2)}, u32[]{:S(2)}) collective-permute-start(bf16[400,768]{1,0:T(8,128)(2,1)S(1)} %collective-permute-done.62), channel_id=1, source_target_pairs={{1,0},{2,3},{5,4},{6,7},{9,8},{10,11},{13,12},{14,15},{17,16},{18,... | collective-permute-start | bytes 1843208 | tf_op jit(solution)/shard_map/ppermute | solution.py:734
  (101 other events, 909.7 us)

commit v5 on v4

--- a/solution.py
+++ b/solution.py
@@ -20,6 +20,7 @@
 BLOCKS = LEN // TILE
 ROWS8 = D // 8
 EXTRA = 16
+PIECES = 2
 
 EPSILON = 1e-06
 MASKED = -1000000000.0
@@ -533,25 +534,31 @@
             wait_all(in_loads(unit))
 
     wi = wi_s[step].reshape(D, D)
-    if fwd:
-        h, slope = gelu_parts(dot(n_s[...], wi))
-        h = h.astype(bf16)
-        if mode == "fwd":
-            h_o[0] = h
-            slope_o[0] = slope.astype(bf16)
-    else:
-        h, slope = h_i[0], slope_i[0].astype(f32)
 
     @pl.when(step == 0)
     def _():
         wait_all(out_loads())
 
     wo = wo_s[pl.ds(2 * step, 2)].reshape(D, D)
-    if fwd:
-        acc[...] += dot(h, wo)
+    hs, dus = [], []
+    for i in range(PIECES):
+        rows = slice(i * LEN // PIECES, (i + 1) * LEN // PIECES)
+        if fwd:
+            h, slope = gelu_parts(dot(n_s[rows, :], wi))
+            h = h.astype(bf16)
+            if mode == "fwd":
+                h_o[0, rows, :] = h
+                slope_o[0, rows, :] = slope.astype(bf16)
+            acc[rows, :] += dot(h, wo)
+        else:
+            h, slope = h_i[0, rows, :], slope_i[0, rows, :].astype(f32)
+        if bwd:
+            du = (slope * dot_nt(g[rows, :], wo)).astype(bf16)
+            dn[rows, :] += dot_nt(du, wi)
+            hs.append(h)
+            dus.append(du)
     if bwd:
-        du = (slope * dot_nt(g[...], wo)).astype(bf16)
-        dn[...] += dot_nt(du, wi)
+        h, du = jnp.concatenate(hs), jnp.concatenate(dus)
         in_rows = pl.ds(pl.multiple_of(step * ROWS8, 32), ROWS8)
         put_blocks(me, dot(nt_s[...], du), in_rows, keep_s, send_s)
         dwo = dot(h.T, g[...]).astype(bf16)

time: 485 us -> 485 us (level)
  no operation moved by 1% of the time
where the time goes in v5:
time: 485 us; the launch traced here: 476 us
  Pallas kernels  156 us (32%)
  starting transfers between devices  133 us (27%)
  waiting for transfers between devices  123 us (25%)
  local copies, waits for them, and re-layouts  30.5 us (6%)
  other arithmetic  29.5 us (6%)
    ppermute x47, starting transfers between devices, across(): return lax.ppermute(x, ('wide', 'narrow'), pairs)  75.9 us
    ppermute x20, waiting for transfers between devices, between(): return lax.ppermute(x, 'narrow', pairs)  68 us
    pallas_call x2, Pallas kernels, attn_bwd(): pl.pallas_call(only(None if has_bias else 0, functools.partial(attn_bwd_k...  55.3 us
    ppermute x47, waiting for transfers between devices, across(): return lax.ppermute(x, ('wide', 'narrow'), pairs)  54.9 us
    pallas_call x2, Pallas kernels, attn_fwd(): pl.pallas_call(only(None if has_bias else 0, functools.partial(attn_fwd_k...  41.9 us
    ppermute x20, starting transfers between devices, between(): return lax.ppermute(x, 'narrow', pairs)  41.5 us
    pallas_call x3, Pallas kernels, ffn(): pl.pallas_call(only(0 if mode == 'both' else 1, functools.partial(ffn_ker...  33.6 us
    all_to_all x2, starting transfers between devices, by_columns(): return lax.all_to_all(x, 'narrow', split_axis=1, concat_axis=0, tiled=True)  15.9 us
  transfers between devices with their start and end apart: 69, of which 28 were waited for; matrix products, arithmetic and copies ran while one was open for 10% of the time, Pallas kernels for 23%

profile of v5, /device:TPU:0, one launch (start us, length us, event | category | flops | bytes accessed | tf_op | source)
XLA Modules:
  0.0 475.5 jit_solution(1069716543898878141)
XLA Ops:
  25.1 5.7 %collective-permute-done.3.refs_10_.refs_15_ = bf16[2,96,768]{2,1,0:T(8,128)(2,1)S(1)} collective-permute-done((bf16[2,96,768]{2,1,0:T(8,128)(2,1)S(1)}, bf16[2,96,768]{2,1,0:T(8,128)(2,1)S(1)}, u32[]{:S(2)}, u32[]{:S(2)}) %collective-permute-start.3) | collective-permute-done | bytes 294944 | tf_op jit(solution)/shard_map/ppermute | solution.py:737
  40.7 21.1 %self_fwd.1 = (f32[512,768]{1,0:T(8,128)}, bf16[512,768]{1,0:T(8,128)(2,1)}, bf16[6,512,128]{2,1,0:T(8,128)(2,1)}, bf16[6,512,128]{2,1,0:T(8,128)(2,1)}, bf16[6,...) custom-call(s32[2]{0:T(128)} %pad_add_fusion.refs_0_.me_ref, ...), custom_call_target="tpu_custom_call" | custom-call | tf_op jit(solution)/shard_map/self_fwd/pallas_call | solution.py:260
  64.5 13.1 %collective-permute-done.12.refs_5_.refs_6_.refs_8_ = bf16[4,96,768]{2,1,0:T(8,128)(2,1)S(1)} collective-permute-done((bf16[4,96,768]{2,1,0:T(8,128)(2,1)S(1)}, bf16[4,96,768]{2,1,0:T(8,128)(2,1)S(1)}, u32[]{:S(2)}, u32[]{:S(2)}) %collective-permute-start.12) | collective-permute-done | bytes 589856 | tf_op jit(solution)/shard_map/ppermute | solution.py:737
  88.4 4.4 ffn_fwd.1
  92.8 3.9 collective-permute-done.18.refs_6_.refs_10_
  108.6 3.6 collective-permute-start.23
  116.4 3.4 collective-permute-done.23.refs_9_.refs_13_
  125.0 20.8 %cross_fwd.1 = (f32[512,768]{1,0:T(8,128)}, bf16[512,768]{1,0:T(8,128)(2,1)}, bf16[6,512,128]{2,1,0:T(8,128)(2,1)}, bf16[6,512,128]{2,1,0:T(8,128)(2,1)}, bf16[6...) custom-call(s32[2]{0:T(128)} %pad_add_fusion.refs_0_.me_ref, ...), custom_call_target="tpu_custom_call" | custom-call | tf_op jit(solution)/shard_map/cross_fwd/pallas_call | solution.py:260
  145.7 24.4 %ffn_both.1 = (bf16[512,768]{1,0:T(8,128)(2,1)}, bf16[512,768]{1,0:T(8,128)(2,1)}, f32[1,768]{1,0:T(1,128)}, bf16[4,768,768]{2,1,0:T(8,128)(2,1)}, bf16[4,768,768]{2,1,0:T(8,128)(2,1)}) custom-call(s32[2]{0:T(128)} %pad_add_fusion.refs_0_.me_ref, bf16[512,768]{1,0:T(8,128)(2,1)} %get-tuple-element.181.refs_0_, f32[1,768]{1,0:T(1,128)} %reshape.157.refs_1_, ...), custom_call_target="tpu_custom_call" | custom-call | tf_op jit(solution)/shard_map/ffn_both/pallas_call | solution.py:636
  172.5 27.6 %cross_bwd.1 = (f32[512,768]{1,0:T(8,128)}, bf16[4,384,768]{2,1,0:T(8,128)(2,1)}, bf16[4,384,768]{2,1,0:T(8,128)(2,1)}, f32[1,768]{1,0:T(1,128)}, bf16[512,768]{1,0:T(8,128)(2,1)}) custom-call(s32[2]{0:T(128)} %pad_add_fusion.refs_0_.me_ref, bf16[512,768]{1,0:T(8,128)(2,1)} %get-tuple-element.185.refs_0_, f32[512,768]{1,0:T(8,128)} %get-tuple-element.170.refs_0_.refs_1_, ...), custom_call_target="tpu_custom_call" | custom-call | tf_op jit(solution)/shard_map/cross_bwd/pallas_call | solution.py:422
  206.8 3.7 diag_add.4
  210.6 3.7 collective-permute-start.30
  217.5 4.0 collective-permute-done.32.refs_2_
  222.3 4.9 %ffn_bwd.1 = (bf16[512,768]{1,0:T(8,128)(2,1)}, f32[1,768]{1,0:T(1,128)}, bf16[4,768,768]{2,1,0:T(8,128)(2,1)}, bf16[4,768,768]{2,1,0:T(8,128)(2,1)}) custom-call(s32[2]{0:T(128)} %pad_add_fusion.refs_0_.me_ref, bf16[512,768]{1,0:T(8,128)(2,1)} %get-tuple-element.171.refs_0_, f32[1,768]{1,0:T(1,128)} %reshape.155.refs_1_, bf16[512,768]{1,0:T(8,128)(2,1)} %copy-done.31, ...), custom_call_target="tpu_custom_call" | custom-call | tf_op jit(solution)/shard_map/ffn_bwd/pallas_call | solution.py:636
  228.1 3.4 collective-permute-done.31.refs_3_
  234.4 5.7 %rest_add.4 = (bf16[768,768]{1,0:T(8,128)(2,1)}, bf16[768,768]{1,0:T(8,128)(2,1)}, bf16[768,768]{1,0:T(8,128)(2,1)}) custom-call(s32[2]{0:T(128)} %pad_add_fusion.refs_0_.me_ref, bf16[4,768,768]{2,1,0:T(8,128)(2,1)} %get-tuple-element.183.refs_0_, bf16[4,768,768]{2,1,0:T(8,128)(2,1)} %collective-permute-done.28.refs_1_, bf16[384,768]{1,0:T(8,128)(2,1)} %copy-done.38, ...), custom_call_target="tpu_custom_call" | custom-call | tf_op jit(solution)/shard_map/rest_add/pallas_call | solution.py:716
  241.3 10.0 %all-to-all-start = ((bf16[512,4,192]{0,2,1:T(8,128)(2,1)}), bf16[512,4,192]{0,2,1:T(8,128)(2,1)S(1)}, u32[]{:S(2)}, u32[]{:S(2)}) async-start(bf16[512,4,192]{0,2,1:T(8,128)(2,1)} %bitcast.15), calls=%async_computation | async-start | bytes 1572864 | tf_op jit(solution)/shard_map/all_to_all | solution.py:975
  251.3 3.5 collective-permute-start.36
  254.8 3.3 collective-permute-start.37
  267.6 27.7 %self_bwd.1 = (bf16[512,768]{1,0:T(8,128)(2,1)}, bf16[4,400,768]{2,1,0:T(8,128)(2,1)}, bf16[4,400,768]{2,1,0:T(8,128)(2,1)}) custom-call(s32[2]{0:T(128)} %pad_add_fusion.refs_0_.me_ref, f32[512,768]{1,0:T(8,128)} %get-tuple-element.217.refs_1_, bf16[512,768]{1,0:T(8,128)(2,1)} %get-tuple-element.160.refs_1_.refs_2_, f32[1,768]{1,0:T(1,128)} %select_n.179.refs_2_.refs_3_, ...), custom_call_target="tpu_custom_call" | custom-call | tf_op jit(solution)/shard_map/self_bwd/pallas_call | solution.py:422
  305.4 3.9 rest_add.7
  309.3 3.3 collective-permute-start.50
  336.4 5.9 %all-to-all-start.1 = ((bf16[512,4,192]{0,2,1:T(8,128)(2,1)}), bf16[512,4,192]{0,2,1:T(8,128)(2,1)S(1)}, u32[]{:S(2)}, u32[]{:S(2)}) async-start(bf16[512,4,192]{0,2,1:T(8,128)(2,1)} %bitcast.17), calls=%async_computation.1 | async-start | bytes 1572864 | tf_op jit(solution)/shard_map/all_to_all | solution.py:975
  346.1 6.2 %collective-permute-start.52 = (bf16[384,768]{1,0:T(8,128)(2,1)S(1)}, bf16[384,768]{1,0:T(8,128)(2,1)}, u32[]{:S(2)}, u32[]{:S(2)}) collective-permute-start(bf16[384,768]{1,0:T(8,128)(2,1)S(1)} %add_convert_fusion.6), channel_id=1, source_target_pairs={{0,1},{3,2},{4,5},{7,6},{8,9},{11,10},{12,13},{15,14},{16,17},{19,... | collective-permute-start | bytes 1769480 | tf_op jit(solution)/shard_map/ppermute | solution.py:741
  354.7 4.0 rest_add.6
  358.6 11.3 %collective-permute-done.65 = bf16[384,768]{1,0:T(8,128)(2,1)} collective-permute-done((bf16[384,768]{1,0:T(8,128)(2,1)}, bf16[384,768]{1,0:T(8,128)(2,1)}, u32[]{:S(2)}, u32[]{:S(2)}) %collective-permute-start.65) | collective-permute-done | bytes 589856 | tf_op jit(solution)/shard_map/ppermute | solution.py:741
  390.5 11.2 %collective-permute-start.55 = (bf16[400,768]{1,0:T(8,128)(2,1)S(1)}, bf16[400,768]{1,0:T(8,128)(2,1)S(1)}, u32[]{:S(2)}, u32[]{:S(2)}) collective-permute-start(bf16[400,768]{1,0:T(8,128)(2,1)S(1)} %add_convert_fusion.1), channel_id=1, source_target_pairs={{0,1},{3,2},{4,5},{7,6},{8,9},{11,10},{12,13},{15,14},{16,17},{19,... | collective-permute-start | bytes 1843208 | tf_op jit(solution)/shard_map/ppermute | solution.py:741
  412.8 14.2 %collective-permute-done.60 = bf16[384,768]{1,0:T(8,128)(2,1)S(1)} collective-permute-done((bf16[384,768]{1,0:T(8,128)(2,1)S(1)}, bf16[384,768]{1,0:T(8,128)(2,1)S(1)}, u32[]{:S(2)}, u32[]{:S(2)}) %collective-permute-start.60) | collective-permute-done | bytes 589856 | tf_op jit(solution)/shard_map/ppermute | solution.py:741
  427.1 6.3 %collective-permute-done.61 = bf16[384,768]{1,0:T(8,128)(2,1)S(1)} collective-permute-done((bf16[384,768]{1,0:T(8,128)(2,1)S(1)}, bf16[384,768]{1,0:T(8,128)(2,1)S(1)}, u32[]{:S(2)}, u32[]{:S(2)}) %collective-permute-start.61) | collective-permute-done | bytes 589856 | tf_op jit(solution)/shard_map/ppermute | solution.py:741
  435.7 14.7 %collective-permute-done.64 = bf16[384,768]{1,0:T(8,128)(2,1)S(1)} collective-permute-done((bf16[384,768]{1,0:T(8,128)(2,1)S(1)}, bf16[384,768]{1,0:T(8,128)(2,1)S(1)}, u32[]{:S(2)}, u32[]{:S(2)}) %collective-permute-start.64) | collective-permute-done | bytes 589856 | tf_op jit(solution)/shard_map/ppermute | solution.py:741
  453.0 10.5 %collective-permute-done.59 = bf16[400,768]{1,0:T(8,128)(2,1)S(1)} collective-permute-done((bf16[400,768]{1,0:T(8,128)(2,1)S(1)}, bf16[400,768]{1,0:T(8,128)(2,1)S(1)}, u32[]{:S(2)}, u32[]{:S(2)}) %collective-permute-start.59) | collective-permute-done | bytes 614432 | tf_op jit(solution)/shard_map/ppermute | solution.py:741
  465.8 6.9 %collective-permute-done.63 = bf16[400,768]{1,0:T(8,128)(2,1)S(1)} collective-permute-done((bf16[400,768]{1,0:T(8,128)(2,1)S(1)}, bf16[400,768]{1,0:T(8,128)(2,1)S(1)}, u32[]{:S(2)}, u32[]{:S(2)}) %collective-permute-start.63) | collective-permute-done | bytes 614432 | tf_op jit(solution)/shard_map/ppermute | solution.py:741
  (318 shorter events, 177.3 us)
Async XLA Ops:
  23.0 38.8 %collective-permute-start.10 = (bf16[8,96,768]{2,1,0:T(8,128)(2,1)S(1)}, bf16[8,96,768]{2,1,0:T(8,128)(2,1)S(1)}, u32[]{:S(2)}, u32[]{:S(2)}) collective-permute-start(bf16[8,96,768]{2,1,0:T(8,128)(2,1)S(1)} %pad_maximum_fusion.refs_2_.refs_3_.refs_5_), channel_id=1, source_target_pairs={{0,16},{1,17},{2,18},{3,19},{4,20},{5,21},{6,22},{7,23},{8,24},{9,... | collective-permute-start | bytes 3538952 | tf_op jit(solution)/shard_map/ppermute | solution.py:737
  23.4 38.5 %collective-permute-start.11 = (bf16[8,96,768]{2,1,0:T(8,128)(2,1)S(1)}, bf16[8,96,768]{2,1,0:T(8,128)(2,1)}, u32[]{:S(2)}, u32[]{:S(2)}) collective-permute-start(bf16[8,96,768]{2,1,0:T(8,128)(2,1)S(1)} %pad_maximum_fusion.refs_2_.refs_3_.refs_5_), channel_id=1, source_target_pairs={{0,4},{1,5},{2,6},{3,7},{4,0},{5,1},{6,2},{7,3},{8,12},{9,13},{10,... | collective-permute-start | bytes 3538952 | tf_op jit(solution)/shard_map/ppermute | solution.py:737
  23.4 38.5 %collective-permute-start.9 = (bf16[8,96,768]{2,1,0:T(8,128)(2,1)S(1)}, bf16[8,96,768]{2,1,0:T(8,128)(2,1)S(1)}, u32[]{:S(2)}, u32[]{:S(2)}) collective-permute-start(bf16[8,96,768]{2,1,0:T(8,128)(2,1)S(1)} %pad_maximum_fusion.refs_2_.refs_3_.refs_5_), channel_id=1, source_target_pairs={{0,8},{1,9},{2,10},{3,11},{4,12},{5,13},{6,14},{7,15},{8,0},{9,1},... | collective-permute-start | bytes 3538952 | tf_op jit(solution)/shard_map/ppermute | solution.py:737
  64.0 23.4 %collective-permute-start.14 = (bf16[8,96,768]{2,1,0:T(8,128)(2,1)S(1)}, bf16[8,96,768]{2,1,0:T(8,128)(2,1)S(1)}, u32[]{:S(2)}, u32[]{:S(2)}) collective-permute-start(bf16[8,96,768]{2,1,0:T(8,128)(2,1)S(1)} %collective-permute-done.9.refs_3_.refs_4_.refs_6_), channel_id=1, source_target_pairs={{0,4},{1,5},{2,6},{3,7},{4,0},{5,1},{6,2},{7,3},{8,12},{9,13},{10,... | collective-permute-start | bytes 3538952 | tf_op jit(solution)/shard_map/ppermute | solution.py:737
  64.0 23.4 %collective-permute-start.15 = (bf16[8,96,768]{2,1,0:T(8,128)(2,1)S(1)}, bf16[8,96,768]{2,1,0:T(8,128)(2,1)}, u32[]{:S(2)}, u32[]{:S(2)}) collective-permute-start(bf16[8,96,768]{2,1,0:T(8,128)(2,1)S(1)} %collective-permute-done.10.refs_4_.refs_5_.refs_7_), channel_id=1, source_target_pairs={{0,4},{1,5},{2,6},{3,7},{4,0},{5,1},{6,2},{7,3},{8,12},{9,13},{10,... | collective-permute-start | bytes 3538952 | tf_op jit(solution)/shard_map/ppermute | solution.py:737
  98.9 24.3 %collective-permute-start.21 = (bf16[512,768]{1,0:T(8,128)(2,1)}, bf16[512,768]{1,0:T(8,128)(2,1)S(1)}, u32[]{:S(2)}, u32[]{:S(2)}) collective-permute-start(bf16[512,768]{1,0:T(8,128)(2,1)} %get-tuple-element.177), channel_id=1, source_target_pairs={{1,0},{2,3},{5,4},{6,7},{9,8},{10,11},{13,12},{14,15},{17,16},{18,... | collective-permute-start | bytes 2359304 | tf_op jit(solution)/shard_map/ppermute | solution.py:741
  101.2 21.6 %collective-permute-start.24 = (bf16[4,96,768]{2,1,0:T(8,128)(2,1)}, bf16[4,96,768]{2,1,0:T(8,128)(2,1)S(1)}, u32[]{:S(2)}, u32[]{:S(2)}) collective-permute-start(bf16[4,96,768]{2,1,0:T(8,128)(2,1)} %collective-permute-done.18.refs_6_.refs_10_), channel_id=1, source_target_pairs={{0,4},{3,7},{4,0},{7,3},{8,12},{11,15},{12,8},{15,11},{16,20},{19,... | collective-permute-start | bytes 1769480 | tf_op jit(solution)/shard_map/ppermute | solution.py:737
  170.1 36.7 %collective-permute-start.28 = (bf16[4,768,768]{2,1,0:T(8,128)(2,1)}, bf16[4,768,768]{2,1,0:T(8,128)(2,1)}, u32[]{:S(2)}, u32[]{:S(2)}) collective-permute-start(bf16[4,768,768]{2,1,0:T(8,128)(2,1)} %get-tuple-element.184), channel_id=1, source_target_pairs={{0,4},{3,7},{4,0},{7,3},{8,12},{11,15},{12,8},{15,11},{16,20},{19,... | collective-permute-start | bytes 14155784 | tf_op jit(solution)/shard_map/ppermute | solution.py:737
  231.4 64.0 %collective-permute-start.33 = (bf16[4,768,768]{2,1,0:T(8,128)(2,1)}, bf16[4,768,768]{2,1,0:T(8,128)(2,1)}, u32[]{:S(2)}, u32[]{:S(2)}) collective-permute-start(bf16[4,768,768]{2,1,0:T(8,128)(2,1)} %get-tuple-element.205), channel_id=1, source_target_pairs={{1,5},{2,6},{5,1},{6,2},{9,13},{10,14},{13,9},{14,10},{17,21},{18,... | collective-permute-start | bytes 14155784 | tf_op jit(solution)/shard_map/ppermute | solution.py:737
  241.3 54.0 %all-to-all-start = ((bf16[512,4,192]{0,2,1:T(8,128)(2,1)}), bf16[512,4,192]{0,2,1:T(8,128)(2,1)S(1)}, u32[]{:S(2)}, u32[]{:S(2)}) async-start(bf16[512,4,192]{0,2,1:T(8,128)(2,1)} %bitcast.15), calls=%async_computation | async-start | bytes 1572864 | tf_op jit(solution)/shard_map/all_to_all | solution.py:975
  251.3 44.2 %collective-permute-start.36 = (bf16[768,768]{1,0:T(8,128)(2,1)}, bf16[768,768]{1,0:T(8,128)(2,1)}, u32[]{:S(2)}, u32[]{:S(2)}) collective-permute-start(bf16[768,768]{1,0:T(8,128)(2,1)} %get-tuple-element.215), channel_id=1, source_target_pairs={{0,8},{3,11},{4,12},{7,15},{8,0},{11,3},{12,4},{15,7},{16,24},{19,... | collective-permute-start | bytes 3538952 | tf_op jit(solution)/shard_map/ppermute | solution.py:737
  254.8 40.7 %collective-permute-start.37 = (bf16[768,768]{1,0:T(8,128)(2,1)}, bf16[768,768]{1,0:T(8,128)(2,1)}, u32[]{:S(2)}, u32[]{:S(2)}) collective-permute-start(bf16[768,768]{1,0:T(8,128)(2,1)} %get-tuple-element.216), channel_id=1, source_target_pairs={{0,16},{3,19},{4,20},{7,23},{8,24},{11,27},{12,28},{15,31},{16,0},... | collective-permute-start | bytes 3538952 | tf_op jit(solution)/shard_map/ppermute | solution.py:737
  262.1 33.3 %collective-permute-start.34 = (bf16[192,768]{1,0:T(8,128)(2,1)}, bf16[192,768]{1,0:T(8,128)(2,1)S(1)}, u32[]{:S(2)}, u32[]{:S(2)}) collective-permute-start(bf16[192,768]{1,0:T(8,128)(2,1)} %get-tuple-element.213), channel_id=1, source_target_pairs={{0,8},{3,11},{4,12},{7,15},{8,0},{11,3},{12,4},{15,7},{16,24},{19,... | collective-permute-start | bytes 884744 | tf_op jit(solution)/shard_map/ppermute | solution.py:737
  264.5 30.9 %collective-permute-start.35 = (bf16[192,768]{1,0:T(8,128)(2,1)}, bf16[192,768]{1,0:T(8,128)(2,1)S(1)}, u32[]{:S(2)}, u32[]{:S(2)}) collective-permute-start(bf16[192,768]{1,0:T(8,128)(2,1)} %get-tuple-element.214), channel_id=1, source_target_pairs={{0,16},{3,19},{4,20},{7,23},{8,24},{11,27},{12,28},{15,31},{16,0},... | collective-permute-start | bytes 884744 | tf_op jit(solution)/shard_map/ppermute | solution.py:737
  296.2 21.9 %collective-permute-start.40 = (bf16[4,400,768]{2,1,0:T(8,128)(2,1)}, bf16[4,400,768]{2,1,0:T(8,128)(2,1)S(1)}, u32[]{:S(2)}, u32[]{:S(2)}) collective-permute-start(bf16[4,400,768]{2,1,0:T(8,128)(2,1)} %get-tuple-element.238), channel_id=1, source_target_pairs={{0,4},{1,5},{2,6},{3,7},{4,0},{5,1},{6,2},{7,3},{8,12},{9,13},{10,... | collective-permute-start | bytes 7372808 | tf_op jit(solution)/shard_map/ppermute | solution.py:737
  319.6 22.8 %collective-permute-start.44 = (bf16[384,768]{1,0:T(8,128)(2,1)}, bf16[384,768]{1,0:T(8,128)(2,1)}, u32[]{:S(2)}, u32[]{:S(2)}) collective-permute-start(bf16[384,768]{1,0:T(8,128)(2,1)} %collective-permute-done.43), channel_id=1, source_target_pairs={{1,2},{2,1},{5,6},{6,5},{9,10},{10,9},{13,14},{14,13},{17,18},{18,... | collective-permute-start | bytes 1769480 | tf_op jit(solution)/shard_map/ppermute | solution.py:741
  331.0 43.6 %collective-permute-start.47 = (bf16[768,768]{1,0:T(8,128)(2,1)}, bf16[768,768]{1,0:T(8,128)(2,1)}, u32[]{:S(2)}, u32[]{:S(2)}) collective-permute-start(bf16[768,768]{1,0:T(8,128)(2,1)} %get-tuple-element.262), channel_id=1, source_target_pairs={{1,9},{2,10},{5,13},{6,14},{9,1},{10,2},{13,5},{14,6},{17,25},{18,... | collective-permute-start | bytes 3538952 | tf_op jit(solution)/shard_map/ppermute | solution.py:737
  332.8 41.9 %collective-permute-start.48 = (bf16[768,768]{1,0:T(8,128)(2,1)}, bf16[768,768]{1,0:T(8,128)(2,1)}, u32[]{:S(2)}, u32[]{:S(2)}) collective-permute-start(bf16[768,768]{1,0:T(8,128)(2,1)} %get-tuple-element.263), channel_id=1, source_target_pairs={{1,17},{2,18},{5,21},{6,22},{9,25},{10,26},{13,29},{14,30},{17,1},... | collective-permute-start | bytes 3538952 | tf_op jit(solution)/shard_map/ppermute | solution.py:737
  336.4 44.6 %all-to-all-start.1 = ((bf16[512,4,192]{0,2,1:T(8,128)(2,1)}), bf16[512,4,192]{0,2,1:T(8,128)(2,1)S(1)}, u32[]{:S(2)}, u32[]{:S(2)}) async-start(bf16[512,4,192]{0,2,1:T(8,128)(2,1)} %bitcast.17), calls=%async_computation.1 | async-start | bytes 1572864 | tf_op jit(solution)/shard_map/all_to_all | solution.py:975
  343.2 26.7 %collective-permute-start.65 = (bf16[384,768]{1,0:T(8,128)(2,1)}, bf16[384,768]{1,0:T(8,128)(2,1)}, u32[]{:S(2)}, u32[]{:S(2)}) collective-permute-start(bf16[384,768]{1,0:T(8,128)(2,1)} %collective-permute-done.44), channel_id=1, source_target_pairs={{1,0},{2,3},{5,4},{6,7},{9,8},{10,11},{13,12},{14,15},{17,16},{18,... | collective-permute-start | bytes 1769480 | tf_op jit(solution)/shard_map/ppermute | solution.py:741
  346.1 27.9 %collective-permute-start.52 = (bf16[384,768]{1,0:T(8,128)(2,1)S(1)}, bf16[384,768]{1,0:T(8,128)(2,1)}, u32[]{:S(2)}, u32[]{:S(2)}) collective-permute-start(bf16[384,768]{1,0:T(8,128)(2,1)S(1)} %add_convert_fusion.6), channel_id=1, source_target_pairs={{0,1},{3,2},{4,5},{7,6},{8,9},{11,10},{12,13},{15,14},{16,17},{19,... | collective-permute-start | bytes 1769480 | tf_op jit(solution)/shard_map/ppermute | solution.py:741
  352.3 22.4 %collective-permute-start.53 = (bf16[384,768]{1,0:T(8,128)(2,1)}, bf16[384,768]{1,0:T(8,128)(2,1)}, u32[]{:S(2)}, u32[]{:S(2)}) collective-permute-start(bf16[384,768]{1,0:T(8,128)(2,1)} %collective-permute-done.49), channel_id=1, source_target_pairs={{1,2},{2,1},{5,6},{6,5},{9,10},{10,9},{13,14},{14,13},{17,18},{18,... | collective-permute-start | bytes 1769480 | tf_op jit(solution)/shard_map/ppermute | solution.py:741
  374.7 30.8 %collective-permute-start.66 = (bf16[384,768]{1,0:T(8,128)(2,1)}, bf16[384,768]{1,0:T(8,128)(2,1)}, u32[]{:S(2)}, u32[]{:S(2)}) collective-permute-start(bf16[384,768]{1,0:T(8,128)(2,1)} %collective-permute-done.53), channel_id=1, source_target_pairs={{1,0},{2,3},{5,4},{6,7},{9,8},{10,11},{13,12},{14,15},{17,16},{18,... | collective-permute-start | bytes 1769480 | tf_op jit(solution)/shard_map/ppermute | solution.py:741
  379.5 23.4 %collective-permute-start.57 = (bf16[384,768]{1,0:T(8,128)(2,1)S(1)}, bf16[384,768]{1,0:T(8,128)(2,1)}, u32[]{:S(2)}, u32[]{:S(2)}) collective-permute-start(bf16[384,768]{1,0:T(8,128)(2,1)S(1)} %get-tuple-element.278), channel_id=1, source_target_pairs={{1,2},{2,1},{5,6},{6,5},{9,10},{10,9},{13,14},{14,13},{17,18},{18,... | collective-permute-start | bytes 1769480 | tf_op jit(solution)/shard_map/ppermute | solution.py:741
  384.4 24.7 %collective-permute-start.56 = (bf16[384,768]{1,0:T(8,128)(2,1)}, bf16[384,768]{1,0:T(8,128)(2,1)S(1)}, u32[]{:S(2)}, u32[]{:S(2)}) collective-permute-start(bf16[384,768]{1,0:T(8,128)(2,1)} %collective-permute-done.52), channel_id=1, source_target_pairs={{1,2},{2,1},{5,6},{6,5},{9,10},{10,9},{13,14},{14,13},{17,18},{18,... | collective-permute-start | bytes 1769480 | tf_op jit(solution)/shard_map/ppermute | solution.py:741
  389.8 19.4 %collective-permute-start.54 = (bf16[400,768]{1,0:T(8,128)(2,1)S(1)}, bf16[400,768]{1,0:T(8,128)(2,1)S(1)}, u32[]{:S(2)}, u32[]{:S(2)}) collective-permute-start(bf16[400,768]{1,0:T(8,128)(2,1)S(1)} %add_convert_fusion.1), channel_id=1, source_target_pairs={{1,2},{2,1},{5,6},{6,5},{9,10},{10,9},{13,14},{14,13},{17,18},{18,... | collective-permute-start | bytes 1843208 | tf_op jit(solution)/shard_map/ppermute | solution.py:741
  402.9 24.1 %collective-permute-start.60 = (bf16[384,768]{1,0:T(8,128)(2,1)S(1)}, bf16[384,768]{1,0:T(8,128)(2,1)S(1)}, u32[]{:S(2)}, u32[]{:S(2)}) collective-permute-start(bf16[384,768]{1,0:T(8,128)(2,1)S(1)} %add_convert_fusion.3), channel_id=1, source_target_pairs={{1,0},{2,3},{5,4},{6,7},{9,8},{10,11},{13,12},{14,15},{17,16},{18,... | collective-permute-start | bytes 1769480 | tf_op jit(solution)/shard_map/ppermute | solution.py:741
  405.5 27.9 %collective-permute-start.61 = (bf16[384,768]{1,0:T(8,128)(2,1)S(1)}, bf16[384,768]{1,0:T(8,128)(2,1)S(1)}, u32[]{:S(2)}, u32[]{:S(2)}) collective-permute-start(bf16[384,768]{1,0:T(8,128)(2,1)S(1)} %add_convert_fusion.2), channel_id=1, source_target_pairs={{1,0},{2,3},{5,4},{6,7},{9,8},{10,11},{13,12},{14,15},{17,16},{18,... | collective-permute-start | bytes 1769480 | tf_op jit(solution)/shard_map/ppermute | solution.py:741
  409.3 41.0 %collective-permute-start.64 = (bf16[384,768]{1,0:T(8,128)(2,1)S(1)}, bf16[384,768]{1,0:T(8,128)(2,1)S(1)}, u32[]{:S(2)}, u32[]{:S(2)}) collective-permute-start(bf16[384,768]{1,0:T(8,128)(2,1)S(1)} %collective-permute-done.56), channel_id=1, source_target_pairs={{1,0},{2,3},{5,4},{6,7},{9,8},{10,11},{13,12},{14,15},{17,16},{18,... | collective-permute-start | bytes 1769480 | tf_op jit(solution)/shard_map/ppermute | solution.py:741
  410.6 41.1 %collective-permute-start.62 = (bf16[400,768]{1,0:T(8,128)(2,1)S(1)}, bf16[400,768]{1,0:T(8,128)(2,1)S(1)}, u32[]{:S(2)}, u32[]{:S(2)}) collective-permute-start(bf16[400,768]{1,0:T(8,128)(2,1)S(1)} %collective-permute-done.55), channel_id=1, source_target_pairs={{1,2},{2,1},{5,6},{6,5},{9,10},{10,9},{13,14},{14,13},{17,18},{18,... | collective-permute-start | bytes 1843208 | tf_op jit(solution)/shard_map/ppermute | solution.py:741
  411.5 52.0 %collective-permute-start.59 = (bf16[400,768]{1,0:T(8,128)(2,1)S(1)}, bf16[400,768]{1,0:T(8,128)(2,1)S(1)}, u32[]{:S(2)}, u32[]{:S(2)}) collective-permute-start(bf16[400,768]{1,0:T(8,128)(2,1)S(1)} %add_convert_fusion), channel_id=1, source_target_pairs={{1,0},{2,3},{5,4},{6,7},{9,8},{10,11},{13,12},{14,15},{17,16},{18,... | collective-permute-start | bytes 1843208 | tf_op jit(solution)/shard_map/ppermute | solution.py:741
  451.7 21.1 %collective-permute-start.63 = (bf16[400,768]{1,0:T(8,128)(2,1)S(1)}, bf16[400,768]{1,0:T(8,128)(2,1)S(1)}, u32[]{:S(2)}, u32[]{:S(2)}) collective-permute-start(bf16[400,768]{1,0:T(8,128)(2,1)S(1)} %collective-permute-done.62), channel_id=1, source_target_pairs={{1,0},{2,3},{5,4},{6,7},{9,8},{10,11},{13,12},{14,15},{17,16},{18,... | collective-permute-start | bytes 1843208 | tf_op jit(solution)/shard_map/ppermute | solution.py:741
  (101 other events, 909.7 us)
